TPU v7x, 32 devices: a whole 2x2x4 slice. The times are simulated.
32 devices in a mesh: dp: 8 (over z, x), mp: 4 (over y, core).
Axes of the slice: x: 2, y: 2, z: 4, core: 2. Of those that a mesh axis runs over, the one named last changes fastest.
Arguments:
- tokens: bfloat16 [16, 2048, 512], P('dp', 'mp'), may hold values from -6 to 6
- segment_ids: int32 [16, 2048], P('dp'), may hold values from 0 to 7, as said below
- routes: int32 [16, 2048, 8], P('dp', 'mp'), may hold values from 0 to 23, as said below
- out_grad: bfloat16 [16, 2048, 512], P('dp', 'mp'), may hold values from -6 to 6
- w_query: bfloat16 [512, 1536], P(('dp', 'mp')), may hold values from -0.25 to 0.25
- w_keyval: bfloat16 [512, 128], P(('dp', 'mp')), may hold values from -0.25 to 0.25
- w_output: bfloat16 [512, 1536], P(('dp', 'mp')), may hold values from -12 to 12
- w_router: bfloat16 [512, 24], P(('dp', 'mp')), may hold values from -0.12988281 to 0.12988281
- norm_gains: float32 [512, 2], P(('dp', 'mp')), may hold values from 0.5 to 1.5
- norm_biases: float32 [512, 2], P(('dp', 'mp')), may hold values from -0.6 to 0.6
- w_up: bfloat16 [512, 2048], P('dp', 'mp'), may hold values from -0.25 to 0.25
- w_down: bfloat16 [512, 2048], P('dp', 'mp'), may hold values from -0.1875 to 0.1875
Outputs:
- outputs: bfloat16 [16, 2048, 512], P('dp', 'mp')
- input_grad: float32 [16, 2048, 512], P('dp', 'mp')
- counts: float32 [24], replicated
- w_query_grad: float32 [512, 1536], P(('dp', 'mp'))
- w_keyval_grad: float32 [512, 128], P(('dp', 'mp'))
- w_output_grad: float32 [512, 1536], P(('dp', 'mp'))
- w_router_grad: float32 [512, 24], P(('dp', 'mp'))
- norm_gains_grad: float32 [512, 2], P(('dp', 'mp'))
- norm_biases_grad: float32 [512, 2], P(('dp', 'mp'))
- w_up_grad: float32 [512, 2048], P('dp', 'mp')
- w_down_grad: float32 [512, 2048], P('dp', 'mp')
Inputs may be any that keep to these rules, and one draw needn't show every extreme that they name: `segment_ids`: within a row the segment ids start at 0 and rise by at most one from a position to the next; in each aligned block of 2 rows one row is a single document. `routes`: each token names 8 different head experts.
All inputs are finite; a program needn't handle non-finite values.
Results may differ from a plain program's by a relative error of at most 0.03.
Values may be sent and summed in bfloat16 or wider, within the bound.
No kernel may reach another device: no remote copies, remote signals or barrier semaphores. Data moves between devices by JAX's collectives and lax.ppermute only.
A program may use at most 192 MiB of HBM per device.

v0:
```python
import jax
import jax.numpy as jnp
from jax import lax
from jax.sharding import PartitionSpec as P

epsilon = 1e-05


def cut_along(array, dim, peers):
    before, after = (array.shape[:dim], array.shape[dim + 1 :])
    return jnp.moveaxis(array.reshape(*before, peers, -1, *after), dim, 0)


def sent_and_summed(array, axis, dim):
    tiles = cut_along(array, dim, lax.axis_size(axis))
    arrived = lax.all_to_all(tiles, axis, split_axis=0, concat_axis=0, tiled=True)
    return arrived.astype(jnp.float32).sum(axis=0)


def side_by_side(arrays, axis, dim, along):
    both = jnp.concatenate(arrays, axis=along)
    filled, at, done = (sent_and_summed(both, axis, dim), 0, [])
    for a in arrays:
        done.append(lax.slice_in_dim(filled, at, at + a.shape[along], axis=along))
        at += a.shape[along]
    return tuple(done)


def layer_norm(values, gain, bias):
    mean = jnp.mean(values, axis=-1, keepdims=True)
    centred = values - mean
    rstd = lax.rsqrt(jnp.mean(centred * centred, axis=-1, keepdims=True) + epsilon)
    normed = centred * rstd
    return (normed * gain + bias, normed, rstd)


def norm_back(grad, normed, rstd, gain):
    scaled = grad * gain
    inner = (
        scaled
        - jnp.mean(scaled, axis=-1, keepdims=True)
        - normed * jnp.mean(scaled * normed, axis=-1, keepdims=True)
    )
    return rstd * inner


def contract_rows(left, right):
    return lax.dot_general(
        left, right, (((0,), (0,)), ((), ())), preferred_element_type=jnp.float32
    )


def against(left, right):
    return lax.dot_general(
        left, right, (((1,), (1,)), ((), ())), preferred_element_type=jnp.float32
    )


def shards(
    tokens,
    segment_ids,
    routes,
    out_grad,
    w_query,
    w_keyval,
    w_output,
    w_router,
    norm_gains,
    norm_biases,
    w_up,
    w_down,
):
    row_count, local_len, model_width = tokens.shape
    length = segment_ids.shape[1]
    head_count = w_router.shape[1]
    headsize = w_keyval.shape[1] // 2
    token_count = row_count * local_len
    seq_place = lax.axis_index("mp")
    full_query, full_keyval, full_output, full_router, full_gains, full_biases = (
        lax.all_gather(w_query, ("dp", "mp"), axis=0, tiled=True),
        lax.all_gather(w_keyval, ("dp", "mp"), axis=0, tiled=True),
        lax.all_gather(w_output, ("dp", "mp"), axis=0, tiled=True),
        lax.all_gather(w_router, ("dp", "mp"), axis=0, tiled=True),
        lax.all_gather(norm_gains.astype(jnp.bfloat16), ("dp", "mp"), axis=0, tiled=True).astype(
            norm_gains.dtype
        ),
        lax.all_gather(norm_biases.astype(jnp.bfloat16), ("dp", "mp"), axis=0, tiled=True).astype(
            norm_biases.dtype
        ),
    )
    up_part, down_part = (
        lax.all_gather(w_up, "dp", axis=0, tiled=True),
        lax.all_gather(w_down, "dp", axis=0, tiled=True),
    )
    residual = tokens.reshape(token_count, model_width).astype(jnp.float32)
    normed_one, plain_one, rstd_one = layer_norm(residual, full_gains[:, 0], full_biases[:, 0])
    input_one = normed_one.astype(jnp.bfloat16)
    queries = jnp.dot(input_one, full_query, preferred_element_type=jnp.float32).astype(
        jnp.bfloat16
    )
    keyvals = jnp.dot(input_one, full_keyval, preferred_element_type=jnp.float32).astype(
        jnp.bfloat16
    )
    logits = jnp.dot(input_one, full_router, preferred_element_type=jnp.float32)
    chosen = jnp.sum(
        (
            routes.reshape(token_count, -1)[:, :, None] == jnp.arange(head_count, dtype=jnp.int32)
        ).astype(jnp.float32),
        axis=1,
    )
    counts = lax.psum(jnp.sum(chosen, axis=0), ("dp", "mp"))
    gate_weights = jax.nn.softmax(jnp.where(chosen > 0, logits, -1e30), axis=-1)
    gathered_kv = lax.all_gather(
        keyvals.reshape(row_count, local_len, 2 * headsize), "mp", axis=1, tiled=True
    )
    query_pos = seq_place * local_len + jnp.arange(local_len, dtype=jnp.int32)
    key_pos = jnp.arange(length, dtype=jnp.int32)
    query_seg = lax.dynamic_slice_in_dim(segment_ids, seq_place * local_len, local_len, 1)
    score_scale = headsize ** (-0.5)
    queries = queries.reshape(row_count, local_len, head_count * headsize)
    head_pairs = head_count // 2
    blocks = row_count // 2 * head_pairs

    def block_scores(block_index):
        row_first = block_index // head_pairs * 2
        column = block_index % head_pairs * 2 * headsize
        query_block = lax.dynamic_slice(
            queries, (row_first, 0, column), (2, local_len, 2 * headsize)
        ).reshape(2, local_len, 2, headsize)
        same_doc = query_seg[:, :, None] == segment_ids[:, None, :]
        visible = (same_doc & (key_pos[None, :] <= query_pos[:, None])[None])[:, None]
        scores = (
            jnp.einsum(
                "rqhd,rkd->rhqk",
                query_block,
                gathered_kv[:, :, :headsize],
                preferred_element_type=jnp.float32,
            )
            * score_scale
        )
        return (jnp.where(visible, scores, -1e30), query_block, gathered_kv, row_first, column)

    def forward_step(block_index, state_pair):
        values, log_total = state_pair
        scores, query_block, kv_block, row_first, column = block_scores(block_index)
        highest = jnp.max(scores, axis=-1, keepdims=True)
        lifted = jnp.exp(scores - highest)
        totals = jnp.sum(lifted, axis=-1, keepdims=True)
        probs_low = (lifted / totals).astype(jnp.bfloat16)
        block_out = jnp.einsum(
            "rhqk,rkd->rqhd",
            probs_low,
            kv_block[:, :, headsize:],
            preferred_element_type=jnp.float32,
        )
        values = lax.dynamic_update_slice(
            values, block_out.reshape(2, local_len, 2 * headsize), (row_first, 0, column)
        )
        log_total = lax.dynamic_update_slice(
            log_total, (highest + jnp.log(totals))[..., 0], (row_first, column // headsize, 0)
        )
        return (values, log_total)

    values, log_total = lax.fori_loop(
        0,
        blocks,
        forward_step,
        (
            jnp.zeros((row_count, local_len, head_count * headsize), jnp.float32),
            jnp.zeros((row_count, head_count, local_len), jnp.float32),
        ),
    )
    attended = values.reshape(token_count, head_count, headsize)
    gated = (
        (attended * gate_weights[:, :, None])
        .astype(jnp.bfloat16)
        .reshape(token_count, head_count * headsize)
    )
    branch = against(gated, full_output)
    middle = residual + branch
    normed_two, plain_two, rstd_two = layer_norm(middle, full_gains[:, 1], full_biases[:, 1])
    input_two = normed_two.astype(jnp.bfloat16)
    grad_out = out_grad.reshape(token_count, model_width)
    gathered_in = lax.all_gather(input_two, "mp", axis=0, tiled=True)
    before = jnp.dot(gathered_in, up_part, preferred_element_type=jnp.float32)
    hidden = jax.nn.gelu(before).astype(jnp.bfloat16)
    ffn_out = lax.psum_scatter(
        against(hidden, down_part).astype(jnp.bfloat16), "mp", scatter_dimension=0, tiled=True
    ).astype(jnp.float32)
    gathered_grad = lax.all_gather(grad_out, "mp", axis=0, tiled=True)
    grad_hidden = jnp.dot(gathered_grad, down_part, preferred_element_type=jnp.float32)
    grad_before = jax.vjp(jax.nn.gelu, before)[1](grad_hidden)[0].astype(jnp.bfloat16)
    grad_normed_two = lax.psum_scatter(
        against(grad_before, up_part).astype(jnp.bfloat16), "mp", scatter_dimension=0, tiled=True
    ).astype(jnp.float32)
    up_grad = contract_rows(gathered_in, grad_before)
    down_grad = contract_rows(gathered_grad, hidden)
    up_grad, down_grad = side_by_side(
        (up_grad.astype(jnp.bfloat16), down_grad.astype(jnp.bfloat16)), "dp", 0, 1
    )
    outputs = (middle + ffn_out).astype(jnp.bfloat16).reshape(row_count, local_len, model_width)
    grad_middle = grad_out.astype(jnp.float32) + norm_back(
        grad_normed_two, plain_two, rstd_two, full_gains[:, 1]
    )
    gain_two = jnp.sum(grad_normed_two * plain_two, axis=0)
    bias_two = jnp.sum(grad_normed_two, axis=0)
    grad_branch = grad_middle.astype(jnp.bfloat16)
    output_grad = contract_rows(grad_branch, gated)
    grad_gated = jnp.dot(grad_branch, full_output, preferred_element_type=jnp.float32).reshape(
        token_count, head_count, headsize
    )
    grad_gate = jnp.sum(grad_gated * attended, axis=-1)
    grad_attended = (
        (grad_gated * gate_weights[:, :, None])
        .astype(jnp.bfloat16)
        .reshape(row_count, local_len, head_count * headsize)
    )
    grad_logits = (
        gate_weights * (grad_gate - jnp.sum(gate_weights * grad_gate, axis=-1, keepdims=True))
    ).astype(jnp.bfloat16)

    def backward_step(block_index, state_pair):
        grad_queries, grad_keyvals = state_pair
        scores, query_block, kv_block, row_first, column = block_scores(block_index)
        block_total = lax.dynamic_slice(
            log_total, (row_first, column // headsize, 0), (2, 2, local_len)
        )
        probs_full = jnp.exp(scores - block_total[..., None])
        grad_block = lax.dynamic_slice(
            grad_attended, (row_first, 0, column), (2, local_len, 2 * headsize)
        ).reshape(2, local_len, 2, headsize)
        grad_probs = jnp.einsum(
            "rqhd,rkd->rhqk",
            grad_block,
            kv_block[:, :, headsize:],
            preferred_element_type=jnp.float32,
        )
        grad_scores = (
            probs_full * (grad_probs - jnp.sum(probs_full * grad_probs, axis=-1, keepdims=True))
        ).astype(jnp.bfloat16)
        grad_qblock = (
            jnp.einsum(
                "rhqk,rkd->rqhd",
                grad_scores,
                kv_block[:, :, :headsize],
                preferred_element_type=jnp.float32,
            )
            * score_scale
        )
        grad_keys = (
            jnp.einsum(
                "rhqk,rqhd->rkd", grad_scores, query_block, preferred_element_type=jnp.float32
            )
            * score_scale
        )
        grad_values = jnp.einsum(
            "rhqk,rqhd->rkd",
            probs_full.astype(jnp.bfloat16),
            grad_block,
            preferred_element_type=jnp.float32,
        )
        grad_queries = lax.dynamic_update_slice(
            grad_queries, grad_qblock.reshape(2, local_len, 2 * headsize), (row_first, 0, column)
        )
        current = grad_keyvals
        grad_keyvals = current + jnp.concatenate([grad_keys, grad_values], axis=-1)
        return (grad_queries, grad_keyvals)

    grad_queries, grad_keyvals = lax.fori_loop(
        0,
        blocks,
        backward_step,
        (
            jnp.zeros((row_count, local_len, head_count * headsize), jnp.float32),
            jnp.zeros((row_count, length, 2 * headsize), jnp.float32),
        ),
    )
    grad_keyvals = lax.psum_scatter(
        grad_keyvals.astype(jnp.bfloat16), "mp", scatter_dimension=1, tiled=True
    ).reshape(token_count, 2 * headsize)
    grad_queries = grad_queries.astype(jnp.bfloat16).reshape(token_count, head_count * headsize)
    grad_normed_one = (
        against(grad_queries, full_query)
        + against(grad_keyvals, full_keyval)
        + against(grad_logits, full_router)
    )
    input_grad = grad_middle + norm_back(grad_normed_one, plain_one, rstd_one, full_gains[:, 0])
    gain_one = jnp.sum(grad_normed_one * plain_one, axis=0)
    bias_one = jnp.sum(grad_normed_one, axis=0)
    query_grad, keyval_grad, out_weight_grad, router_grad, gains_grad, biases_grad = (
        lax.psum_scatter(
            contract_rows(input_one, grad_queries), ("dp", "mp"), scatter_dimension=0, tiled=True
        ),
        lax.psum_scatter(
            contract_rows(input_one, grad_keyvals), ("dp", "mp"), scatter_dimension=0, tiled=True
        ),
        lax.psum_scatter(output_grad, ("dp", "mp"), scatter_dimension=0, tiled=True),
        lax.psum_scatter(
            contract_rows(input_one, grad_logits), ("dp", "mp"), scatter_dimension=0, tiled=True
        ),
        lax.psum_scatter(
            jnp.stack([gain_one, gain_two], axis=1), ("dp", "mp"), scatter_dimension=0, tiled=True
        ),
        lax.psum_scatter(
            jnp.stack([bias_one, bias_two], axis=1), ("dp", "mp"), scatter_dimension=0, tiled=True
        ),
    )
    return (
        outputs,
        input_grad.reshape(row_count, local_len, model_width),
        counts,
        query_grad,
        keyval_grad,
        out_weight_grad,
        router_grad,
        gains_grad,
        biases_grad,
        up_grad,
        down_grad,
    )


def solution(mesh):
    in_specs = (
        P("dp", "mp", None),
        P("dp", None),
        P("dp", "mp", None),
        P("dp", "mp", None),
        P(("dp", "mp"), None),
        P(("dp", "mp"), None),
        P(("dp", "mp"), None),
        P(("dp", "mp"), None),
        P(("dp", "mp"), None),
        P(("dp", "mp"), None),
        P("dp", "mp"),
        P("dp", "mp"),
    )
    out_specs = (
        P("dp", "mp", None),
        P("dp", "mp", None),
        P(),
        P(("dp", "mp"), None),
        P(("dp", "mp"), None),
        P(("dp", "mp"), None),
        P(("dp", "mp"), None),
        P(("dp", "mp"), None),
        P(("dp", "mp"), None),
        P("dp", "mp"),
        P("dp", "mp"),
    )
    return jax.shard_map(shards, mesh=mesh, in_specs=in_specs, out_specs=out_specs, check_vma=False)
```

profile of v0, /device:TPU:0, one launch (start us, length us, event | category | flops | bytes accessed | tf_op | source)
XLA Modules:
  0.0 2044.2 jit_solution(11629977940619635978)
XLA Ops:
  13.0 43.0 %all-gather.1 = bf16[32,16,2]{1,2,0:T(2,128)(2,1)S(1)} all-gather(bf16[1,16,2]{1,2,0:T(2,128)(2,1)S(1)} %convert_bitcast_fusion), channel_id=1, replica_groups=mesh['dp'=8,'mp'=4] {'dp','mp'}, dimensions={0}, use_global_device_ids=true | all-gather | bytes 2112 | tf_op jit(solution)/shard_map/all_gather | solution.py:87
  56.8 36.4 %all-gather = bf16[32,16,2]{1,2,0:T(2,128)(2,1)S(1)} all-gather(bf16[1,16,2]{1,2,0:T(2,128)(2,1)S(1)} %convert_bitcast_fusion.1), channel_id=1, replica_groups=mesh['dp'=8,'mp'=4] {'dp','mp'}, dimensions={0}, use_global_device_ids=true | all-gather | bytes 2112 | tf_op jit(solution)/shard_map/all_gather | solution.py:84
  93.6 38.6 %all_gather.36 = bf16[512,128]{1,0:T(8,128)(2,1)S(1)} all-gather(bf16[16,128]{1,0:T(8,128)(2,1)} %param.21), channel_id=1, replica_groups=mesh['dp'=8,'mp'=4] {'dp','mp'}, dimensions={0}, use_global_device_ids=true | all-gather | bytes 135168 | tf_op jit(solution)/shard_map/all_gather | solution.py:81
  138.6 37.3 %all_gather.38 = bf16[512,24]{1,0:T(8,128)(2,1)S(1)} all-gather(bf16[16,24]{1,0:T(8,128)(2,1)S(1)} %copy-done.39), channel_id=1, replica_groups=mesh['dp'=8,'mp'=4] {'dp','mp'}, dimensions={0}, use_global_device_ids=true | all-gather | bytes 25344 | tf_op jit(solution)/shard_map/all_gather | solution.py:83
  201.3 226.4 %while.36 = (s32[]{:T(128)}, f32[2,512,1536]{1,2,0:T(8,128)}, f32[2,24,512]{2,1,0:T(8,128)S(1)}, s32[2,512]{1,0:T(2,128)S(1)}, s32[2,2048]{1,0:T(2,128)S(1)}, /*...) while((s32[]{:T(128)}, f32[2,512,1536]{1,2,0:T(8,128)}, ...), condition=%wide.region_5.6_spmd.clone, body=%wide.region_2.5_spmd.clone.sunk | while | flops 1129314816 | bytes 64332220 | solution.py:164
  448.9 31.7 %all_gather.41 = bf16[512,512]{1,0:T(8,128)(2,1)S(1)} all-gather(bf16[64,512]{1,0:T(8,128)(2,1)S(1)} %copy-done.32), channel_id=1, replica_groups=mesh['dp'=8,'mp'=4] {'dp'}, dimensions={0}, use_global_device_ids=true | all-gather | bytes 589824 | tf_op jit(solution)/shard_map/all_gather | solution.py:92
  480.6 31.2 %all_gather.42 = bf16[512,512]{1,0:T(8,128)(2,1)S(1)} all-gather(bf16[64,512]{1,0:T(8,128)(2,1)S(1)} %copy-done.33), channel_id=1, replica_groups=mesh['dp'=8,'mp'=4] {'dp'}, dimensions={0}, use_global_device_ids=true | all-gather | bytes 589824 | tf_op jit(solution)/shard_map/all_gather | solution.py:93
  557.1 23.0 %reduce-scatter.16.cloned.1.call-done = bf16[1024,512]{1,0:T(8,128)(2,1)} async-done(((bf16[4096,512]{1,0:T(8,128)(2,1)}), bf16[1024,512]{1,0:T(8,128)(2,1)}) %reduce-scatter.16.cloned.1.call-update) | async-done | bytes 1048592 | tf_op jit(solution)/shard_map/reduce_scatter | solution.py:193
  583.6 43.7 %reduce-scatter.14.cloned.1.call-done = bf16[1024,512]{1,0:T(8,128)(2,1)} async-done(((bf16[4096,512]{1,0:T(8,128)(2,1)}), bf16[1024,512]{1,0:T(8,128)(2,1)}) %reduce-scatter.14.cloned.1.call-update) | async-done | bytes 1048592 | tf_op jit(solution)/shard_map/reduce_scatter | solution.py:187
  656.3 594.8 %while.37 = (s32[]{:T(128)}, bf16[2,512,1536]{2,1,0:T(8,128)(2,1)}, f32[2,2048,128]{1,2,0:T(8,128)S(1)}, s32[2,512]{1,0:T(2,128)S(1)}, s32[2,2048]{1,0:T(2,128)S...) while((s32[]{:T(128)}, bf16[2,512,1536]{2,1,0:T(8,128)(2,1)}, ...), condition=%wide.region_17.18_spmd.clone, body=%wide.region_15.17_spmd.clone.sunk | while | flops 2754607616 | bytes 217399824 | solution.py:269
  674.1 12.3 fusion.163
  686.4 12.1 fusion.164
  723.6 12.3 fusion.163
  773.2 12.3 fusion.163
  785.5 12.1 fusion.164
  822.7 12.3 fusion.163
  835.0 12.1 fusion.164
  872.2 12.3 fusion.163
  921.7 12.3 fusion.163
  971.3 12.3 fusion.163
  1020.8 12.3 fusion.163
  1070.3 12.3 fusion.163
  1119.9 12.3 fusion.163
  1169.4 12.3 fusion.163
  1219.0 12.3 fusion.163
  1330.5 45.3 %psum.7 = f32[24]{0:T(128)} all-reduce(f32[24]{0:T(128)S(1)} %copy-done.40), channel_id=1, replica_groups=mesh['dp'=8,'mp'=4] {'dp','mp'}, use_global_device_ids=true, to_apply=%region_24.25 | all-reduce | flops 24 | bytes 192 | tf_op jit(solution)/shard_map/psum | solution.py:111
  1381.0 47.5 %reduce-scatter.30.cloned.1.call-done = f32[16,2]{1,0:T(8,128)} async-done(((f32[512,2]{1,0:T(8,128)}), f32[16,2]{1,0:T(8,128)}) %reduce-scatter.30.cloned.1.call-update) | async-done | bytes 144
  1429.8 130.6 %reduce-scatter.28.cloned.1.call-done = f32[16,2]{1,0:T(8,128)} async-done(((f32[512,2]{1,0:T(8,128)}), f32[16,2]{1,0:T(8,128)}) %reduce-scatter.28.cloned.1.call-update) | async-done | bytes 144
  1561.8 131.3 %reduce-scatter.26.cloned.1.call-done = f32[16,24]{1,0:T(8,128)} async-done(((f32[512,24]{1,0:T(8,128)}), f32[16,24]{1,0:T(8,128)}) %reduce-scatter.26.cloned.1.call-update) | async-done | bytes 1552 | tf_op jit(solution)/shard_map/reduce_scatter | solution.py:298
  1693.1 132.4 %reduce-scatter.22.cloned.1.call-done = f32[16,128]{1,0:T(8,128)} async-done(((f32[512,128]{1,0:T(8,128)}), f32[16,128]{1,0:T(8,128)}) %reduce-scatter.22.cloned.1.call-update) | async-done | bytes 8208 | tf_op jit(solution)/shard_map/reduce_scatter | solution.py:294
  1825.5 104.4 %reduce-scatter.24.cloned.1.call-done = f32[16,1536]{1,0:T(8,128)} async-done(((f32[512,1536]{1,0:T(8,128)}), f32[16,1536]{1,0:T(8,128)}) %reduce-scatter.24.cloned.1.call-update) | async-done | bytes 98320 | tf_op jit(solution)/shard_map/reduce_scatter | solution.py:297
  1929.9 107.3 %reduce-scatter.20.cloned.1.call-done = f32[16,1536]{1,0:T(8,128)} async-done(((f32[512,1536]{1,0:T(8,128)}), f32[16,1536]{1,0:T(8,128)}) %reduce-scatter.20.cloned.1.call-update) | async-done | bytes 98320 | tf_op jit(solution)/shard_map/reduce_scatter | solution.py:291
  (524 shorter events, 859.2 us)
Async XLA Ops:
  7.2 130.7 %copy-start.34 = (s32[2,512,8]{1,2,0:T(8,128)S(1)}, s32[2,512,8]{1,2,0:T(8,128)}, u32[]{:S(2)}) copy-start(s32[2,512,8]{1,2,0:T(8,128)} %param.18) | copy-start | bytes 98308
  7.2 131.4 %copy-start.39 = (bf16[16,24]{1,0:T(8,128)(2,1)S(1)}, bf16[16,24]{1,0:T(8,128)(2,1)}, u32[]{:S(2)}) copy-start(bf16[16,24]{1,0:T(8,128)(2,1)} %param.23) | copy-start | bytes 2308
  7.2 181.1 %all-gather.8.cloned.1.call-start = ((), (), s32[]{:S(2)}) async-start(), calls=%async_computation.10 | async-start | bytes 1622016 | tf_op jit(solution)/shard_map/all_gather | solution.py:80
  7.9 189.9 %all-gather.10.cloned.1.call-start = ((), (), s32[]{:S(2)}) async-start(), calls=%async_computation.11 | async-start | bytes 1310720 | tf_op jit(solution)/shard_map/all_gather | solution.py:113
  9.5 124.0 %copy-start.26 = (f32[1,4,2,128]{3,1,2,0:T(4,128)}, f32[1,4,2,128]{3,1,2,0:T(4,128)S(1)}, u32[]{:S(2)}) copy-start(f32[1,4,2,128]{3,1,2,0:T(4,128)S(1)} %copy.133) | copy-start | bytes 12292
  12.3 121.1 %copy-start.28 = (f32[1,4,2,128]{3,1,2,0:T(4,128)}, f32[1,4,2,128]{3,1,2,0:T(4,128)S(1)}, u32[]{:S(2)}) copy-start(f32[1,4,2,128]{3,1,2,0:T(4,128)S(1)} %copy.134) | copy-start | bytes 12292
  135.1 53.1 %copy-start.7 = (bf16[1024,512]{1,0:T(8,128)(2,1)}, bf16[1024,512]{1,0:T(8,128)(2,1)S(1)}, u32[]{:S(2)}) copy-start(bf16[1024,512]{1,0:T(8,128)(2,1)S(1)} %fusion.68) | copy-start | bytes 3145732
  136.5 305.4 %all-gather.12.cloned.1.call-start = ((), (), s32[]{:S(2)}) async-start(), calls=%async_computation.12 | async-start | bytes 1622016 | tf_op jit(solution)/shard_map/all_gather | solution.py:82
  137.2 374.7 %all-gather.16.cloned.1.call-start = ((), (), s32[]{:S(2)}) async-start(), calls=%async_computation.15 | async-start | bytes 5242880 | tf_op jit(solution)/shard_map/all_gather | solution.py:190
  137.8 381.8 %all-gather.14.cloned.1.call-start = ((), (), s32[]{:S(2)}) async-start(), calls=%async_computation.13 | async-start | bytes 5242880 | tf_op jit(solution)/shard_map/all_gather | solution.py:184
  181.7 6.6 copy-start.11
  434.5 7.4 copy-start.4
  446.1 34.5 %copy-start.33 = (bf16[64,512]{1,0:T(8,128)(2,1)S(1)}, bf16[64,512]{1,0:T(8,128)(2,1)}, u32[]{:S(2)}) copy-start(bf16[64,512]{1,0:T(8,128)(2,1)} %param.27) | copy-start | bytes 196612
  448.8 131.2 %reduce-scatter.16.cloned.1.call-start = ((), (), s32[]{:S(2)}) async-start(), calls=%async_computation.16 | async-start | bytes 5242880 | tf_op jit(solution)/shard_map/reduce_scatter | solution.py:193
  537.9 89.4 %reduce-scatter.14.cloned.1.call-start = ((), (), s32[]{:S(2)}) async-start(), calls=%async_computation.14 | async-start | bytes 5242880 | tf_op jit(solution)/shard_map/reduce_scatter | solution.py:187
  547.6 741.6 %reduce-scatter.18.cloned.1.call-start = ((), (), s32[]{:S(2)}) async-start(), calls=%async_computation.17 | async-start | bytes 1310720 | tf_op jit(solution)/shard_map/reduce_scatter | solution.py:278
  1252.6 175.9 %reduce-scatter.30.cloned.1.call-start = ((), (), s32[]{:S(2)}) async-start(), calls=%async_computation.23 | async-start | bytes 270336
  1280.6 6.6 copy-start.8
  1280.6 6.6 copy-start.42
  1290.6 6.8 copy-start.18
  1290.6 6.8 copy-start.21
  1290.7 6.8 copy-start.25
  1293.0 7.0 copy-start.3
  1293.9 266.5 %reduce-scatter.28.cloned.1.call-start = ((), (), s32[]{:S(2)}) async-start(), calls=%async_computation.22 | async-start | bytes 270336
  1294.9 398.2 %reduce-scatter.26.cloned.1.call-start = ((), (), s32[]{:S(2)}) async-start(), calls=%async_computation.21 | async-start | bytes 270336 | tf_op jit(solution)/shard_map/reduce_scatter | solution.py:298
  1297.4 528.2 %reduce-scatter.22.cloned.1.call-start = ((), (), s32[]{:S(2)}) async-start(), calls=%async_computation.19 | async-start | bytes 270336 | tf_op jit(solution)/shard_map/reduce_scatter | solution.py:294
  1300.0 629.9 %reduce-scatter.24.cloned.1.call-start = ((), (), s32[]{:S(2)}) async-start(), calls=%async_computation.20 | async-start | bytes 3244032 | tf_op jit(solution)/shard_map/reduce_scatter | solution.py:297
  1305.4 731.8 %reduce-scatter.20.cloned.1.call-start = ((), (), s32[]{:S(2)}) async-start(), calls=%async_computation.18 | async-start | bytes 3244032 | tf_op jit(solution)/shard_map/reduce_scatter | solution.py:291
  1311.3 7.9 copy-start.41
  1311.4 7.9 copy-start.44
  1321.7 8.8 copy-start.40
  1325.0 50.8 %all-to-all-start = ((bf16[8,64,1024]{2,1,0:T(8,128)(2,1)}), bf16[8,64,1024]{2,1,0:T(8,128)(2,1)}, u32[]{:S(2)}, u32[]{:S(2)}) async-start(bf16[8,64,1024]{2,1,0:T(8,128)(2,1)} %bitcast.256), calls=%async_computation.7 | async-start | bytes 2097152 | tf_op jit(solution)/shard_map/all_to_all | solution.py:16
  (39 other events, 152.7 us)
Sparse Core Ops, SparseCore 0:
  10.9 57.7 all-gather.7
  136.6 13.1 all-gather.9
  152.7 54.9 all-gather.11
  209.1 33.3 all-gather.15
  448.9 32.0 all-gather.13
  538.0 41.9 reduce-scatter.15
  582.7 44.5 reduce-scatter.13
  1252.7 24.8 reduce-scatter.17
  1294.1 134.4 reduce-scatter.29
  1430.6 129.8 reduce-scatter.27
  1563.4 129.7 reduce-scatter.25
  1695.8 129.7 reduce-scatter.21
  1832.4 97.4 reduce-scatter.23
  1936.7 100.5 reduce-scatter.19
where the time goes:
time: 2050 us; the launch traced here: 2040 us
  waiting for transfers between devices  722 us (35%)
  matrix products  478 us (23%)
  other arithmetic  316 us (15%)
  blocking collectives  264 us (13%)
  local copies, waits for them, and re-layouts  241 us (12%)
    unnamed x16, waiting for transfers between devices  180 us
    dot_general x12, matrix products, backward_step(): jnp.einsum('rqhd,rkd->rhqk', grad_block, kv_block[:, :, headsize:], prefe...  148 us
    convert_element_type x12, other arithmetic, backward_step(): grad_scores = (probs_full * (grad_probs - jnp.sum(probs_full * grad_probs...  146 us
    reduce_scatter x1, waiting for transfers between devices, shards(): lax.psum_scatter(contract_rows(input_one, grad_keyvals), ('dp', 'mp'), sc...  132 us
    reduce_scatter x1, waiting for transfers between devices, shards(): lax.psum_scatter(contract_rows(input_one, grad_logits), ('dp', 'mp'), sca...  131 us
    reduce_scatter x1, waiting for transfers between devices, shards(): lax.psum_scatter(contract_rows(input_one, grad_queries), ('dp', 'mp'), sc...  107 us
    reduce_scatter x1, waiting for transfers between devices, shards(): lax.psum_scatter(output_grad, ('dp', 'mp'), scatter_dimension=0, tiled=True)  104 us
    dot_general x24, matrix products, block_scores(): jnp.einsum('rqhd,rkd->rhqk', query_block, gathered_kv[:, :, :headsize], p...  72.2 us
  transfers between devices with their start and end apart: 15, of which 8 were waited for; matrix products, arithmetic and copies ran while one was open for 19% of the time, Pallas kernels for 0%

commit v1 on v0

v1 whole, which is shorter than its diff:
```python
import functools
import math
import jax
import jax.numpy as jnp
from jax import lax
from jax.experimental import pallas as pl
from jax.experimental.pallas import tpu as pltpu
from jax.sharding import PartitionSpec as P

epsilon = 1e-05
f32, bf16 = jnp.float32, jnp.bfloat16
NN = (((1,), (0,)), ((), ()))
NT = (((1,), (1,)), ((), ()))
LANES = 128
LOG2E = math.log2(math.e)
MIB = 2**20


def dot(left, right, dims=NN):
    return lax.dot_general(left, right, dims, preferred_element_type=f32)


def bits_of(axis):
    return (lax.axis_size(axis) - 1).bit_length()


def bit_groups(axis):
    count = bits_of(axis)
    groups, at = [], 0
    if count % 2:
        groups.append((0, 1))
        at = 1
    while at < count:
        groups.append((at, 2))
        at += 2
    return groups


def flip(x, axis, mask):
    return lax.ppermute(x, axis, [(i, i ^ mask) for i in range(lax.axis_size(axis))])


def gather_bits(x, axis, group, dim):
    low, width = group
    mine = lax.axis_index(axis) >> low
    pieces = [x] + [flip(x, axis, k << low) for k in range(1, 2**width)]
    for b in range(width):
        odd = (mine >> b) & 1 == 1
        pieces = [jnp.where(odd, pieces[q ^ (1 << b)], pieces[q]) for q in range(2**width)]
    return jnp.stack(pieces, axis=dim)


def gather_axis(x, axis, dim):
    for group in reversed(bit_groups(axis)):
        x = gather_bits(x, axis, group, dim)
        dim += 1
    return x


def gather_each_bit(x, axis, dim):
    for b in reversed(range(bits_of(axis))):
        x = gather_bits(x, axis, (b, 1), dim)
        dim += 1
    return x


def scatter_bits(x, axis, group, dim):
    low, width = group
    mine = (lax.axis_index(axis) >> low) & (2**width - 1)
    total = None
    got = [
        flip(lax.dynamic_index_in_dim(x, mine ^ k, dim, keepdims=False), axis, k << low)
        for k in range(1, 2**width)
    ]
    total = lax.dynamic_index_in_dim(x, mine, dim, keepdims=False).astype(f32)
    for g in got:
        total = total + g.astype(f32)
    return total


def split_dims(axis, each):
    groups = [(b, 1) for b in range(bits_of(axis))] if each else bit_groups(axis)
    return groups, [2**width for _, width in reversed(groups)]


def halves(row_first, row_second, like):
    lane = lax.broadcasted_iota(jnp.int32, like, 1)
    return jnp.where(lane < LANES // 2, row_first, row_second)


def slot_experts(routes, pairs):
    shape = (routes.shape[0], LANES)
    return [halves(routes[:, 2 * j : 2 * j + 1], routes[:, 2 * j + 1 : 2 * j + 2], shape) for j in range(pairs)]


def turn_half(x):
    return pltpu.roll(x, LANES // 2, 1)


def compact(wide, experts, head_pairs):
    lane = lax.broadcasted_iota(jnp.int32, experts[0].shape, 1)
    high = (lane >= LANES // 2).astype(jnp.int32)
    straight = [e - high for e in experts]
    crossed = [e + high for e in experts]
    found = [jnp.zeros(experts[0].shape, f32) for _ in experts]
    for i in range(head_pairs):
        block = wide(i)
        turned = turn_half(block)
        for j in range(len(experts)):
            found[j] = jnp.where(straight[j] == 2 * i, block, found[j])
            found[j] = jnp.where(crossed[j] == 2 * i + 1, turned, found[j])
    return found


def expand(narrow, experts, head_pairs):
    lane = lax.broadcasted_iota(jnp.int32, experts[0].shape, 1)
    high = (lane >= LANES // 2).astype(jnp.int32)
    sources = []
    for block, e in zip(narrow, experts):
        sources.append((e - high, block))
        sources.append((turn_half(e) - high, turn_half(block)))
    wide = []
    for i in range(head_pairs):
        out = jnp.zeros(experts[0].shape, f32)
        for e, block in sources:
            out = jnp.where(e == 2 * i, block, out)
        wide.append(out.astype(bf16))
    return jnp.concatenate(wide, axis=1)


def normed_parts(values):
    mean = jnp.mean(values, axis=1, keepdims=True)
    centred = values - mean
    rstd = lax.rsqrt(jnp.mean(centred * centred, axis=1, keepdims=True) + epsilon)
    return centred * rstd, rstd


def norm_back(grad, normed, rstd, gain):
    scaled = grad * gain
    return rstd * (
        scaled
        - jnp.mean(scaled, axis=1, keepdims=True)
        - normed * jnp.mean(scaled * normed, axis=1, keepdims=True)
    )


def norm_kernel(x_ref, w_ref, n_ref, kv_ref, norms_ref, *, at_kv, at_misc, heads):
    misc = w_ref[:, at_misc : at_misc + LANES].astype(f32).T
    norms = misc[heads : heads + 8, :]
    norms = jnp.concatenate(
        [norms[0:2] + norms[2:4], norms[4:6] + norms[6:8], jnp.zeros_like(norms[0:4])], axis=0
    )
    norms_ref[...] = norms
    normed, _ = normed_parts(x_ref[0].astype(f32))
    low = (normed * norms[0:1] + norms[2:3]).astype(bf16)
    n_ref[0] = low
    kv_ref[0] = dot(low, w_ref[:, at_kv : at_kv + LANES]).astype(bf16)


def query_kernel(
    n_ref, w_ref, routes_ref, routes_t_ref, q_ref, gate_ref, gate_t_ref, *, at_misc, heads, slots, hs
):
    low = n_ref[0]
    head_pairs = heads // 2
    queries = dot(low, w_ref[:, : heads * hs]) * (hs**-0.5 * LOG2E)
    experts = slot_experts(routes_ref[0], slots // 2)
    found = compact(lambda i: queries[:, i * LANES : (i + 1) * LANES], experts, head_pairs)
    q_ref[0] = jnp.concatenate([f.astype(bf16) for f in found], axis=1)
    logits = dot(low, w_ref[:, at_misc : at_misc + LANES]).T[:heads, :]
    expert = lax.broadcasted_iota(jnp.int32, logits.shape, 0)
    routes_t = routes_t_ref[0]
    picked = [
        jnp.sum(jnp.where(expert == routes_t[s : s + 1, :], logits, 0.0), axis=0, keepdims=True)
        for s in range(slots)
    ]
    chosen = jnp.concatenate(picked, axis=0)
    lifted = jnp.exp(chosen - jnp.max(chosen, axis=0, keepdims=True))
    gate = lifted / jnp.sum(lifted, axis=0, keepdims=True)
    gate_t_ref[0] = gate
    padded = jnp.concatenate([gate, jnp.zeros((LANES - slots, gate.shape[1]), f32)], axis=0)
    gate_ref[0] = padded.T


def key_bias(first_key, first_query, start, keys, queries):
    key = first_key + lax.broadcasted_iota(jnp.int32, (keys, queries), 0)
    query = first_query + lax.broadcasted_iota(jnp.int32, (keys, queries), 1)
    return jnp.where((key <= query) & (key >= start), 0.0, -1e30)


def kv_place(row, chunk, rows, peers):
    half = chunk % 2
    owner = jnp.where(half == 0, chunk // 2, peers - 1 - chunk // 2)
    return owner * (2 * rows) + row * 2 + half


def over_keys(plan, start_ref, bias, block, keys, queries):
    b = pl.program_id(0)
    row, last, first, full = plan[4 * b], plan[4 * b + 1], plan[4 * b + 2], plan[4 * b + 3]

    def masked(i, carry):
        chunk = jnp.where(i == 0, last, first + i - 1)
        bias[...] = key_bias(chunk * keys, last * keys, start_ref[0], keys, queries)
        block(row, chunk, True)
        return carry

    def plain(chunk, carry):
        block(row, chunk, False)
        return carry

    lax.fori_loop(0, 1 + full - first, masked, 0)
    lax.fori_loop(full, last, plain, 0)


def attend_kernel(
    plan, q_ref, kv_ref, start_ref, gate_ref, out_ref, lse_ref, kvt, qt, acc, top, tot, bias, *, slots, hs, rows, peers
):
    queries, keys = q_ref.shape[1], kv_ref.shape[1]

    @pl.when(pl.program_id(0) == 0)
    def _():
        for i in range(kv_ref.shape[0]):
            kvt[i] = kv_ref[i].T

    qt[...] = q_ref[0].T
    acc[...] = jnp.zeros_like(acc)
    top[...] = jnp.full_like(top, -1e30)
    tot[...] = jnp.zeros_like(tot)
    part = [slice(h * hs, (h + 1) * hs) for h in range(slots)]

    def block(row, chunk, masked):
        at = kv_place(row, chunk, rows, peers)
        k = kv_ref[at][:, :hs]
        vt = kvt[at, hs : 2 * hs, :]
        tops, tots = top[...], tot[...]
        scores = [dot(k, qt[part[h], :]) for h in range(slots)]
        if masked:
            scores = [s + bias[...] for s in scores]
        highest = [
            jnp.maximum(tops[h : h + 1], jnp.max(scores[h], axis=0, keepdims=True)) for h in range(slots)
        ]
        probs = [jnp.exp2(scores[h] - highest[h]) for h in range(slots)]
        shrink = [jnp.exp2(tops[h : h + 1] - highest[h]) for h in range(slots)]
        totals = [
            tots[h : h + 1] * shrink[h] + jnp.sum(probs[h], axis=0, keepdims=True) for h in range(slots)
        ]
        for h in range(slots):
            acc[part[h], :] = acc[part[h], :] * shrink[h] + dot(vt, probs[h].astype(bf16))
        top[...] = jnp.concatenate(highest, axis=0)
        tot[...] = jnp.concatenate(totals, axis=0)

    over_keys(plan, start_ref, bias, block, keys, queries)
    for h in range(slots):
        acc[part[h], :] = acc[part[h], :] * (gate_ref[0, h : h + 1, :] / tot[h : h + 1, :])
    lse_ref[0] = top[...] + jnp.log2(tot[...])
    out_ref[0] = acc[...].astype(bf16).T


def attend_back_kernel(
    plan, q_ref, g_ref, kv_ref, start_ref, lse_ref, delta_ref, dq_ref, dkv_ref,
    kvt, v_rows, qt, gt, dqt, dk, dv, bias, *, slots, hs, rows, peers,
):
    queries, keys = q_ref.shape[1], kv_ref.shape[1]
    b = pl.program_id(0)

    @pl.when(b == 0)
    def _():
        for i in range(kv_ref.shape[0]):
            kvt[i] = kv_ref[i].T
            v_rows[i] = kv_ref[i][:, hs:]
        dk[...] = jnp.zeros_like(dk)
        dv[...] = jnp.zeros_like(dv)

    qt[...] = q_ref[0].T
    gt[...] = g_ref[0].T
    dqt[...] = jnp.zeros_like(dqt)
    part = [slice(h * hs, (h + 1) * hs) for h in range(slots)]

    def block(row, chunk, masked):
        at = kv_place(row, chunk, rows, peers)
        k = kv_ref[at][:, :hs]
        v = v_rows[at]
        kt = kvt[at, :hs, :]
        scores = [dot(k, qt[part[h], :]) for h in range(slots)]
        grads = [dot(v, gt[part[h], :]) for h in range(slots)]
        if masked:
            scores = [s + bias[...] for s in scores]
        probs = [jnp.exp2(scores[h] - lse_ref[0, h : h + 1, :]) for h in range(slots)]
        ds = [(probs[h] * (grads[h] - delta_ref[0, h : h + 1, :])).astype(bf16) for h in range(slots)]
        low = [p.astype(bf16) for p in probs]
        for h in range(slots):
            dqt[part[h], :] += dot(kt, ds[h])
        dk[at] += sum(dot(ds[h], qt[part[h], :], NT) for h in range(slots))
        dv[at] += sum(dot(low[h], gt[part[h], :], NT) for h in range(slots))

    over_keys(plan, start_ref, bias, block, keys, queries)
    dq_ref[0] = (dqt[...] * hs**-0.5).astype(bf16).T

    @pl.when(b == pl.num_programs(0) - 1)
    def _():
        for i in range(kv_ref.shape[0]):
            dkv_ref[i] = jnp.concatenate([dk[i] * (1.0 / LOG2E), dv[i]], axis=1).astype(bf16)


def middle_kernel(
    gc_ref, gate_ref, routes_ref, x_ref, og_ref, wo_ref, ff_ref, norms_ref,
    out_ref, gm_ref, gbr_ref, gated_ref, n2_ref, hid_ref, gbef_ref, gatt_ref, delta_ref, glog_ref, sums_ref,
    *, heads, slots, hs, width,
):
    tokens, model = x_ref.shape[1], x_ref.shape[2]
    head_pairs, pairs = heads // 2, slots // 2
    experts = slot_experts(routes_ref[0], pairs)
    gc = [gc_ref[0][:, j * LANES : (j + 1) * LANES].astype(f32) for j in range(pairs)]
    gated = expand(gc, experts, head_pairs)
    gated_ref[0] = gated
    middle = x_ref[0].astype(f32) + dot(gated, wo_ref[...], NT)
    gain, shift = norms_ref[1:2, :], norms_ref[3:4, :]
    vhat, rstd = normed_parts(middle)
    low = (vhat * gain + shift).astype(bf16)
    n2_ref[0] = low
    og = og_ref[0]
    out = middle
    back = jnp.zeros((tokens, model), f32)
    slope = math.sqrt(2.0 / math.pi)
    for c in range(ff_ref.shape[0]):
        up, down = ff_ref[c, :, :width], ff_ref[c, :, width:]
        v = dot(low, up)
        square = v * v
        bent = jnp.tanh(slope * v * (1.0 + 0.044715 * square))
        rise = 0.5 * (1.0 + bent)
        hidden = (v * rise).astype(bf16)
        slant = rise + 0.5 * v * (1.0 - bent * bent) * (slope + 3.0 * slope * 0.044715 * square)
        before = (dot(og, down) * slant).astype(bf16)
        out = out + dot(hidden, down, NT)
        back = back + dot(before, up, NT)
        hid_ref[0, :, c * width : (c + 1) * width] = hidden
        gbef_ref[0, :, c * width : (c + 1) * width] = before
    out_ref[0] = out.astype(bf16)
    gm = og.astype(f32) + norm_back(back, vhat, rstd, gain)
    gm_ref[0] = gm
    sums = jnp.concatenate(
        [
            jnp.sum(back * vhat, axis=0, keepdims=True),
            jnp.sum(back, axis=0, keepdims=True),
            jnp.zeros((6, model), f32),
        ],
        axis=0,
    )

    @pl.when(pl.program_id(0) == 0)
    def _():
        sums_ref[...] = jnp.zeros_like(sums_ref)

    sums_ref[...] += sums
    gbr = gm.astype(bf16)
    gbr_ref[0] = gbr
    found = compact(
        lambda i: dot(gbr, wo_ref[:, i * LANES : (i + 1) * LANES]), experts, head_pairs
    )
    gate = gate_ref[0]
    shape = (tokens, LANES)
    attended, products = [], []
    for j in range(pairs):
        spread = halves(gate[:, 2 * j : 2 * j + 1], gate[:, 2 * j + 1 : 2 * j + 2], shape)
        attended.append((found[j] * spread).astype(bf16))
        products.append(found[j] * gc[j])
    gatt_ref[0] = jnp.concatenate(attended, axis=1)
    product = jnp.concatenate(products, axis=1)
    owner = lax.broadcasted_iota(jnp.int32, (slots * hs, LANES), 0) // hs
    ones = (owner == lax.broadcasted_iota(jnp.int32, (slots * hs, LANES), 1)).astype(bf16)
    coarse = product.astype(bf16)
    fine = (product - coarse.astype(f32)).astype(bf16)
    inner = dot(coarse, ones) + dot(fine, ones)
    delta_ref[0] = inner.T[:slots, :]
    logit = inner - gate * jnp.sum(inner, axis=1, keepdims=True)
    lane = lax.broadcasted_iota(jnp.int32, shape, 1)
    spread_out = jnp.zeros(shape, f32)
    routes = routes_ref[0]
    for s in range(slots):
        spread_out = jnp.where(lane == routes[:, s : s + 1], logit[:, s : s + 1], spread_out)
    glog_ref[0] = spread_out.astype(bf16)


def weights_kernel(
    n2_ref, og_ref, gbr_ref, gbef_ref, hid_ref, gated_ref, ff_ref, wo_ref, n2t, ogt, gbrt, *, width
):
    @pl.when(pl.program_id(0) == 0)
    def _():
        n2t[...] = n2_ref[...].T
        ogt[...] = og_ref[...].T
        gbrt[...] = gbr_ref[...].T

    ff_ref[0, :, :width] = dot(n2t[...], gbef_ref[...]).astype(bf16)
    ff_ref[0, :, width:] = dot(ogt[...], hid_ref[...]).astype(bf16)
    wo_ref[...] = dot(gbrt[...], gated_ref[...]).astype(bf16)


def query_back_kernel(
    dq_ref, routes_ref, n_ref, w_ref, glog_ref, wq_ref, wr_ref, dn_ref, accq, accr, *, at_misc, heads, slots, hs
):
    pairs = slots // 2
    experts = slot_experts(routes_ref[0], pairs)
    dq = [dq_ref[0][:, j * LANES : (j + 1) * LANES].astype(f32) for j in range(pairs)]
    wide = expand(dq, experts, heads // 2)
    nt = n_ref[0].T
    glog = glog_ref[0]
    dn_ref[0] = dot(wide, w_ref[:, : heads * hs], NT) + dot(
        glog, w_ref[:, at_misc : at_misc + LANES], NT
    )

    @pl.when(pl.program_id(0) == 0)
    def _():
        accq[...] = jnp.zeros_like(accq)
        accr[...] = jnp.zeros_like(accr)

    accq[...] += dot(nt, wide)
    accr[...] += dot(nt, glog)

    @pl.when(pl.program_id(0) == pl.num_programs(0) - 1)
    def _():
        wq_ref[...] = accq[...].astype(bf16)
        wr_ref[...] = accr[...]


def input_kernel(
    dn_ref, dkv_ref, w_ref, x_ref, n_ref, gm_ref, norms_ref, wr_ref, sums_ref, ig_ref, small_ref, acck, sums, *, at_kv, heads
):
    dkv = dkv_ref[0]
    dn = dn_ref[0] + dot(dkv, w_ref[:, at_kv : at_kv + LANES], NT)
    vhat, rstd = normed_parts(x_ref[0].astype(f32))
    ig_ref[0] = gm_ref[0] + norm_back(dn, vhat, rstd, norms_ref[0:1, :])

    @pl.when(pl.program_id(0) == 0)
    def _():
        acck[...] = jnp.zeros_like(acck)
        sums[...] = jnp.zeros_like(sums)

    acck[...] += dot(n_ref[0].T, dkv)
    sums[0:1, :] += jnp.sum(dn * vhat, axis=0, keepdims=True)
    sums[1:2, :] += jnp.sum(dn, axis=0, keepdims=True)

    @pl.when(pl.program_id(0) == pl.num_programs(0) - 1)
    def _():
        second = sums_ref[...]
        model = second.shape[1]
        rows = jnp.concatenate(
            [
                jnp.zeros((heads, model), f32),
                sums[0:1, :], second[0:1, :], sums[1:2, :], second[1:2, :],
                jnp.zeros((LANES - heads - 4, model), f32),
            ],
            axis=0,
        )
        small_ref[:, :LANES] = acck[...].astype(bf16)
        small_ref[:, LANES:] = (wr_ref[...] + rows.T).astype(bf16)


def fixed(shape):
    return pl.BlockSpec(shape, lambda b, *_: (0,) * len(shape))


def per_block(*shape):
    return pl.BlockSpec((1, *shape), lambda b, *_: (b,) + (0,) * len(shape))


def like(shape, kind):
    return jax.ShapeDtypeStruct(shape, kind)


def cost(flops, size, exps=0):
    return pl.CostEstimate(flops=int(flops), bytes_accessed=int(size), transcendentals=int(exps))


def shards(
    tokens, segment_ids, routes, out_grad, w_query, w_keyval, w_output, w_router,
    norm_gains, norm_biases, w_up, w_down,
):
    rows, local, model = tokens.shape
    peers = lax.axis_size("mp")
    slots = routes.shape[2]
    heads = w_router.shape[1]
    hs = w_keyval.shape[1] // 2
    width = w_up.shape[1]
    chunk = local // 2
    blocks = rows * 2
    count = rows * local
    place = lax.axis_index("mp")
    wide = heads * hs
    slim = slots * hs
    at_kv, at_misc = wide, wide + 2 * hs

    def two(v):
        high = lax.reduce_precision(v, 8, 7)
        return [high.astype(bf16), (v - high).astype(bf16)]

    pads = jnp.zeros((w_query.shape[0], LANES - heads - 8), bf16)
    first = jnp.concatenate(
        [w_query, w_keyval, w_router, *two(norm_gains), *two(norm_biases), pads], axis=1
    )
    first = gather_axis(first, "dp", 0)
    held_out, held_up, held_down, first = lax.optimization_barrier((w_output, w_up, w_down, first))
    first = gather_each_bit(first, "mp", len(bit_groups("dp")))
    weights = first.reshape(model, at_misc + LANES)

    def swap(a):
        return flip(a, "mp", peers - 1)

    half_tokens = tokens[:, chunk:, :].reshape(rows * chunk, model)
    half_routes = routes[:, chunk:, :].astype(bf16).reshape(-1, model)
    met = swap(jnp.concatenate([half_tokens, half_routes], axis=0))
    met_tokens = met[: rows * chunk].reshape(rows, chunk, model)
    met_routes = met[rows * chunk :].reshape(rows, chunk, slots).astype(jnp.int32)

    def joined(near, far):
        return jnp.stack([near[:, :chunk], far], axis=1).reshape(blocks, chunk, -1)

    x = joined(tokens, met_tokens)
    picks = joined(routes, met_routes)
    picks_t = jnp.swapaxes(picks, 1, 2)
    chosen = (routes[..., None] == jnp.arange(heads, dtype=jnp.int32)).astype(f32)
    counts = lax.psum(jnp.sum(chosen, axis=(0, 1, 2)), ("dp", "mp"))

    near, far = 2 * place, 2 * (peers - 1 - place) + 1
    ids = jnp.arange(8, dtype=jnp.int32)
    sizes = jnp.sum((segment_ids[:, :, None] == ids).astype(jnp.int32), axis=1)
    own = jnp.stack(
        [lax.dynamic_slice_in_dim(segment_ids, c * chunk, chunk, 1) for c in (near, far)], axis=1
    )
    start = jnp.sum(jnp.where(ids < own[..., None], sizes[:, None, None, :], 0), axis=-1)
    last = jnp.broadcast_to(jnp.stack([near, far]), (rows, 2))
    full = jnp.minimum((start[:, :, -1] + chunk - 1) // chunk, last)
    which = jnp.broadcast_to(jnp.arange(rows, dtype=jnp.int32)[:, None], (rows, 2))
    plan = jnp.stack([which, last, start[:, :, 0] // chunk, full], axis=-1).astype(jnp.int32)
    plan = plan.reshape(-1)
    start = start.astype(jnp.int32).reshape(blocks, 1, chunk)

    n1, kv, norms = pl.pallas_call(
        functools.partial(norm_kernel, at_kv=at_kv, at_misc=at_misc, heads=heads),
        grid=(blocks,),
        in_specs=[per_block(chunk, model), fixed(weights.shape)],
        out_specs=[per_block(chunk, model), per_block(chunk, 2 * hs), fixed((8, model))],
        out_shape=[
            like((blocks, chunk, model), bf16),
            like((blocks, chunk, 2 * hs), bf16),
            like((8, model), f32),
        ],
        cost_estimate=cost(2 * count * model * LANES, 4 * MIB),
        name="norm_one",
    )(x, weights)
    kv_all = gather_each_bit(kv, "mp", 0).reshape(peers * blocks, chunk, 2 * hs)

    q, gate, gate_t = pl.pallas_call(
        functools.partial(query_kernel, at_misc=at_misc, heads=heads, slots=slots, hs=hs),
        grid=(blocks,),
        in_specs=[
            per_block(chunk, model), fixed(weights.shape), per_block(chunk, slots), per_block(slots, chunk),
        ],
        out_specs=[per_block(chunk, slim), per_block(chunk, LANES), per_block(slots, chunk)],
        out_shape=[
            like((blocks, chunk, slim), bf16),
            like((blocks, chunk, LANES), f32),
            like((blocks, slots, chunk), f32),
        ],
        compiler_params=pltpu.CompilerParams(vmem_limit_bytes=32 * MIB),
        cost_estimate=cost(2 * count * model * wide * 2, 6 * MIB),
        name="queries",
    )(n1, weights, picks, picks_t)

    out_full = gather_axis(held_out, "dp", 0)
    out_full = gather_each_bit(out_full, "mp", len(bit_groups("dp"))).reshape(model, wide)
    ff = gather_axis(jnp.concatenate([held_up, held_down], axis=1), "dp", 0)
    ff = gather_each_bit(ff.reshape(model, 2 * width), "mp", 0).reshape(peers, model, 2 * width)
    grads = joined(out_grad, swap(out_grad[:, chunk:, :]))

    attention = dict(slots=slots, hs=hs, rows=rows, peers=peers)
    total = peers * blocks
    gc, lse = pl.pallas_call(
        functools.partial(attend_kernel, **attention),
        grid_spec=pltpu.PrefetchScalarGridSpec(
            num_scalar_prefetch=1,
            grid=(blocks,),
            in_specs=[
                per_block(chunk, slim), fixed(kv_all.shape), per_block(1, chunk), per_block(slots, chunk),
            ],
            out_specs=[per_block(chunk, slim), per_block(slots, chunk)],
            scratch_shapes=[
                pltpu.VMEM((total, 2 * hs, chunk), bf16),
                pltpu.VMEM((slim, chunk), bf16),
                pltpu.VMEM((slim, chunk), f32),
                pltpu.VMEM((slots, chunk), f32),
                pltpu.VMEM((slots, chunk), f32),
                pltpu.VMEM((chunk, chunk), f32),
            ],
        ),
        out_shape=[like((blocks, chunk, slim), bf16), like((blocks, slots, chunk), f32)],
        compiler_params=pltpu.CompilerParams(vmem_limit_bytes=40 * MIB),
        cost_estimate=cost(12e9, 4 * MIB),
        name="attend",
    )(plan, q, kv_all, start, gate_t)

    outs, gm, gbr, gated, n2, hid, gbef, gatt, delta, glog, sums = pl.pallas_call(
        functools.partial(middle_kernel, heads=heads, slots=slots, hs=hs, width=width),
        grid=(blocks,),
        in_specs=[
            per_block(chunk, slim), per_block(chunk, LANES), per_block(chunk, slots),
            per_block(chunk, model), per_block(chunk, model),
            fixed(out_full.shape), fixed(ff.shape), fixed(norms.shape),
        ],
        out_specs=[
            per_block(chunk, model), per_block(chunk, model), per_block(chunk, model),
            per_block(chunk, wide), per_block(chunk, model),
            per_block(chunk, peers * width), per_block(chunk, peers * width),
            per_block(chunk, slim), per_block(slots, chunk), per_block(chunk, LANES), fixed((8, model)),
        ],
        out_shape=[
            like((blocks, chunk, model), bf16),
            like((blocks, chunk, model), f32),
            like((blocks, chunk, model), bf16),
            like((blocks, chunk, wide), bf16),
            like((blocks, chunk, model), bf16),
            like((blocks, chunk, peers * width), bf16),
            like((blocks, chunk, peers * width), bf16),
            like((blocks, chunk, slim), bf16),
            like((blocks, slots, chunk), f32),
            like((blocks, chunk, LANES), bf16),
            like((8, model), f32),
        ],
        compiler_params=pltpu.CompilerParams(vmem_limit_bytes=56 * MIB),
        cost_estimate=cost(18e9, 24 * MIB),
        name="middle",
    )(gc, gate, picks, x, grads, out_full, ff, norms)

    def flat(a):
        return a.reshape(count, -1)

    def column(w):
        return pl.BlockSpec((count, w), lambda m: (0, m))

    part = wide // peers
    ff_sum, out_sum = pl.pallas_call(
        functools.partial(weights_kernel, width=width),
        grid=(peers,),
        in_specs=[fixed((count, model))] * 3 + [column(width), column(width), column(part)],
        out_specs=[per_block(model, 2 * width), pl.BlockSpec((model, part), lambda m: (0, m))],
        out_shape=[like((peers, model, 2 * width), bf16), like((model, wide), bf16)],
        scratch_shapes=[pltpu.VMEM((model, count), bf16)] * 3,
        compiler_params=pltpu.CompilerParams(vmem_limit_bytes=48 * MIB),
        cost_estimate=cost(6e9, 20 * MIB),
        name="weight_grads",
    )(flat(n2), flat(grads), flat(gbr), flat(gbef), flat(hid), flat(gated))

    mp_bits, mp_dims = split_dims("mp", True)
    dp_bits, dp_dims = split_dims("dp", False)

    def scatter_all(a, lead):
        for group in mp_bits:
            dim = (0 if lead else len(dp_dims)) + len(mp_dims) - 1 - mp_bits.index(group)
            a = scatter_bits(a, "mp", group, dim).astype(bf16)
        for i, group in enumerate(dp_bits):
            a = scatter_bits(a, "dp", group, len(dp_dims) - 1 - i)
            if i < len(dp_bits) - 1:
                a = a.astype(bf16)
        return a

    per = w_query.shape[0]
    ff_grad = scatter_all(ff_sum.reshape(*mp_dims, *dp_dims, w_up.shape[0], 2 * width), True)
    out_grads = scatter_all(out_sum.reshape(*dp_dims, *mp_dims, per, wide), False)

    def unswapped(a):
        a = a.reshape(rows, 2, chunk, model)
        return jnp.concatenate([a[:, 0], swap(a[:, 1].astype(bf16)).astype(a.dtype)], axis=1)

    outputs = unswapped(outs)

    dq, dkv = pl.pallas_call(
        functools.partial(attend_back_kernel, **attention),
        grid_spec=pltpu.PrefetchScalarGridSpec(
            num_scalar_prefetch=1,
            grid=(blocks,),
            in_specs=[
                per_block(chunk, slim), per_block(chunk, slim), fixed(kv_all.shape), per_block(1, chunk),
                per_block(slots, chunk), per_block(slots, chunk),
            ],
            out_specs=[per_block(chunk, slim), fixed(kv_all.shape)],
            scratch_shapes=[
                pltpu.VMEM((total, 2 * hs, chunk), bf16),
                pltpu.VMEM((total, chunk, hs), bf16),
                pltpu.VMEM((slim, chunk), bf16),
                pltpu.VMEM((slim, chunk), bf16),
                pltpu.VMEM((slim, chunk), f32),
                pltpu.VMEM((total, chunk, hs), f32),
                pltpu.VMEM((total, chunk, hs), f32),
                pltpu.VMEM((chunk, chunk), f32),
            ],
        ),
        out_shape=[like((blocks, chunk, slim), bf16), like(kv_all.shape, bf16)],
        compiler_params=pltpu.CompilerParams(vmem_limit_bytes=48 * MIB),
        cost_estimate=cost(25e9, 6 * MIB),
        name="attend_back",
    )(plan, q, gatt, kv_all, start, lse, delta)

    dkv = dkv.reshape(*mp_dims, blocks * chunk, 2 * hs)
    for group in mp_bits:
        dkv = scatter_bits(dkv, "mp", group, len(mp_dims) - 1 - mp_bits.index(group)).astype(bf16)
    dkv = dkv.reshape(blocks, chunk, 2 * hs)

    wq_sum, wr_sum, dn = pl.pallas_call(
        functools.partial(query_back_kernel, at_misc=at_misc, heads=heads, slots=slots, hs=hs),
        grid=(blocks,),
        in_specs=[
            per_block(chunk, slim), per_block(chunk, slots), per_block(chunk, model),
            fixed(weights.shape), per_block(chunk, LANES),
        ],
        out_specs=[fixed((model, wide)), fixed((model, LANES)), per_block(chunk, model)],
        out_shape=[
            like((model, wide), bf16),
            like((model, LANES), f32),
            like((blocks, chunk, model), f32),
        ],
        scratch_shapes=[pltpu.VMEM((model, wide), f32), pltpu.VMEM((model, LANES), f32)],
        compiler_params=pltpu.CompilerParams(vmem_limit_bytes=40 * MIB),
        cost_estimate=cost(4e9, 10 * MIB),
        name="queries_back",
    )(dq, picks, n1, weights, glog)
    query_grad = scatter_all(wq_sum.reshape(*dp_dims, *mp_dims, per, wide), False)

    ig, small = pl.pallas_call(
        functools.partial(input_kernel, at_kv=at_kv, heads=heads),
        grid=(blocks,),
        in_specs=[
            per_block(chunk, model), per_block(chunk, 2 * hs), fixed(weights.shape),
            per_block(chunk, model), per_block(chunk, model), per_block(chunk, model),
            fixed((8, model)), fixed((model, LANES)), fixed((8, model)),
        ],
        out_specs=[per_block(chunk, model), fixed((model, 2 * LANES))],
        out_shape=[like((blocks, chunk, model), f32), like((model, 2 * LANES), bf16)],
        scratch_shapes=[pltpu.VMEM((model, 2 * hs), f32), pltpu.VMEM((8, model), f32)],
        compiler_params=pltpu.CompilerParams(vmem_limit_bytes=32 * MIB),
        cost_estimate=cost(1e9, 10 * MIB),
        name="inputs_back",
    )(dn, dkv, weights, x, n1, gm, norms, wr_sum, sums)

    tiles = small.reshape(model // per, per, 2 * LANES)
    tiles = lax.all_to_all(tiles, ("dp", "mp"), split_axis=0, concat_axis=0, tiled=True)
    smalls = jnp.sum(tiles.astype(f32), axis=0)
    return (
        outputs,
        unswapped(ig),
        counts,
        query_grad,
        smalls[:, : 2 * hs],
        out_grads,
        smalls[:, LANES : LANES + heads],
        smalls[:, LANES + heads : LANES + heads + 2],
        smalls[:, LANES + heads + 2 : LANES + heads + 4],
        ff_grad[:, :width],
        ff_grad[:, width:],
    )


def solution(mesh):
    in_specs = (
        P("dp", "mp", None),
        P("dp", None),
        P("dp", "mp", None),
        P("dp", "mp", None),
        P(("dp", "mp"), None),
        P(("dp", "mp"), None),
        P(("dp", "mp"), None),
        P(("dp", "mp"), None),
        P(("dp", "mp"), None),
        P(("dp", "mp"), None),
        P("dp", "mp"),
        P("dp", "mp"),
    )
    out_specs = (
        P("dp", "mp", None),
        P("dp", "mp", None),
        P(),
        P(("dp", "mp"), None),
        P(("dp", "mp"), None),
        P(("dp", "mp"), None),
        P(("dp", "mp"), None),
        P(("dp", "mp"), None),
        P(("dp", "mp"), None),
        P("dp", "mp"),
        P("dp", "mp"),
    )
    return jax.shard_map(shards, mesh=mesh, in_specs=in_specs, out_specs=out_specs, check_vma=False)
```

time: 2050 us -> 374 us (0.18)
  waiting for transfers between devices: 722 us -> 85.5 us
  matrix products: 478 us -> 0 us
  other arithmetic: 316 us -> 28.4 us
  local copies, waits for them, and re-layouts: 241 us -> 31.6 us
  blocking collectives: 264 us -> 57 us
  Pallas kernels: 0 us -> 102 us
  starting transfers between devices: 6.77 us -> 63.8 us
    reduce_scatter x7 -> x0, waiting for transfers between devices: 542 us -> none  [the longest x1 132 us: shards(): lax.psum_scatter(contract_rows(input_one, grad_keyvals), ('dp', 'mp'), sc...]
    dot_general x102 -> x0, matrix products: 478 us -> none  [the longest x12 148 us: backward_step(): jnp.einsum('rqhd,rkd->rhqk', grad_block, kv_block[:, :, headsize:], prefe...]
    all_gather x6 -> x0, blocking collectives: 218 us -> none  [the longest x1 43 us: shards(): lax.all_gather(norm_biases.astype(jnp.bfloat16), ('dp', 'mp'), axis=0, ti...]
    unnamed x16 -> x0, waiting for transfers between devices: 180 us -> none
    convert_element_type x17 -> x15, other arithmetic: 165 us -> 8.78 us  [the longest x6 5.64 us: scatter_all(): a = scatter_bits(a, 'mp', group, dim).astype(bf16)]
    pallas_call x0 -> x8, Pallas kernels: none -> 102 us  [the longest x1 33.1 us: shards(): pl.pallas_call(functools.partial(middle_kernel, heads=heads, slots=slots,...]
    while x27 -> x0, local copies, waits for them, and re-layouts: 89.1 us -> none
    ppermute x0 -> x44, waiting for transfers between devices: none -> 78.1 us  [flip(): lax.ppermute(x, axis, [(i, i ^ mask) for i in range(lax.axis_size(axis))])]
  transfers between devices with their start and end apart: 15 -> 45, of which waited for: 8 -> 16; matrix products, arithmetic and copies ran while one was open for 19% -> 12% of each run, Pallas kernels for 0% -> 13%
where the time goes in v1:
time: 374 us; the launch traced here: 370 us
  Pallas kernels  102 us (27%)
  waiting for transfers between devices  85.5 us (23%)
  starting transfers between devices  63.8 us (17%)
  blocking collectives  57 us (15%)
  local copies, waits for them, and re-layouts  31.6 us (8%)
  other arithmetic  28.4 us (8%)
    ppermute x44, waiting for transfers between devices, flip(): lax.ppermute(x, axis, [(i, i ^ mask) for i in range(lax.axis_size(axis))])  78.1 us
    ppermute x44, starting transfers between devices, flip(): lax.ppermute(x, axis, [(i, i ^ mask) for i in range(lax.axis_size(axis))])  58.7 us
    psum x1, blocking collectives, shards(): counts = lax.psum(jnp.sum(chosen, axis=(0, 1, 2)), ('dp', 'mp'))  57 us
    pallas_call x1, Pallas kernels, shards(): pl.pallas_call(functools.partial(middle_kernel, heads=heads, slots=slots,...  33.1 us
    pallas_call x1, Pallas kernels, shards(): pl.pallas_call(functools.partial(attend_back_kernel, **attention), grid_s...  21.3 us
    pallas_call x1, Pallas kernels, shards(): pl.pallas_call(functools.partial(attend_kernel, **attention), grid_spec=p...  12 us
    another operation x28, other arithmetic, gather_bits(): return jnp.stack(pieces, axis=dim)  11.8 us
    pallas_call x1, Pallas kernels, shards(): pl.pallas_call(functools.partial(weights_kernel, width=width), grid=(peer...  10.7 us
  transfers between devices with their start and end apart: 45, of which 16 were waited for; matrix products, arithmetic and copies ran while one was open for 12% of the time, Pallas kernels for 13%

profile of v1, /device:TPU:0, one launch (start us, length us, event | category | flops | bytes accessed | tf_op | source)
XLA Modules:
  0.0 370.0 jit_solution(11742711750901988325)
XLA Ops:
  3.4 5.0 %collective-permute-start.1 = (bf16[16,1792]{1,0:T(8,128)(2,1)S(1)}, bf16[16,1792]{1,0:T(8,128)(2,1)S(1)}, u32[]{:S(2)}, u32[]{:S(2)}) collective-permute-start(bf16[16,1792]{1,0:T(8,128)(2,1)S(1)} %concatenate.16), channel_id=1, source_target_pairs={{0,24},{4,28},{8,16},{12,20},{16,8},{20,12},{24,0},{28,4},{1,25},{... | collective-permute-start | bytes 172040 | tf_op jit(solution)/shard_map/ppermute | solution.py:40
  15.0 57.0 %psum.7 = f32[24]{0:T(128)} all-reduce(f32[24]{0:T(128)S(1)} %convert_reduce_fusion), channel_id=1, replica_groups=mesh['dp'=8,'mp'=4] {'dp','mp'}, use_global_device_ids=true, to_apply=%region_3.4 | all-reduce | flops 24 | bytes 192 | tf_op jit(solution)/shard_map/psum | solution.py:520
  74.8 4.1 %collective-permute-done.4 = bf16[4,16,1792]{2,1,0:T(8,128)(2,1)S(1)} collective-permute-done((bf16[4,16,1792]{2,1,0:T(8,128)(2,1)S(1)}, bf16[4,16,1792]{2,1,0:T(8,128)(2,1)S(1)}, u32[]{:S(2)}, u32[]{:S(2)}) %collective-permute-start.4) | collective-permute-done | bytes 229408 | tf_op jit(solution)/shard_map/ppermute | solution.py:40
  80.7 2.8 collective-permute-start.12
  87.5 3.0 collective-permute-start.18
  93.6 2.8 collective-permute-done.17
  101.6 2.7 collective-permute-done.13
  109.2 4.0 %collective-permute-done.14 = bf16[4,2,16,1536]{3,2,0,1:T(8,128)(2,1)} collective-permute-done((bf16[4,2,16,1536]{3,2,0,1:T(8,128)(2,1)}, bf16[4,2,16,1536]{3,2,0,1:T(8,128)(2,1)}, u32[]{:S(2)}, u32[]{:S(2)}) %collective-permute-start.14) | collective-permute-done | bytes 393248 | tf_op jit(solution)/shard_map/ppermute | solution.py:40
  121.1 4.8 %norm_one.1 = (bf16[4,256,512]{2,1,0:T(8,128)(2,1)}, bf16[4,256,128]{2,1,0:T(8,128)(2,1)}, f32[8,512]{1,0:T(8,128)}) custom-call(bf16[4,256,512]{2,1,0:T(8,128)(2,1)} %bitcast.215, bf16[512,1792]{1,0:T(8,128)(2,1)} %bitcast.211), custom_call_target="tpu_custom_call" | custom-call | flops 134217728 | bytes 4194304 | tf_op jit(solution)/shard_map/norm_one/pallas_call | solution.py:536
  128.0 7.0 %queries.1 = (bf16[4,256,512]{2,1,0:T(8,128)(2,1)S(1)}, f32[4,256,128]{2,1,0:T(8,128)S(1)}, f32[4,8,256]{2,1,0:T(8,128)S(1)}) custom-call(bf16[4,256,512]{2,1,0:T(8,128)(2,1)S(1)} %copy-done.6, bf16[512,1792]{1,0:T(8,128)(2,1)S(1)} %bitcast.212, s32[4,256,8]{2,1,0:T(8,128)S(1)} %bitcast.219, s32[4,8,256]{2,1,0:T(8,128)S(1)} %copy.119.routes_t_ref), custom_call_target="tpu_custom_call" | custom-call | flops 3221225472 | bytes 6291456 | tf_op jit(solution)/shard_map/queries/pallas_call | solution.py:551
  135.0 14.6 %collective-permute-done.7 = bf16[4,256,128]{2,1,0:T(8,128)(2,1)S(1)} collective-permute-done((bf16[4,256,128]{2,1,0:T(8,128)(2,1)}, bf16[4,256,128]{2,1,0:T(8,128)(2,1)S(1)}, u32[]{:S(2)}, u32[]{:S(2)}) %collective-permute-start.7) | collective-permute-done | bytes 262176 | tf_op jit(solution)/shard_map/ppermute | solution.py:40
  155.6 12.0 %attend.1 = (bf16[4,256,512]{2,1,0:T(8,128)(2,1)S(1)}, f32[4,8,256]{2,1,0:T(8,128)S(1)}) custom-call(s32[16]{0:T(128)S(1)} %reshape.149.plan, bf16[4,256,512]{2,1,0:T(8,128)(2,1)S(1)} %get-tuple-element.45.q_ref, bf16[16,256,128]{2,1,0:T(8,128)(2,1)S(1)} %bitcast.228, s32[4,1,256]{2,1,0:T(1,128)S(1)} %reshape.156.start_ref, ...), custom_call_target="tpu_custom_call" | custom-call | flops 12000000000 | bytes 4194304 | tf_op jit(solution)/shard_map/attend/pallas_call | solution.py:576
  169.0 2.5 copy.124
  171.5 33.1 %middle.1 = (bf16[4,256,512]{2,1,0:T(8,128)(2,1)}, f32[4,256,512]{2,1,0:T(8,128)}, bf16[4,256,512]{2,1,0:T(8,128)(2,1)}, bf16[4,256,1536]{2,1,0:T(8,128)(2,1)}, ...) custom-call(bf16[4,256,512]{2,1,0:T(8,128)(2,1)} %copy-done.15, ...), custom_call_target="tpu_custom_call" | custom-call | flops 17999998976 | bytes 25165824 | tf_op jit(solution)/shard_map/middle/pallas_call | solution.py:600
  206.6 21.3 %attend_back.1 = (bf16[4,256,512]{2,1,0:T(8,128)(2,1)S(1)}, bf16[16,256,128]{2,1,0:T(8,128)(2,1)S(1)}) custom-call(s32[16]{0:T(128)S(1)} %reshape.149.plan, bf16[4,256,512]{2,1,0:T(8,128)(2,1)S(1)} %get-tuple-element.45.q_ref, bf16[4,256,512]{2,1,0:T(8,128)(2,1)S(1)} %copy-done.16, bf16[16,256,128]{2,1,0:T(8,128)(2,1)S(1)} %bitcast.229, ...), custom_call_target="tpu_custom_call" | custom-call | flops 24999999488 | bytes 6291456 | tf_op jit(solution)/shard_map/attend_back/pallas_call | solution.py:674
  228.0 5.4 %collective-permute-start.23 = (bf16[2,1024,128]{2,1,0:T(8,128)(2,1)S(1)}, bf16[2,1024,128]{2,1,0:T(8,128)(2,1)S(1)}, u32[]{:S(2)}, u32[]{:S(2)}) collective-permute-start(bf16[2,1024,128]{2,1,0:T(8,128)(2,1)S(1)} %dynamic-slice_bitcast_fusion.2), channel_id=1, source_target_pairs={{0,1},{1,0},{2,3},{3,2},{4,5},{5,4},{6,7},{7,6},{8,9},{9,8},{10,11... | collective-permute-start | bytes 1572872 | tf_op jit(solution)/shard_map/ppermute | solution.py:40
  233.5 9.5 %queries_back.1 = (bf16[512,1536]{1,0:T(8,128)(2,1)S(1)}, f32[512,128]{1,0:T(8,128)S(1)}, f32[4,256,512]{2,1,0:T(8,128)S(1)}) custom-call(bf16[4,256,512]{2,1,0:T(8,128)(2,1)S(1)} %get-tuple-element.58.dq_ref, s32[4,256,8]{2,1,0:T(8,128)S(1)} %bitcast.221, bf16[4,256,512]{2,1,0:T(8,128)(2,1)S(1)} %copy-done.7, bf16[512,1792]{1,0:T(8,128)(2,1)S(1)} %bitcast.213, ...), custom_call_target="tpu_custom_call" | custom-call | flops 4000000000 | bytes 10485760 | tf_op jit(solution)/shard_map/queries_back/pallas_call | solution.py:706
  243.0 10.7 %weight_grads.1 = (bf16[4,512,1024]{2,1,0:T(8,128)(2,1)}, bf16[512,1536]{1,0:T(8,128)(2,1)S(1)}) custom-call(bf16[1024,512]{1,0:T(8,128)(2,1)S(1)} %bitcast.234, bf16[1024,512]{1,0:T(8,128)(2,1)S(1)} %bitcast.227, bf16[1024,512]{1,0:T(8,128)(2,1)S(1)} %bitcast.233, bf16[1024,2048]{1,0:T(8,128)(2,1)} %bitcast.245, bf16[1024,2048]{1,0:T(8,128)(2,1)} %bitcast.244, ...), custom_call_target="tpu_custom_call" | custom-call | flops 6000000000 | bytes 20971520 | tf_op jit(solution)/shard_map/weight_grads/pallas_call | solution.py:639
  261.4 8.1 %collective-permute-done.22 = bf16[2,256,512]{2,1,0:T(8,128)(2,1)S(1)} collective-permute-done((bf16[2,256,512]{2,1,0:T(8,128)(2,1)S(1)}, bf16[2,256,512]{2,1,0:T(8,128)(2,1)S(1)}, u32[]{:S(2)}, u32[]{:S(2)}) %collective-permute-start.22) | collective-permute-done | bytes 524320 | tf_op jit(solution)/shard_map/ppermute | solution.py:40
  275.7 3.7 %inputs_back.1 = (f32[4,256,512]{2,1,0:T(8,128)S(1)}, bf16[512,256]{1,0:T(8,128)(2,1)}) custom-call(f32[4,256,512]{2,1,0:T(8,128)S(1)} %get-tuple-element.60.dn_ref, bf16[4,256,128]{2,1,0:T(8,128)(2,1)S(1)} %bitcast.230, bf16[512,1792]{1,0:T(8,128)(2,1)S(1)} %bitcast.214, bf16[4,256,512]{2,1,0:T(8,128)(2,1)S(1)} %bitcast.217, ...), custom_call_target="tpu_custom_call" | custom-call | flops 1000000000 | bytes 10485760 | tf_op jit(solution)/shard_map/inputs_back/pallas_call | solution.py:726
  281.6 5.1 %all-to-all-start = ((bf16[32,16,256]{2,1,0:T(8,128)(2,1)}), bf16[32,16,256]{2,1,0:T(8,128)(2,1)}, u32[]{:S(2)}, u32[]{:S(2)}) async-start(bf16[32,16,256]{2,1,0:T(8,128)(2,1)} %bitcast.75), calls=%async_computation | async-start | bytes 524288 | tf_op jit(solution)/shard_map/all_to_all | solution.py:743
  291.4 2.8 collective-permute-done.27
  295.3 3.6 collective-permute-start.28
  298.9 7.4 %all-to-all-done = bf16[32,16,256]{2,1,0:T(8,128)(2,1)} async-done(((bf16[32,16,256]{2,1,0:T(8,128)(2,1)}), bf16[32,16,256]{2,1,0:T(8,128)(2,1)}, u32[]{:S(2)}, u32[]{:S(2)}) %all-to-all-start) | async-done | bytes 262176 | tf_op jit(solution)/shard_map/all_to_all | solution.py:743
  313.3 2.5 fusion
  317.2 4.0 %collective-permute-start.37 = (bf16[16,1536]{1,0:T(8,128)(2,1)S(1)}, bf16[16,1536]{1,0:T(8,128)(2,1)S(1)}, u32[]{:S(2)}, u32[]{:S(2)}) collective-permute-start(bf16[16,1536]{1,0:T(8,128)(2,1)S(1)} %get-tuple-element.167), channel_id=1, source_target_pairs={{0,24},{4,28},{8,16},{12,20},{16,8},{20,12},{24,0},{28,4},{1,25},{... | collective-permute-start | bytes 147464 | tf_op jit(solution)/shard_map/ppermute | solution.py:40
  321.3 19.9 %collective-permute-done.39 = bf16[4,2,64,1024]{3,2,0,1:T(8,128)(2,1)S(1)} collective-permute-done((bf16[4,2,64,1024]{3,2,0,1:T(8,128)(2,1)S(1)}, bf16[4,2,64,1024]{3,2,0,1:T(8,128)(2,1)S(1)}, u32[]{:S(2)}, u32[]{:S(2)}) %collective-permute-start.39) | collective-permute-done | bytes 1048608 | tf_op jit(solution)/shard_map/ppermute | solution.py:40
  341.7 3.3 collective-permute-start.40
  345.2 4.2 %collective-permute-start.31 = (bf16[16,1536]{1,0:T(8,128)(2,1)S(1)}, bf16[16,1536]{1,0:T(8,128)(2,1)S(1)}, u32[]{:S(2)}, u32[]{:S(2)}) collective-permute-start(bf16[16,1536]{1,0:T(8,128)(2,1)S(1)} %get-tuple-element.170), channel_id=1, source_target_pairs={{0,24},{4,28},{8,16},{12,20},{16,8},{20,12},{24,0},{28,4},{1,25},{... | collective-permute-start | bytes 147464 | tf_op jit(solution)/shard_map/ppermute | solution.py:40
  350.1 6.5 %collective-permute-done.40 = bf16[4,64,1024]{2,1,0:T(8,128)(2,1)S(1)} collective-permute-done((bf16[4,64,1024]{2,1,0:T(8,128)(2,1)S(1)}, bf16[4,64,1024]{2,1,0:T(8,128)(2,1)S(1)}, u32[]{:S(2)}, u32[]{:S(2)}) %collective-permute-start.40) | collective-permute-done | bytes 524320 | tf_op jit(solution)/shard_map/ppermute | solution.py:40
  357.0 4.3 %collective-permute-start.43 = (bf16[64,1024]{1,0:T(8,128)(2,1)S(1)}, bf16[64,1024]{1,0:T(8,128)(2,1)S(1)}, u32[]{:S(2)}, u32[]{:S(2)}) collective-permute-start(bf16[64,1024]{1,0:T(8,128)(2,1)S(1)} %get-tuple-element.148), channel_id=1, source_target_pairs={{0,24},{4,28},{8,16},{12,20},{16,8},{20,12},{24,0},{28,4},{1,25},{... | collective-permute-start | bytes 393224 | tf_op jit(solution)/shard_map/ppermute | solution.py:40
  363.7 5.5 %collective-permute-done.42 = bf16[64,1024]{1,0:T(8,128)(2,1)S(1)} collective-permute-done((bf16[64,1024]{1,0:T(8,128)(2,1)S(1)}, bf16[64,1024]{1,0:T(8,128)(2,1)S(1)}, u32[]{:S(2)}, u32[]{:S(2)}) %collective-permute-start.42) | collective-permute-done | bytes 131104 | tf_op jit(solution)/shard_map/ppermute | solution.py:40
  (247 shorter events, 85.1 us)
Async XLA Ops:
  3.4 68.6 %collective-permute-start.1 = (bf16[16,1792]{1,0:T(8,128)(2,1)S(1)}, bf16[16,1792]{1,0:T(8,128)(2,1)S(1)}, u32[]{:S(2)}, u32[]{:S(2)}) collective-permute-start(bf16[16,1792]{1,0:T(8,128)(2,1)S(1)} %concatenate.16), channel_id=1, source_target_pairs={{0,24},{4,28},{8,16},{12,20},{16,8},{20,12},{24,0},{28,4},{1,25},{... | collective-permute-start | bytes 172040 | tf_op jit(solution)/shard_map/ppermute | solution.py:40
  8.5 63.6 %collective-permute-start.2 = (bf16[16,1792]{1,0:T(8,128)(2,1)S(1)}, bf16[16,1792]{1,0:T(8,128)(2,1)S(1)}, u32[]{:S(2)}, u32[]{:S(2)}) collective-permute-start(bf16[16,1792]{1,0:T(8,128)(2,1)S(1)} %concatenate.16), channel_id=1, source_target_pairs={{0,16},{4,20},{8,24},{12,28},{16,0},{20,4},{24,8},{28,12},{1,17},{... | collective-permute-start | bytes 172040 | tf_op jit(solution)/shard_map/ppermute | solution.py:40
  8.5 63.6 %collective-permute-start.3 = (bf16[16,1792]{1,0:T(8,128)(2,1)S(1)}, bf16[16,1792]{1,0:T(8,128)(2,1)S(1)}, u32[]{:S(2)}, u32[]{:S(2)}) collective-permute-start(bf16[16,1792]{1,0:T(8,128)(2,1)S(1)} %concatenate.16), channel_id=1, source_target_pairs={{0,8},{4,12},{8,0},{12,4},{16,24},{20,28},{24,16},{28,20},{1,9},{5... | collective-permute-start | bytes 172040 | tf_op jit(solution)/shard_map/ppermute | solution.py:40
  11.6 94.6 %collective-permute-start = (bf16[520,512]{1,0:T(8,128)(2,1)}, bf16[520,512]{1,0:T(8,128)(2,1)S(1)}, u32[]{:S(2)}, u32[]{:S(2)}) collective-permute-start(bf16[520,512]{1,0:T(8,128)(2,1)} %pad_maximum_fusion.12), channel_id=1, source_target_pairs={{0,3},{1,2},{2,1},{3,0},{4,7},{5,6},{6,5},{7,4},{8,11},{9,10},{10,... | collective-permute-start | bytes 1597448 | tf_op jit(solution)/shard_map/ppermute | solution.py:40
  12.9 86.5 %collective-permute-start.9 = (bf16[2,256,512]{2,1,0:T(8,128)(2,1)}, bf16[2,256,512]{2,1,0:T(8,128)(2,1)}, u32[]{:S(2)}, u32[]{:S(2)}) collective-permute-start(bf16[2,256,512]{2,1,0:T(8,128)(2,1)} %get-tuple-element.138), channel_id=1, source_target_pairs={{0,3},{1,2},{2,1},{3,0},{4,7},{5,6},{6,5},{7,4},{8,11},{9,10},{10,... | collective-permute-start | bytes 1572872 | tf_op jit(solution)/shard_map/ppermute | solution.py:40
  92.6 15.3 %collective-permute-start.5 = (bf16[4,2,16,1792]{3,2,0,1:T(8,128)(2,1)S(1)}, bf16[4,2,16,1792]{3,2,0,1:T(8,128)(2,1)}, u32[]{:S(2)}, u32[]{:S(2)}) collective-permute-start(bf16[4,2,16,1792]{3,2,0,1:T(8,128)(2,1)S(1)} %pad_maximum_fusion.15), channel_id=1, source_target_pairs={{0,2},{1,3},{2,0},{3,1},{4,6},{5,7},{6,4},{7,5},{8,10},{9,11},{10,... | collective-permute-start | bytes 1376264 | tf_op jit(solution)/shard_map/ppermute | solution.py:40
  98.4 17.6 %collective-permute-start.19 = (bf16[4,64,1024]{2,1,0:T(8,128)(2,1)}, bf16[4,64,1024]{2,1,0:T(8,128)(2,1)}, u32[]{:S(2)}, u32[]{:S(2)}) collective-permute-start(bf16[4,64,1024]{2,1,0:T(8,128)(2,1)} %pad_maximum_fusion.14), channel_id=1, source_target_pairs={{0,4},{4,0},{8,12},{12,8},{16,20},{20,16},{24,28},{28,24},{1,5},{5... | collective-permute-start | bytes 1572872 | tf_op jit(solution)/shard_map/ppermute | solution.py:40
  116.0 36.3 %collective-permute-start.15 = (bf16[4,2,2,16,1536]{4,3,0,1,2:T(8,128)(2,1)}, bf16[4,2,2,16,1536]{4,3,0,1,2:T(8,128)(2,1)}, u32[]{:S(2)}, u32[]{:S(2)}) collective-permute-start(bf16[4,2,2,16,1536]{4,3,0,1,2:T(8,128)(2,1)} %pad_maximum_fusion.11), channel_id=1, source_target_pairs={{0,1},{1,0},{2,3},{3,2},{4,5},{5,4},{6,7},{7,6},{8,9},{9,8},{10,11... | collective-permute-start | bytes 2359304 | tf_op jit(solution)/shard_map/ppermute | solution.py:40
  118.2 31.6 %collective-permute-start.20 = (bf16[512,1024]{1,0:T(8,128)(2,1)}, bf16[512,1024]{1,0:T(8,128)(2,1)}, u32[]{:S(2)}, u32[]{:S(2)}) collective-permute-start(bf16[512,1024]{1,0:T(8,128)(2,1)} %bitcast.46), channel_id=1, source_target_pairs={{0,2},{1,3},{2,0},{3,1},{4,6},{5,7},{6,4},{7,5},{8,10},{9,11},{10,... | collective-permute-start | bytes 3145736 | tf_op jit(solution)/shard_map/ppermute | solution.py:40
  125.9 23.7 %collective-permute-start.7 = (bf16[4,256,128]{2,1,0:T(8,128)(2,1)}, bf16[4,256,128]{2,1,0:T(8,128)(2,1)S(1)}, u32[]{:S(2)}, u32[]{:S(2)}) collective-permute-start(bf16[4,256,128]{2,1,0:T(8,128)(2,1)} %get-tuple-element.46), channel_id=1, source_target_pairs={{0,2},{1,3},{2,0},{3,1},{4,6},{5,7},{6,4},{7,5},{8,10},{9,11},{10,... | collective-permute-start | bytes 786440 | tf_op jit(solution)/shard_map/ppermute | solution.py:40
  151.7 15.9 %collective-permute-start.21 = (bf16[2,512,1024]{2,1,0:T(8,128)(2,1)S(1)}, bf16[2,512,1024]{2,1,0:T(8,128)(2,1)S(1)}, u32[]{:S(2)}, u32[]{:S(2)}) collective-permute-start(bf16[2,512,1024]{2,1,0:T(8,128)(2,1)S(1)} %pad_maximum_fusion.1), channel_id=1, source_target_pairs={{0,1},{1,0},{2,3},{3,2},{4,5},{5,4},{6,7},{7,6},{8,9},{9,8},{10,11... | collective-permute-start | bytes 6291464 | tf_op jit(solution)/shard_map/ppermute | solution.py:40
  228.0 32.2 %collective-permute-start.23 = (bf16[2,1024,128]{2,1,0:T(8,128)(2,1)S(1)}, bf16[2,1024,128]{2,1,0:T(8,128)(2,1)S(1)}, u32[]{:S(2)}, u32[]{:S(2)}) collective-permute-start(bf16[2,1024,128]{2,1,0:T(8,128)(2,1)S(1)} %dynamic-slice_bitcast_fusion.2), channel_id=1, source_target_pairs={{0,1},{1,0},{2,3},{3,2},{4,5},{5,4},{6,7},{7,6},{8,9},{9,8},{10,11... | collective-permute-start | bytes 1572872 | tf_op jit(solution)/shard_map/ppermute | solution.py:40
  254.1 16.5 %collective-permute-start.32 = (bf16[4,2,2,16,1536]{4,3,0,1,2:T(8,128)(2,1)S(1)}, bf16[4,2,2,16,1536]{4,3,0,1,2:T(8,128)(2,1)S(1)}, u32[]{:S(2)}, u32[]{:S(2)}) collective-permute-start(bf16[4,2,2,16,1536]{4,3,0,1,2:T(8,128)(2,1)S(1)} %bitcast.242), channel_id=1, source_target_pairs={{0,1},{1,0},{2,3},{3,2},{4,5},{5,4},{6,7},{7,6},{8,9},{9,8},{10,11... | collective-permute-start | bytes 2359304 | tf_op jit(solution)/shard_map/ppermute | solution.py:40
  255.4 14.1 %collective-permute-start.22 = (bf16[2,256,512]{2,1,0:T(8,128)(2,1)S(1)}, bf16[2,256,512]{2,1,0:T(8,128)(2,1)S(1)}, u32[]{:S(2)}, u32[]{:S(2)}) collective-permute-start(bf16[2,256,512]{2,1,0:T(8,128)(2,1)S(1)} %get-tuple-element.134), channel_id=1, source_target_pairs={{0,3},{1,2},{2,1},{3,0},{4,7},{5,6},{6,5},{7,4},{8,11},{9,10},{10,... | collective-permute-start | bytes 1572872 | tf_op jit(solution)/shard_map/ppermute | solution.py:40
  259.6 52.9 %collective-permute-start.38 = (bf16[2,4,2,64,1024]{4,3,1,2,0:T(8,128)(2,1)}, bf16[2,4,2,64,1024]{4,3,1,2,0:T(8,128)(2,1)}, u32[]{:S(2)}, u32[]{:S(2)}) collective-permute-start(bf16[2,4,2,64,1024]{4,3,1,2,0:T(8,128)(2,1)} %bitcast.208), channel_id=1, source_target_pairs={{0,1},{1,0},{2,3},{3,2},{4,5},{5,4},{6,7},{7,6},{8,9},{9,8},{10,11... | collective-permute-start | bytes 6291464 | tf_op jit(solution)/shard_map/ppermute | solution.py:40
  259.7 12.3 %collective-permute-start.26 = (bf16[4,2,2,16,1536]{4,3,0,1,2:T(8,128)(2,1)S(1)}, bf16[4,2,2,16,1536]{4,3,0,1,2:T(8,128)(2,1)S(1)}, u32[]{:S(2)}, u32[]{:S(2)}) collective-permute-start(bf16[4,2,2,16,1536]{4,3,0,1,2:T(8,128)(2,1)S(1)} %bitcast.243), channel_id=1, source_target_pairs={{0,1},{1,0},{2,3},{3,2},{4,5},{5,4},{6,7},{7,6},{8,9},{9,8},{10,11... | collective-permute-start | bytes 2359304 | tf_op jit(solution)/shard_map/ppermute | solution.py:40
  260.4 15.1 %collective-permute-start.24 = (bf16[1024,128]{1,0:T(8,128)(2,1)S(1)}, bf16[1024,128]{1,0:T(8,128)(2,1)S(1)}, u32[]{:S(2)}, u32[]{:S(2)}) collective-permute-start(bf16[1024,128]{1,0:T(8,128)(2,1)S(1)} %dynamic-slice_bitcast_fusion.5), channel_id=1, source_target_pairs={{0,2},{1,3},{2,0},{3,1},{4,6},{5,7},{6,4},{7,5},{8,10},{9,11},{10,... | collective-permute-start | bytes 786440 | tf_op jit(solution)/shard_map/ppermute | solution.py:40
  271.6 16.5 %collective-permute-start.33 = (bf16[4,2,16,1536]{3,2,0,1:T(8,128)(2,1)}, bf16[4,2,16,1536]{3,2,0,1:T(8,128)(2,1)}, u32[]{:S(2)}, u32[]{:S(2)}) collective-permute-start(bf16[4,2,16,1536]{3,2,0,1:T(8,128)(2,1)} %dynamic-slice_bitcast_fusion.3), channel_id=1, source_target_pairs={{0,2},{1,3},{2,0},{3,1},{4,6},{5,7},{6,4},{7,5},{8,10},{9,11},{10,... | collective-permute-start | bytes 1179656 | tf_op jit(solution)/shard_map/ppermute | solution.py:40
  273.0 21.2 %collective-permute-start.27 = (bf16[4,2,16,1536]{3,2,0,1:T(8,128)(2,1)}, bf16[4,2,16,1536]{3,2,0,1:T(8,128)(2,1)}, u32[]{:S(2)}, u32[]{:S(2)}) collective-permute-start(bf16[4,2,16,1536]{3,2,0,1:T(8,128)(2,1)} %dynamic-slice_bitcast_fusion.4), channel_id=1, source_target_pairs={{0,2},{1,3},{2,0},{3,1},{4,6},{5,7},{6,4},{7,5},{8,10},{9,11},{10,... | collective-permute-start | bytes 1179656 | tf_op jit(solution)/shard_map/ppermute | solution.py:40
  281.6 28.2 %collective-permute-start.25 = (bf16[2,256,512]{2,1,0:T(8,128)(2,1)}, bf16[2,256,512]{2,1,0:T(8,128)(2,1)}, u32[]{:S(2)}, u32[]{:S(2)}) collective-permute-start(bf16[2,256,512]{2,1,0:T(8,128)(2,1)} %fusion.8), channel_id=1, source_target_pairs={{0,3},{1,2},{2,1},{3,0},{4,7},{5,6},{6,5},{7,4},{8,11},{9,10},{10,... | collective-permute-start | bytes 1572872 | tf_op jit(solution)/shard_map/ppermute | solution.py:40
  281.6 24.6 %all-to-all-start = ((bf16[32,16,256]{2,1,0:T(8,128)(2,1)}), bf16[32,16,256]{2,1,0:T(8,128)(2,1)}, u32[]{:S(2)}, u32[]{:S(2)}) async-start(bf16[32,16,256]{2,1,0:T(8,128)(2,1)} %bitcast.75), calls=%async_computation | async-start | bytes 524288 | tf_op jit(solution)/shard_map/all_to_all | solution.py:743
  289.2 27.5 %collective-permute-start.34 = (bf16[4,16,1536]{2,1,0:T(8,128)(2,1)S(1)}, bf16[4,16,1536]{2,1,0:T(8,128)(2,1)S(1)}, u32[]{:S(2)}, u32[]{:S(2)}) collective-permute-start(bf16[4,16,1536]{2,1,0:T(8,128)(2,1)S(1)} %dynamic-slice_bitcast_fusion.6), channel_id=1, source_target_pairs={{0,4},{4,0},{8,12},{12,8},{16,20},{20,16},{24,28},{28,24},{1,5},{5... | collective-permute-start | bytes 589832 | tf_op jit(solution)/shard_map/ppermute | solution.py:40
  295.3 25.9 %collective-permute-start.28 = (bf16[4,16,1536]{2,1,0:T(8,128)(2,1)S(1)}, bf16[4,16,1536]{2,1,0:T(8,128)(2,1)S(1)}, u32[]{:S(2)}, u32[]{:S(2)}) collective-permute-start(bf16[4,16,1536]{2,1,0:T(8,128)(2,1)S(1)} %dynamic-slice_bitcast_fusion.7), channel_id=1, source_target_pairs={{0,4},{4,0},{8,12},{12,8},{16,20},{20,16},{24,28},{28,24},{1,5},{5... | collective-permute-start | bytes 589832 | tf_op jit(solution)/shard_map/ppermute | solution.py:40
  316.0 25.2 %collective-permute-start.39 = (bf16[4,2,64,1024]{3,2,0,1:T(8,128)(2,1)S(1)}, bf16[4,2,64,1024]{3,2,0,1:T(8,128)(2,1)S(1)}, u32[]{:S(2)}, u32[]{:S(2)}) collective-permute-start(bf16[4,2,64,1024]{3,2,0,1:T(8,128)(2,1)S(1)} %dynamic-slice_bitcast_fusion), channel_id=1, source_target_pairs={{0,2},{1,3},{2,0},{3,1},{4,6},{5,7},{6,4},{7,5},{8,10},{9,11},{10,... | collective-permute-start | bytes 3145736 | tf_op jit(solution)/shard_map/ppermute | solution.py:40
  316.8 28.3 %collective-permute-start.35 = (bf16[16,1536]{1,0:T(8,128)(2,1)S(1)}, bf16[16,1536]{1,0:T(8,128)(2,1)S(1)}, u32[]{:S(2)}, u32[]{:S(2)}) collective-permute-start(bf16[16,1536]{1,0:T(8,128)(2,1)S(1)} %get-tuple-element.166), channel_id=1, source_target_pairs={{0,8},{4,12},{8,0},{12,4},{16,24},{20,28},{24,16},{28,20},{1,9},{5... | collective-permute-start | bytes 147464 | tf_op jit(solution)/shard_map/ppermute | solution.py:40
  317.2 27.9 %collective-permute-start.36 = (bf16[16,1536]{1,0:T(8,128)(2,1)S(1)}, bf16[16,1536]{1,0:T(8,128)(2,1)S(1)}, u32[]{:S(2)}, u32[]{:S(2)}) collective-permute-start(bf16[16,1536]{1,0:T(8,128)(2,1)S(1)} %get-tuple-element.168), channel_id=1, source_target_pairs={{0,16},{4,20},{8,24},{12,28},{16,0},{20,4},{24,8},{28,12},{1,17},{... | collective-permute-start | bytes 147464 | tf_op jit(solution)/shard_map/ppermute | solution.py:40
  317.2 32.2 %collective-permute-start.37 = (bf16[16,1536]{1,0:T(8,128)(2,1)S(1)}, bf16[16,1536]{1,0:T(8,128)(2,1)S(1)}, u32[]{:S(2)}, u32[]{:S(2)}) collective-permute-start(bf16[16,1536]{1,0:T(8,128)(2,1)S(1)} %get-tuple-element.167), channel_id=1, source_target_pairs={{0,24},{4,28},{8,16},{12,20},{16,8},{20,12},{24,0},{28,4},{1,25},{... | collective-permute-start | bytes 147464 | tf_op jit(solution)/shard_map/ppermute | solution.py:40
  341.7 14.9 %collective-permute-start.40 = (bf16[4,64,1024]{2,1,0:T(8,128)(2,1)S(1)}, bf16[4,64,1024]{2,1,0:T(8,128)(2,1)S(1)}, u32[]{:S(2)}, u32[]{:S(2)}) collective-permute-start(bf16[4,64,1024]{2,1,0:T(8,128)(2,1)S(1)} %dynamic-slice_bitcast_fusion.1), channel_id=1, source_target_pairs={{0,4},{4,0},{8,12},{12,8},{16,20},{20,16},{24,28},{28,24},{1,5},{5... | collective-permute-start | bytes 1572872 | tf_op jit(solution)/shard_map/ppermute | solution.py:40
  345.0 16.3 %collective-permute-start.30 = (bf16[16,1536]{1,0:T(8,128)(2,1)S(1)}, bf16[16,1536]{1,0:T(8,128)(2,1)S(1)}, u32[]{:S(2)}, u32[]{:S(2)}) collective-permute-start(bf16[16,1536]{1,0:T(8,128)(2,1)S(1)} %get-tuple-element.171), channel_id=1, source_target_pairs={{0,16},{4,20},{8,24},{12,28},{16,0},{20,4},{24,8},{28,12},{1,17},{... | collective-permute-start | bytes 147464 | tf_op jit(solution)/shard_map/ppermute | solution.py:40
  345.2 16.2 %collective-permute-start.31 = (bf16[16,1536]{1,0:T(8,128)(2,1)S(1)}, bf16[16,1536]{1,0:T(8,128)(2,1)S(1)}, u32[]{:S(2)}, u32[]{:S(2)}) collective-permute-start(bf16[16,1536]{1,0:T(8,128)(2,1)S(1)} %get-tuple-element.170), channel_id=1, source_target_pairs={{0,24},{4,28},{8,16},{12,20},{16,8},{20,12},{24,0},{28,4},{1,25},{... | collective-permute-start | bytes 147464 | tf_op jit(solution)/shard_map/ppermute | solution.py:40
  357.0 12.3 %collective-permute-start.42 = (bf16[64,1024]{1,0:T(8,128)(2,1)S(1)}, bf16[64,1024]{1,0:T(8,128)(2,1)S(1)}, u32[]{:S(2)}, u32[]{:S(2)}) collective-permute-start(bf16[64,1024]{1,0:T(8,128)(2,1)S(1)} %get-tuple-element.149), channel_id=1, source_target_pairs={{0,16},{4,20},{8,24},{12,28},{16,0},{20,4},{24,8},{28,12},{1,17},{... | collective-permute-start | bytes 393224 | tf_op jit(solution)/shard_map/ppermute | solution.py:40
  357.0 12.2 %collective-permute-start.43 = (bf16[64,1024]{1,0:T(8,128)(2,1)S(1)}, bf16[64,1024]{1,0:T(8,128)(2,1)S(1)}, u32[]{:S(2)}, u32[]{:S(2)}) collective-permute-start(bf16[64,1024]{1,0:T(8,128)(2,1)S(1)} %get-tuple-element.148), channel_id=1, source_target_pairs={{0,24},{4,28},{8,16},{12,20},{16,8},{20,12},{24,0},{28,4},{1,25},{... | collective-permute-start | bytes 393224 | tf_op jit(solution)/shard_map/ppermute | solution.py:40
  (45 other events, 540.5 us)

commit v2 on v1

v2 whole, which is shorter than its diff:
```python
import functools
import math
import jax
import jax.numpy as jnp
from jax import lax
from jax.experimental import pallas as pl
from jax.experimental.pallas import tpu as pltpu
from jax.sharding import PartitionSpec as P

epsilon = 1e-05
f32, bf16 = jnp.float32, jnp.bfloat16
NN = (((1,), (0,)), ((), ()))
NT = (((1,), (1,)), ((), ()))
LANES = 128
LOG2E = math.log2(math.e)
MIB = 2**20


def dot(left, right, dims=NN):
    return lax.dot_general(left, right, dims, preferred_element_type=f32)


def bits_of(axis):
    return (lax.axis_size(axis) - 1).bit_length()


def bit_groups(axis):
    count = bits_of(axis)
    groups, at = [], 0
    if count % 2:
        groups.append((0, 1))
        at = 1
    while at < count:
        groups.append((at, 2))
        at += 2
    return groups


def flip(x, axis, mask):
    return lax.ppermute(x, axis, [(i, i ^ mask) for i in range(lax.axis_size(axis))])


def after(x, *others):
    return lax.optimization_barrier((x, *others))[0]


def gather_bits(x, axis, group, dim, until=None):
    low, width = group
    mine = lax.axis_index(axis) >> low
    got = [flip(x, axis, k << low) for k in range(1, 2**width)]
    if until is not None:
        got = lax.optimization_barrier((*got, until))[:-1]
    shape = [1] * (x.ndim + 1)
    shape[dim] = 2**width
    way = lax.iota(jnp.int32, 2**width).reshape(shape) ^ (mine & (2**width - 1))
    pieces = [jnp.expand_dims(p, dim) for p in (x, *got)]
    for b in range(width):
        odd = (way >> b) & 1 == 1
        pieces = [jnp.where(odd, pieces[k + 1], pieces[k]) for k in range(0, len(pieces), 2)]
    return pieces[0]


def scatter_bits(x, axis, group, dim, until=None):
    low, width = group
    mine = (lax.axis_index(axis) >> low) & (2**width - 1)
    got = [
        flip(lax.dynamic_index_in_dim(x, mine ^ k, dim, keepdims=False), axis, k << low)
        for k in range(1, 2**width)
    ]
    if until is not None:
        got = lax.optimization_barrier((*got, until))[:-1]
    total = lax.dynamic_index_in_dim(x, mine, dim, keepdims=False).astype(f32)
    for g in got:
        total = total + g.astype(f32)
    return total


def halves(row_first, row_second, like):
    lane = lax.broadcasted_iota(jnp.int32, like, 1)
    return jnp.where(lane < LANES // 2, row_first, row_second)


def slot_experts(routes, pairs):
    shape = (routes.shape[0], LANES)
    return [halves(routes[:, 2 * j : 2 * j + 1], routes[:, 2 * j + 1 : 2 * j + 2], shape) for j in range(pairs)]


def turn_half(x):
    return pltpu.roll(x, LANES // 2, 1)


def compact(wide, experts, head_pairs):
    lane = lax.broadcasted_iota(jnp.int32, experts[0].shape, 1)
    high = (lane >= LANES // 2).astype(jnp.int32)
    straight = [e - high for e in experts]
    crossed = [e + high for e in experts]
    found = [jnp.zeros(experts[0].shape, f32) for _ in experts]
    for i in range(head_pairs):
        block = wide(i)
        turned = turn_half(block)
        for j in range(len(experts)):
            found[j] = jnp.where(straight[j] == 2 * i, block, found[j])
            found[j] = jnp.where(crossed[j] == 2 * i + 1, turned, found[j])
    return found


def expand(narrow, experts, head_pairs):
    lane = lax.broadcasted_iota(jnp.int32, experts[0].shape, 1)
    high = (lane >= LANES // 2).astype(jnp.int32)
    sources = []
    for block, e in zip(narrow, experts):
        sources.append((e - high, block))
        sources.append((turn_half(e) - high, turn_half(block)))
    wide = []
    for i in range(head_pairs):
        out = jnp.zeros(experts[0].shape, f32)
        for e, block in sources:
            out = jnp.where(e == 2 * i, block, out)
        wide.append(out.astype(bf16))
    return jnp.concatenate(wide, axis=1)


def split_core(value, core, per, send_ref, keep_ref):
    rows, columns = value.shape
    if per % 16 == 0:
        parts = value.reshape(rows // (2 * per), 2, per, columns)
        first, second = parts[:, 0], parts[:, 1]
        send = jnp.where(core == 0, second, first).reshape(rows // 2, columns)
        keep = jnp.where(core == 0, first, second).reshape(rows // 2, columns)
        send_ref[...], keep_ref[...] = send.astype(bf16), keep.astype(bf16)
        return
    shape = (rows // 2, rows)
    target, source = (lax.broadcasted_iota(jnp.int32, shape, i) for i in range(2))
    start = target // per * (2 * per) + target % per
    for ref, side in ((send_ref, 1 - core), (keep_ref, core)):
        chosen = (source == start + side * per).astype(bf16)
        ref[...] = dot(chosen, value.astype(bf16)).astype(bf16)


def normed_parts(values):
    mean = jnp.mean(values, axis=1, keepdims=True)
    centred = values - mean
    rstd = lax.rsqrt(jnp.mean(centred * centred, axis=1, keepdims=True) + epsilon)
    return centred * rstd, rstd


def norm_back(grad, normed, rstd, gain):
    scaled = grad * gain
    return rstd * (
        scaled
        - jnp.mean(scaled, axis=1, keepdims=True)
        - normed * jnp.mean(scaled * normed, axis=1, keepdims=True)
    )


def norm_kernel(x_ref, w_ref, n_ref, kv_ref, norms_ref, *, at_kv, at_misc, heads):
    misc = w_ref[:, at_misc : at_misc + LANES].astype(f32).T
    norms = misc[heads : heads + 8, :]
    norms = jnp.concatenate(
        [norms[0:2] + norms[2:4], norms[4:6] + norms[6:8], jnp.zeros_like(norms[0:4])], axis=0
    )
    norms_ref[...] = norms
    normed, _ = normed_parts(x_ref[0].astype(f32))
    low = (normed * norms[0:1] + norms[2:3]).astype(bf16)
    n_ref[0] = low
    kv_ref[0] = dot(low, w_ref[:, at_kv : at_kv + LANES]).astype(bf16)


def query_kernel(
    n_ref, w_ref, routes_ref, routes_t_ref, q_ref, gate_ref, gate_t_ref, *, at_misc, heads, slots, hs
):
    low = n_ref[0]
    head_pairs = heads // 2
    queries = dot(low, w_ref[:, : heads * hs]) * (hs**-0.5 * LOG2E)
    experts = slot_experts(routes_ref[0], slots // 2)
    found = compact(lambda i: queries[:, i * LANES : (i + 1) * LANES], experts, head_pairs)
    q_ref[0] = jnp.concatenate([f.astype(bf16) for f in found], axis=1)
    logits = dot(low, w_ref[:, at_misc : at_misc + LANES]).T[:heads, :]
    expert = lax.broadcasted_iota(jnp.int32, logits.shape, 0)
    routes_t = routes_t_ref[0]
    picked = [
        jnp.sum(jnp.where(expert == routes_t[s : s + 1, :], logits, 0.0), axis=0, keepdims=True)
        for s in range(slots)
    ]
    chosen = jnp.concatenate(picked, axis=0)
    lifted = jnp.exp(chosen - jnp.max(chosen, axis=0, keepdims=True))
    gate = lifted / jnp.sum(lifted, axis=0, keepdims=True)
    gate_t_ref[0] = gate
    padded = jnp.concatenate([gate, jnp.zeros((LANES - slots, gate.shape[1]), f32)], axis=0)
    gate_ref[0] = padded.T


def key_bias(first_key, first_query, start, keys, queries):
    key = first_key + lax.broadcasted_iota(jnp.int32, (keys, queries), 0)
    query = first_query + lax.broadcasted_iota(jnp.int32, (keys, queries), 1)
    return jnp.where((key <= query) & (key >= start), 0.0, -1e30)


def kv_place(row, chunk, single, rows, peers):
    half, owner = chunk % 2, chunk // 2
    owner = jnp.where((half == 1) & (row == single), peers - 1 - owner, owner)
    return owner * (2 * rows) + row * 2 + half


def over_keys(plan, start_ref, bias, block, keys, queries):
    b = pl.program_id(0)
    row, last, first, full = plan[4 * b], plan[4 * b + 1], plan[4 * b + 2], plan[4 * b + 3]

    def masked(i, carry):
        chunk = jnp.where(i == 0, last, first + i - 1)
        bias[...] = key_bias(chunk * keys, last * keys, start_ref[0], keys, queries)
        block(row, chunk, True)
        return carry

    def plain(chunk, carry):
        block(row, chunk, False)
        return carry

    lax.fori_loop(0, 1 + full - first, masked, 0)
    lax.fori_loop(full, last, plain, 0)


def attend_kernel(
    plan, q_ref, kv_ref, start_ref, gate_ref, out_ref, lse_ref, kvt, qt, acc, top, tot, bias, *, slots, hs, rows, peers
):
    queries, keys = q_ref.shape[1], kv_ref.shape[1]

    @pl.when(pl.program_id(0) == 0)
    def _():
        for i in range(kv_ref.shape[0]):
            kvt[i] = kv_ref[i].T

    qt[...] = q_ref[0].T
    acc[...] = jnp.zeros_like(acc)
    top[...] = jnp.full_like(top, -1e30)
    tot[...] = jnp.zeros_like(tot)
    part = [slice(h * hs, (h + 1) * hs) for h in range(slots)]

    def block(row, chunk, masked):
        at = kv_place(row, chunk, plan[8 * rows], rows, peers)
        k = kv_ref[at][:, :hs]
        vt = kvt[at, hs : 2 * hs, :]
        tops, tots = top[...], tot[...]
        scores = [dot(k, qt[part[h], :]) for h in range(slots)]
        if masked:
            scores = [s + bias[...] for s in scores]
        highest = [
            jnp.maximum(tops[h : h + 1], jnp.max(scores[h], axis=0, keepdims=True)) for h in range(slots)
        ]
        probs = [jnp.exp2(scores[h] - highest[h]) for h in range(slots)]
        shrink = [jnp.exp2(tops[h : h + 1] - highest[h]) for h in range(slots)]
        totals = [
            tots[h : h + 1] * shrink[h] + jnp.sum(probs[h], axis=0, keepdims=True) for h in range(slots)
        ]
        for h in range(slots):
            acc[part[h], :] = acc[part[h], :] * shrink[h] + dot(vt, probs[h].astype(bf16))
        top[...] = jnp.concatenate(highest, axis=0)
        tot[...] = jnp.concatenate(totals, axis=0)

    over_keys(plan, start_ref, bias, block, keys, queries)
    for h in range(slots):
        acc[part[h], :] = acc[part[h], :] * (gate_ref[0, h : h + 1, :] / tot[h : h + 1, :])
    lse_ref[0] = top[...] + jnp.log2(tot[...])
    out_ref[0] = acc[...].astype(bf16).T


def attend_back_kernel(
    plan, q_ref, g_ref, kv_ref, start_ref, lse_ref, delta_ref, dq_ref, send_ref, keep_ref,
    kvt, v_rows, qt, gt, dqt, dk, dv, bias, *, slots, hs, rows, peers,
):
    queries, keys = q_ref.shape[1], kv_ref.shape[1]
    b = pl.program_id(0)

    @pl.when(b == 0)
    def _():
        for i in range(kv_ref.shape[0]):
            kvt[i] = kv_ref[i].T
            v_rows[i] = kv_ref[i][:, hs:]
        dk[...] = jnp.zeros_like(dk)
        dv[...] = jnp.zeros_like(dv)

    qt[...] = q_ref[0].T
    gt[...] = g_ref[0].T
    dqt[...] = jnp.zeros_like(dqt)
    part = [slice(h * hs, (h + 1) * hs) for h in range(slots)]

    def block(row, chunk, masked):
        at = kv_place(row, chunk, plan[8 * rows], rows, peers)
        k = kv_ref[at][:, :hs]
        v = v_rows[at]
        kt = kvt[at, :hs, :]
        scores = [dot(k, qt[part[h], :]) for h in range(slots)]
        grads = [dot(v, gt[part[h], :]) for h in range(slots)]
        if masked:
            scores = [s + bias[...] for s in scores]
        probs = [jnp.exp2(scores[h] - lse_ref[0, h : h + 1, :]) for h in range(slots)]
        ds = [(probs[h] * (grads[h] - delta_ref[0, h : h + 1, :])).astype(bf16) for h in range(slots)]
        low = [p.astype(bf16) for p in probs]
        for h in range(slots):
            dqt[part[h], :] += dot(kt, ds[h])
        dk[at] += sum(dot(ds[h], qt[part[h], :], NT) for h in range(slots))
        dv[at] += sum(dot(low[h], gt[part[h], :], NT) for h in range(slots))

    over_keys(plan, start_ref, bias, block, keys, queries)
    dq_ref[0] = (dqt[...] * hs**-0.5).astype(bf16).T

    @pl.when(b == pl.num_programs(0) - 1)
    def _():
        core, each = plan[8 * rows + 1], kv_ref.shape[0] // peers
        for i in range(send_ref.shape[0]):
            at = i + each * (i // each)
            for ref, place in ((send_ref, at + each * (1 - core)), (keep_ref, at + each * core)):
                ref[i] = jnp.concatenate([dk[place] * (1.0 / LOG2E), dv[place]], axis=1).astype(bf16)


def forward_kernel(
    gc_ref, routes_ref, x_ref, og_ref, wo_ref, ff_ref, norms_ref,
    gated_ref, mid_ref, out_ref, back_ref, sum_ref, n2t, ogt, hid, gbef,
    *, heads, slots, width, blocks,
):
    step = pl.program_id(0)
    tokens, model = x_ref.shape[1], x_ref.shape[2]
    peers = ff_ref.shape[1]

    @pl.when(step < blocks)
    def _():
        pairs = slots // 2
        experts = slot_experts(routes_ref[0], pairs)
        gc = [gc_ref[0][:, j * LANES : (j + 1) * LANES].astype(f32) for j in range(pairs)]
        gated = expand(gc, experts, heads // 2)
        gated_ref[0] = gated
        middle = x_ref[0].astype(f32) + dot(gated, wo_ref[:, : gated.shape[1]], NT)
        mid_ref[0] = middle
        vhat, _ = normed_parts(middle)
        low = (vhat * norms_ref[1:2, :] + norms_ref[3:4, :]).astype(bf16)
        og = og_ref[0]
        n2t[step] = low.T
        ogt[step] = og.T
        out = middle
        back = jnp.zeros_like(out)
        slope = math.sqrt(2.0 / math.pi)
        for c in range(peers):
            up, down = (ff_ref[:, c, :, at : at + width].reshape(model, width) for at in (0, width))
            v = dot(low, up)
            square = v * v
            bent = jnp.tanh(slope * v * (1.0 + 0.044715 * square))
            rise = 0.5 * (1.0 + bent)
            hidden = (v * rise).astype(bf16)
            slant = rise + 0.5 * v * (1.0 - bent * bent) * (slope + 3.0 * slope * 0.044715 * square)
            before = (dot(og, down) * slant).astype(bf16)
            out = out + dot(hidden, down, NT)
            back = back + dot(before, up, NT)
            hid[c, step] = hidden
            gbef[c, step] = before
        out_ref[0] = out.astype(bf16)
        back_ref[0] = back

    @pl.when(step >= blocks)
    def _():
        c = step - blocks
        up = sum(dot(n2t[b], gbef[c, b]) for b in range(blocks))
        down = sum(dot(ogt[b], hid[c, b]) for b in range(blocks))
        shape = (sum_ref.shape[1], sum_ref.shape[2] // 2, sum_ref.shape[3])
        sum_ref[0] = jnp.concatenate([up.reshape(shape), down.reshape(shape)], axis=1).astype(bf16)


def branch_back_kernel(
    core, back_ref, mid_ref, og_ref, gc_ref, gate_ref, routes_ref, wo_ref, norms_ref, gated_ref,
    gm_ref, gatt_ref, delta_ref, glog_ref, sums_ref, send_ref, keep_ref, gbrt,
    *, heads, slots, hs, blocks, per,
):
    step = pl.program_id(0)

    @pl.when(step < blocks)
    def _():
        branch_back_block(
            step, back_ref, mid_ref, og_ref, gc_ref, gate_ref, routes_ref, wo_ref, norms_ref,
            gm_ref, gatt_ref, delta_ref, glog_ref, sums_ref, gbrt, heads, slots, hs,
        )

    @pl.when(step >= blocks)
    def _():
        total = sum(dot(gbrt[b], gated_ref[b]) for b in range(blocks))
        split_core(total, core[0], per, send_ref, keep_ref)


def branch_back_block(
    step, back_ref, mid_ref, og_ref, gc_ref, gate_ref, routes_ref, wo_ref, norms_ref,
    gm_ref, gatt_ref, delta_ref, glog_ref, sums_ref, gbrt, heads, slots, hs,
):
    tokens, model = mid_ref.shape[1], mid_ref.shape[2]
    head_pairs, pairs = heads // 2, slots // 2
    experts = slot_experts(routes_ref[0], pairs)
    back = back_ref[0]
    vhat, rstd = normed_parts(mid_ref[0])
    gm = og_ref[0].astype(f32) + norm_back(back, vhat, rstd, norms_ref[1:2, :])
    gm_ref[0] = gm

    @pl.when(step == 0)
    def _():
        sums_ref[...] = jnp.zeros_like(sums_ref)

    sums_ref[0:1, :] += jnp.sum(back * vhat, axis=0, keepdims=True)
    sums_ref[1:2, :] += jnp.sum(back, axis=0, keepdims=True)
    gbr = gm.astype(bf16)
    gbrt[step] = gbr.T
    wide = dot(gbr, wo_ref[:, : heads * hs])
    found = compact(lambda i: wide[:, i * LANES : (i + 1) * LANES], experts, head_pairs)
    gate = gate_ref[0]
    shape = (tokens, LANES)
    attended, products = [], []
    for j in range(pairs):
        spread = halves(gate[:, 2 * j : 2 * j + 1], gate[:, 2 * j + 1 : 2 * j + 2], shape)
        attended.append((found[j] * spread).astype(bf16))
        products.append(found[j] * gc_ref[0][:, j * LANES : (j + 1) * LANES].astype(f32))
    gatt_ref[0] = jnp.concatenate(attended, axis=1)
    product = jnp.concatenate(products, axis=1)
    owner = lax.broadcasted_iota(jnp.int32, (slots * hs, LANES), 0) // hs
    ones = (owner == lax.broadcasted_iota(jnp.int32, (slots * hs, LANES), 1)).astype(bf16)
    coarse = product.astype(bf16)
    fine = (product - coarse.astype(f32)).astype(bf16)
    inner = dot(coarse, ones) + dot(fine, ones)
    delta_ref[0] = inner.T[:slots, :]
    logit = inner - gate * jnp.sum(inner, axis=1, keepdims=True)
    lane = lax.broadcasted_iota(jnp.int32, shape, 1)
    spread_out = jnp.zeros(shape, f32)
    routes = routes_ref[0]
    for s in range(slots):
        spread_out = jnp.where(lane == routes[:, s : s + 1], logit[:, s : s + 1], spread_out)
    glog_ref[0] = spread_out.astype(bf16)


def query_weights_kernel(
    core, dq_ref, routes_ref, n_ref, send_ref, keep_ref, wide_ref, acc, *, heads, slots, per
):
    pairs = slots // 2
    experts = slot_experts(routes_ref[0], pairs)
    dq = [dq_ref[0][:, j * LANES : (j + 1) * LANES].astype(f32) for j in range(pairs)]
    wide = expand(dq, experts, heads // 2)
    wide_ref[0] = wide

    @pl.when(pl.program_id(0) == 0)
    def _():
        acc[...] = jnp.zeros_like(acc)

    acc[...] += dot(n_ref[0].T, wide)

    @pl.when(pl.program_id(0) == pl.num_programs(0) - 1)
    def _():
        split_core(acc[...], core[0], per, send_ref, keep_ref)


def input_kernel(
    wide_ref, glog_ref, dkv_ref, w_ref, x_ref, n_ref, gm_ref, norms_ref, sums_ref,
    ig_ref, small_ref, acck, accr, sums, *, at_kv, at_misc, heads,
):
    dkv, glog = dkv_ref[0], glog_ref[0]
    dn = (
        dot(wide_ref[0], w_ref[:, :at_kv], NT)
        + dot(dkv, w_ref[:, at_kv:at_misc], NT)
        + dot(glog, w_ref[:, at_misc : at_misc + LANES], NT)
    )
    vhat, rstd = normed_parts(x_ref[0].astype(f32))
    ig_ref[0] = gm_ref[0] + norm_back(dn, vhat, rstd, norms_ref[0:1, :])

    @pl.when(pl.program_id(0) == 0)
    def _():
        acck[...] = jnp.zeros_like(acck)
        accr[...] = jnp.zeros_like(accr)
        sums[...] = jnp.zeros_like(sums)

    nt = n_ref[0].T
    acck[...] += dot(nt, dkv)
    accr[...] += dot(nt, glog)
    sums[0:1, :] += jnp.sum(dn * vhat, axis=0, keepdims=True)
    sums[1:2, :] += jnp.sum(dn, axis=0, keepdims=True)

    @pl.when(pl.program_id(0) == pl.num_programs(0) - 1)
    def _():
        second = sums_ref[...]
        model = second.shape[1]
        rows = jnp.concatenate(
            [
                jnp.zeros((heads, model), f32),
                sums[0:1, :], second[0:1, :], sums[1:2, :], second[1:2, :],
                jnp.zeros((LANES - heads - 4, model), f32),
            ],
            axis=0,
        )
        small_ref[:, :LANES] = acck[...].astype(bf16)
        small_ref[:, LANES:] = (accr[...] + rows.T).astype(bf16)


def fixed(shape):
    return pl.BlockSpec(shape, lambda b, *_: (0,) * len(shape))


def per_block(*shape):
    return pl.BlockSpec((1, *shape), lambda b, *_: (b,) + (0,) * len(shape))


def like(shape, kind):
    return jax.ShapeDtypeStruct(shape, kind)


def cost(flops, size, exps=0):
    return pl.CostEstimate(flops=int(flops), bytes_accessed=int(size), transcendentals=int(exps))


def shards(
    tokens, segment_ids, routes, out_grad, w_query, w_keyval, w_output, w_router,
    norm_gains, norm_biases, w_up, w_down,
):
    rows, local, model = tokens.shape
    peers = lax.axis_size("mp")
    slots = routes.shape[2]
    heads = w_router.shape[1]
    hs = w_keyval.shape[1] // 2
    width = w_up.shape[1]
    chunk = local // 2
    blocks = rows * 2
    count = rows * local
    place = lax.axis_index("mp")
    wide = heads * hs
    slim = slots * hs
    at_kv, at_misc = wide, wide + 2 * hs

    def two(v):
        high = lax.reduce_precision(v, 8, 7)
        return [high.astype(bf16), (v - high).astype(bf16)]

    pads = jnp.zeros((w_query.shape[0], LANES - heads - 8), bf16)
    first = jnp.concatenate(
        [w_query, w_keyval, w_router, *two(norm_gains), *two(norm_biases), pads], axis=1
    )
    dp_groups = bit_groups("dp")
    far_groups, near_group = dp_groups[1:], dp_groups[0]
    depth = len(dp_groups)

    def far_stage(a, until=None):
        for i, group in enumerate(reversed(far_groups)):
            a = gather_bits(a, "dp", group, i, until)
        return a

    both = jnp.concatenate([w_up, w_down], axis=1)
    feed = lax.all_gather(both, ("dp", "mp"), axis=0, tiled=False)
    feed = feed.reshape(lax.axis_size("dp"), peers, *both.shape)
    y_bit, core_bit = (1, 1), (0, 1)
    first = far_stage(first)
    chosen = after(routes, first)
    chosen = (chosen[..., None] == jnp.arange(heads, dtype=jnp.int32)).astype(f32)
    held = jnp.sum(chosen, axis=(0, 1, 2))
    held_high = lax.reduce_precision(held, 8, 7)
    held = jnp.concatenate([held_high, held - held_high, jnp.zeros(LANES - 2 * heads, f32)])
    held = jnp.broadcast_to(held.astype(bf16), (w_output.shape[0], LANES))
    first_y = gather_bits(first, "mp", y_bit, depth - 1)
    proj = far_stage(after(jnp.concatenate([w_output, held], axis=1), first), first_y)
    first_x = gather_bits(first_y, "dp", near_group, depth - 1)
    first = gather_bits(first_x, "mp", core_bit, depth + 1)
    proj = gather_bits(after(proj, first_y), "mp", y_bit, depth - 1, first)
    weights = first.reshape(model, at_misc + LANES)

    single = jnp.argmax(segment_ids[:, -1] == 0).astype(jnp.int32)

    def swapped(a, start=None, until=None):
        kind = a.dtype
        if start is not None:
            a = after(a, start)
        a = a.reshape(rows, 2, chunk, -1)
        piece = lax.dynamic_index_in_dim(a[:, 1], single, 0, keepdims=False)
        piece = flip(piece.astype(bf16), "mp", peers - 1)
        if until is not None:
            piece = after(piece, until)
        return lax.dynamic_update_slice(a, piece.astype(kind)[None, None], (single, 1, 0, 0))

    def blocked(a):
        return a.reshape(blocks, chunk, -1)

    x = blocked(swapped(tokens))
    picks = blocked(swapped(routes, first_y, first_x))
    picks_t = jnp.swapaxes(picks, 1, 2)
    segments = after(segment_ids, first_x)
    near, far = 2 * place, 2 * (peers - 1 - place) + 1
    one = jnp.arange(rows, dtype=jnp.int32) == single
    last = jnp.stack(
        [jnp.full((rows,), near, jnp.int32), jnp.where(one, far, near + 1).astype(jnp.int32)], axis=1
    )
    ids = jnp.arange(8, dtype=jnp.int32)
    sizes = jnp.sum((segments[:, :, None] == ids).astype(jnp.int32), axis=1)
    own = jnp.stack(
        [
            jnp.stack(
                [lax.dynamic_slice(segments, (r, last[r, i] * chunk), (1, chunk))[0] for i in range(2)]
            )
            for r in range(rows)
        ]
    )
    start = jnp.sum(jnp.where(ids < own[..., None], sizes[:, None, None, :], 0), axis=-1)
    full = jnp.minimum((start[:, :, -1] + chunk - 1) // chunk, last)
    which = jnp.broadcast_to(jnp.arange(rows, dtype=jnp.int32)[:, None], (rows, 2))
    plan = jnp.stack([which, last, start[:, :, 0] // chunk, full], axis=-1).astype(jnp.int32)
    plan = jnp.concatenate([plan.reshape(-1), single[None], (place & 1).astype(jnp.int32)[None]])
    start = start.astype(jnp.int32).reshape(blocks, 1, chunk)

    n1, kv, norms = pl.pallas_call(
        functools.partial(norm_kernel, at_kv=at_kv, at_misc=at_misc, heads=heads),
        grid=(blocks,),
        in_specs=[per_block(chunk, model), fixed(weights.shape)],
        out_specs=[per_block(chunk, model), per_block(chunk, 2 * hs), fixed((8, model))],
        out_shape=[
            like((blocks, chunk, model), bf16),
            like((blocks, chunk, 2 * hs), bf16),
            like((8, model), f32),
        ],
        cost_estimate=cost(2 * count * model * LANES, 4 * MIB),
        name="norm_one",
    )(x, weights)
    kv_half = gather_bits(kv, "mp", y_bit, 0)
    kv_all = gather_bits(kv_half, "mp", core_bit, 1).reshape(peers * blocks, chunk, 2 * hs)
    proj = gather_bits(after(proj, weights), "dp", near_group, depth - 1, kv_half)

    q, gate, gate_t = pl.pallas_call(
        functools.partial(query_kernel, at_misc=at_misc, heads=heads, slots=slots, hs=hs),
        grid=(blocks,),
        in_specs=[
            per_block(chunk, model), fixed(weights.shape), per_block(chunk, slots), per_block(slots, chunk),
        ],
        out_specs=[per_block(chunk, slim), per_block(chunk, LANES), per_block(slots, chunk)],
        out_shape=[
            like((blocks, chunk, slim), bf16),
            like((blocks, chunk, LANES), f32),
            like((blocks, slots, chunk), f32),
        ],
        compiler_params=pltpu.CompilerParams(vmem_limit_bytes=24 * MIB),
        cost_estimate=cost(2 * count * model * wide * 2, 6 * MIB),
        name="queries",
    )(n1, weights, picks, picks_t)

    attention = dict(slots=slots, hs=hs, rows=rows, peers=peers)
    total = peers * blocks
    gc, lse = pl.pallas_call(
        functools.partial(attend_kernel, **attention),
        grid_spec=pltpu.PrefetchScalarGridSpec(
            num_scalar_prefetch=1,
            grid=(blocks,),
            in_specs=[
                per_block(chunk, slim), fixed(kv_all.shape), per_block(1, chunk), per_block(slots, chunk),
            ],
            out_specs=[per_block(chunk, slim), per_block(slots, chunk)],
            scratch_shapes=[
                pltpu.VMEM((total, 2 * hs, chunk), bf16),
                pltpu.VMEM((slim, chunk), bf16),
                pltpu.VMEM((slim, chunk), f32),
                pltpu.VMEM((slots, chunk), f32),
                pltpu.VMEM((slots, chunk), f32),
                pltpu.VMEM((chunk, chunk), f32),
            ],
        ),
        out_shape=[like((blocks, chunk, slim), bf16), like((blocks, slots, chunk), f32)],
        compiler_params=pltpu.CompilerParams(vmem_limit_bytes=24 * MIB),
        cost_estimate=cost(12e9, 4 * MIB),
        name="attend",
    )(plan, q, kv_all, start, gate_t)

    proj = gather_bits(proj, "mp", core_bit, depth + 1, gc).reshape(model, wide + LANES)
    grads = blocked(swapped(out_grad, kv_half, gc))
    core = (place & 1).astype(jnp.int32)[None]
    pair = peers // 2
    per = w_query.shape[0]

    def early(*shape):
        return pl.BlockSpec((1, *shape), lambda b, *_: (jnp.minimum(b, blocks - 1),) + (0,) * len(shape))

    def once(shape):
        return pl.BlockSpec(shape, lambda b, *_: (0,) * len(shape), pipeline_mode=pl.Buffered(1))

    feed_shape = (lax.axis_size("dp"), 2 * w_up.shape[0], width)
    gated, mid, outs, back, feed_sum = pl.pallas_call(
        functools.partial(forward_kernel, heads=heads, slots=slots, width=width, blocks=blocks),
        grid=(blocks + peers,),
        in_specs=[
            early(chunk, slim), early(chunk, slots), early(chunk, model), early(chunk, model),
            once(proj.shape), once(feed.shape), once(norms.shape),
        ],
        out_specs=[
            early(chunk, wide), early(chunk, model), early(chunk, model), early(chunk, model),
            pl.BlockSpec((1, *feed_shape), lambda b: (jnp.maximum(b - blocks, 0), 0, 0, 0)),
        ],
        scratch_shapes=[
            pltpu.VMEM((blocks, model, chunk), bf16),
            pltpu.VMEM((blocks, model, chunk), bf16),
            pltpu.VMEM((peers, blocks, chunk, width), bf16),
            pltpu.VMEM((peers, blocks, chunk, width), bf16),
        ],
        out_shape=[
            like((blocks, chunk, wide), bf16),
            like((blocks, chunk, model), f32),
            like((blocks, chunk, model), bf16),
            like((blocks, chunk, model), f32),
            like((peers, *feed_shape), bf16),
        ],
        compiler_params=pltpu.CompilerParams(vmem_limit_bytes=60 * MIB),
        cost_estimate=cost(24e9, 24 * MIB),
        name="forward",
    )(gc, picks, x, grads, proj, feed, norms)

    part, parts = model, wide // model

    def late_columns(b, core):
        return 0, jnp.maximum(b - blocks, 0)

    gm, gatt, delta, glog, sums, out_send, out_keep = pl.pallas_call(
        functools.partial(branch_back_kernel, heads=heads, slots=slots, hs=hs, blocks=blocks, per=per),
        grid_spec=pltpu.PrefetchScalarGridSpec(
            num_scalar_prefetch=1,
            grid=(blocks + parts,),
            in_specs=[
                early(chunk, model), early(chunk, model), early(chunk, model),
                early(chunk, slim), early(chunk, LANES), early(chunk, slots),
                once(proj.shape), once(norms.shape),
                pl.BlockSpec((blocks, chunk, part), lambda b, core: (0, *late_columns(b, core))),
            ],
            out_specs=[
                early(chunk, model), early(chunk, slim),
                early(slots, chunk), early(chunk, LANES), fixed((8, model)),
                pl.BlockSpec((model // 2, part), late_columns),
                pl.BlockSpec((model // 2, part), late_columns),
            ],
            scratch_shapes=[pltpu.VMEM((blocks, model, chunk), bf16)],
        ),
        out_shape=[
            like((blocks, chunk, model), f32),
            like((blocks, chunk, slim), bf16),
            like((blocks, slots, chunk), f32),
            like((blocks, chunk, LANES), bf16),
            like((8, model), f32),
            like((model // 2, wide), bf16),
            like((model // 2, wide), bf16),
        ],
        compiler_params=pltpu.CompilerParams(vmem_limit_bytes=60 * MIB),
        cost_estimate=cost(8e9, 14 * MIB),
        name="branch_back",
    )(core, back, mid, grads, gc, gate, picks, proj, norms, gated)

    def low_bits(a, axis, group, dim, until=None):
        return scatter_bits(a, axis, group, dim, until).astype(bf16)

    def across(send, keep, until):
        got = flip(send, "mp", 1)
        if until is not None:
            got = after(got, until)
        return (keep.astype(f32) + got.astype(f32)).astype(bf16)

    def far_scatter(a, until=None):
        for i, group in enumerate(far_groups):
            a = scatter_bits(a, "dp", group, depth - 2 - i, until)
            if i < len(far_groups) - 1:
                a = a.astype(bf16)
        return a

    def across(send, keep, until):
        got = flip(send, "mp", 1)
        if until is not None:
            got = after(got, until)
        return (keep.astype(f32) + got.astype(f32)).astype(bf16)

    groups = [2**bits for _, bits in reversed(dp_groups)]
    feed_part = lax.psum_scatter(feed_sum, "mp", scatter_dimension=0, tiled=False)
    feed_part = feed_part.reshape(*groups, *feed_shape[1:])
    half_kv = (total // 2, chunk, 2 * hs)
    dq, dkv_send, dkv_keep = pl.pallas_call(
        functools.partial(attend_back_kernel, **attention),
        grid_spec=pltpu.PrefetchScalarGridSpec(
            num_scalar_prefetch=1,
            grid=(blocks,),
            in_specs=[
                per_block(chunk, slim), per_block(chunk, slim), fixed(kv_all.shape), per_block(1, chunk),
                per_block(slots, chunk), per_block(slots, chunk),
            ],
            out_specs=[per_block(chunk, slim), fixed(half_kv), fixed(half_kv)],
            scratch_shapes=[
                pltpu.VMEM((total, 2 * hs, chunk), bf16),
                pltpu.VMEM((total, chunk, hs), bf16),
                pltpu.VMEM((slim, chunk), bf16),
                pltpu.VMEM((slim, chunk), bf16),
                pltpu.VMEM((slim, chunk), f32),
                pltpu.VMEM((total, chunk, hs), f32),
                pltpu.VMEM((total, chunk, hs), f32),
                pltpu.VMEM((chunk, chunk), f32),
            ],
        ),
        out_shape=[like((blocks, chunk, slim), bf16), like(half_kv, bf16), like(half_kv, bf16)],
        compiler_params=pltpu.CompilerParams(vmem_limit_bytes=32 * MIB),
        cost_estimate=cost(25e9, 6 * MIB),
        name="attend_back",
    )(plan, q, gatt, kv_all, start, lse, delta)

    outputs = swapped(outs, gatt, dq).reshape(rows, local, model)
    wq_send, wq_keep, spread = pl.pallas_call(
        functools.partial(query_weights_kernel, heads=heads, slots=slots, per=per),
        grid_spec=pltpu.PrefetchScalarGridSpec(
            num_scalar_prefetch=1,
            grid=(blocks,),
            in_specs=[per_block(chunk, slim), per_block(chunk, slots), per_block(chunk, model)],
            out_specs=[
                fixed((model // 2, wide)), fixed((model // 2, wide)), per_block(chunk, wide),
            ],
            scratch_shapes=[pltpu.VMEM((model, wide), f32)],
        ),
        out_shape=[
            like((model // 2, wide), bf16),
            like((model // 2, wide), bf16),
            like((blocks, chunk, wide), bf16),
        ],
        compiler_params=pltpu.CompilerParams(vmem_limit_bytes=28 * MIB),
        cost_estimate=cost(4e9, 10 * MIB),
        name="query_weights",
    )(core, dq, picks, n1)
    feed_part = low_bits(after(feed_part, dq), "dp", near_group, depth - 1, wq_send)
    out_part = across(out_send, out_keep, dq).reshape(*groups, 2, per, wide)
    out_part = low_bits(out_part, "mp", y_bit, depth, wq_send)
    dkv = across(dkv_send, dkv_keep, wq_send).reshape(pair, blocks * chunk, 2 * hs)
    dkv = low_bits(dkv, "mp", y_bit, 0).reshape(blocks, chunk, 2 * hs)
    query_part = across(wq_send, wq_keep, None).reshape(*groups, 2, per, wide)

    ig, small = pl.pallas_call(
        functools.partial(input_kernel, at_kv=at_kv, at_misc=at_misc, heads=heads),
        grid=(blocks,),
        in_specs=[
            per_block(chunk, wide), per_block(chunk, LANES), per_block(chunk, 2 * hs),
            fixed(weights.shape), per_block(chunk, model), per_block(chunk, model),
            per_block(chunk, model), fixed((8, model)), fixed((8, model)),
        ],
        out_specs=[per_block(chunk, model), fixed((model, 2 * LANES))],
        out_shape=[like((blocks, chunk, model), f32), like((model, 2 * LANES), bf16)],
        scratch_shapes=[
            pltpu.VMEM((model, 2 * hs), f32), pltpu.VMEM((model, LANES), f32), pltpu.VMEM((8, model), f32),
        ],
        compiler_params=pltpu.CompilerParams(vmem_limit_bytes=28 * MIB),
        cost_estimate=cost(4e9, 12 * MIB),
        name="inputs_back",
    )(after(spread, query_part), glog, dkv, weights, x, n1, gm, norms, sums)

    feed_grad = far_scatter(feed_part, ig)
    query_part = low_bits(query_part, "mp", y_bit, depth, ig)
    joint = jnp.concatenate([query_part, out_part], axis=-1)
    joint = low_bits(joint, "dp", near_group, depth - 1)
    tiles = after(small, query_part).reshape(model // per, per, 2 * LANES)
    tiles = lax.all_to_all(tiles, ("dp", "mp"), split_axis=0, concat_axis=0, tiled=True)
    smalls = jnp.sum(tiles.astype(f32), axis=0)
    up_rows = w_up.shape[0]
    joint = far_scatter(joint)
    input_grad = swapped(ig).reshape(rows, local, model)
    tallies = jnp.sum(proj.reshape(-1, per, wide + LANES)[:, 0, wide:].astype(f32), axis=0)
    counts = tallies[:heads] + tallies[heads : 2 * heads]
    return (
        outputs,
        input_grad,
        counts,
        joint[:, :wide],
        smalls[:, : 2 * hs],
        joint[:, wide:],
        smalls[:, LANES : LANES + heads],
        smalls[:, LANES + heads : LANES + heads + 2],
        smalls[:, LANES + heads + 2 : LANES + heads + 4],
        feed_grad[:up_rows],
        feed_grad[up_rows:],
    )


def solution(mesh):
    in_specs = (
        P("dp", "mp", None),
        P("dp", None),
        P("dp", "mp", None),
        P("dp", "mp", None),
        P(("dp", "mp"), None),
        P(("dp", "mp"), None),
        P(("dp", "mp"), None),
        P(("dp", "mp"), None),
        P(("dp", "mp"), None),
        P(("dp", "mp"), None),
        P("dp", "mp"),
        P("dp", "mp"),
    )
    out_specs = (
        P("dp", "mp", None),
        P("dp", "mp", None),
        P(),
        P(("dp", "mp"), None),
        P(("dp", "mp"), None),
        P(("dp", "mp"), None),
        P(("dp", "mp"), None),
        P(("dp", "mp"), None),
        P(("dp", "mp"), None),
        P("dp", "mp"),
        P("dp", "mp"),
    )
    return jax.shard_map(shards, mesh=mesh, in_specs=in_specs, out_specs=out_specs, check_vma=False)
```

time: 374 us -> 278 us (0.74)
  blocking collectives: 57 us -> 0 us
  starting transfers between devices: 63.8 us -> 44.6 us
  between operations: 1.51 us -> 18.2 us
  waiting for transfers between devices: 85.5 us -> 70.1 us
  other arithmetic: 28.4 us -> 14.8 us
  local copies, waits for them, and re-layouts: 31.6 us -> 22.2 us
  Pallas kernels: 102 us -> 107 us
    psum x1 -> x0, blocking collectives: 57 us -> none  [shards(): counts = lax.psum(jnp.sum(chosen, axis=(0, 1, 2)), ('dp', 'mp'))]
    ppermute x44 -> x33, starting transfers between devices: 58.7 us -> 40.1 us  [flip(): lax.ppermute(x, axis, [(i, i ^ mask) for i in range(lax.axis_size(axis))])]
    another operation x33 -> x5, other arithmetic: 13.2 us -> 0.68 us  [the longest x1 0.65 us: shards(): single = jnp.argmax(segment_ids[:, -1] == 0).astype(jnp.int32)]
    ppermute x44 -> x33, waiting for transfers between devices: 78.1 us -> 65.6 us  [flip(): lax.ppermute(x, axis, [(i, i ^ mask) for i in range(lax.axis_size(axis))])]
    another operation x11 -> x0, local copies, waits for them, and re-layouts: 9.68 us -> none  [the longest x4 5.36 us: gather_bits(): return jnp.stack(pieces, axis=dim)]
    select_n x0 -> x12, other arithmetic: none -> 8.03 us  [the longest x10 6.73 us: gather_bits(): jnp.where(odd, pieces[k + 1], pieces[k])]
    convert_element_type x13 -> x9, other arithmetic: 7.32 us -> 1.03 us  [the longest x3 0.53 us: across(): return (keep.astype(f32) + got.astype(f32)).astype(bf16)]
    pallas_call x4, Pallas kernels: 57.1 us -> 61.4 us  [the longest x1 28.4 us: shards(): pl.pallas_call(functools.partial(forward_kernel, heads=heads, slots=slots...]
  transfers between devices with their start and end apart: 45 -> 36, of which waited for: 16 -> 16; matrix products, arithmetic and copies ran while one was open for 12% -> 9% of each run, Pallas kernels for 13% -> 28%
where the time goes in v2:
time: 278 us; the launch traced here: 276 us
  Pallas kernels  107 us (38%)
  waiting for transfers between devices  70.1 us (25%)
  starting transfers between devices  44.6 us (16%)
  local copies, waits for them, and re-layouts  22.2 us (8%)
  between operations  18.2 us (7%)
  other arithmetic  14.8 us (5%)
    ppermute x33, waiting for transfers between devices, flip(): lax.ppermute(x, axis, [(i, i ^ mask) for i in range(lax.axis_size(axis))])  65.6 us
    ppermute x33, starting transfers between devices, flip(): lax.ppermute(x, axis, [(i, i ^ mask) for i in range(lax.axis_size(axis))])  40.1 us
    pallas_call x1, Pallas kernels, shards(): pl.pallas_call(functools.partial(forward_kernel, heads=heads, slots=slots...  28.4 us
    pallas_call x1, Pallas kernels, shards(): pl.pallas_call(functools.partial(attend_back_kernel, **attention), grid_s...  21.4 us
    pallas_call x1, Pallas kernels, shards(): pl.pallas_call(functools.partial(branch_back_kernel, heads=heads, slots=s...  18.9 us
    pallas_call x1, Pallas kernels, shards(): pl.pallas_call(functools.partial(attend_kernel, **attention), grid_spec=p...  12 us
    unnamed x93, local copies, waits for them, and re-layouts  11.6 us
    pallas_call x1, Pallas kernels, shards(): pl.pallas_call(functools.partial(query_weights_kernel, heads=heads, slots...  8.32 us
  transfers between devices with their start and end apart: 36, of which 16 were waited for; matrix products, arithmetic and copies ran while one was open for 9% of the time, Pallas kernels for 28%

profile of v2, /device:TPU:0, one launch (start us, length us, event | category | flops | bytes accessed | tf_op | source)
XLA Modules:
  0.0 276.4 jit_solution(16548738766989480385)
XLA Ops:
  10.3 3.0 %collective-permute-start.2 = (bf16[16,1792]{1,0:T(8,128)(2,1)S(1)}, bf16[16,1792]{1,0:T(8,128)(2,1)S(1)}, u32[]{:S(2)}, u32[]{:S(2)}) collective-permute-start(bf16[16,1792]{1,0:T(8,128)(2,1)S(1)} %concatenate.19), channel_id=1, source_target_pairs={{0,8},{4,12},{8,0},{12,4},{16,24},{20,28},{24,16},{28,20},{1,9},{5... | collective-permute-start | bytes 172040 | tf_op jit(solution)/shard_map/ppermute | solution.py:40
  13.3 2.6 collective-permute-start.1
  27.3 3.7 %collective-permute-start.13 = (bf16[16,1664]{1,0:T(8,128)(2,1)S(1)}, bf16[16,1664]{1,0:T(8,128)(2,1)S(1)}, u32[]{:S(2)}, u32[]{:S(2)}) collective-permute-start(bf16[16,1664]{1,0:T(8,128)(2,1)S(1)} %pad_maximum_fusion.1), channel_id=1, source_target_pairs={{0,24},{4,28},{8,16},{12,20},{16,8},{20,12},{24,0},{28,4},{1,25},{... | collective-permute-start | bytes 159752 | tf_op jit(solution)/shard_map/ppermute | solution.py:40
  31.8 2.9 %collective-permute-done.3 = bf16[4,16,1792]{2,1,0:T(8,128)(2,1)S(1)} collective-permute-done((bf16[4,16,1792]{2,1,0:T(8,128)(2,1)S(1)}, bf16[4,16,1792]{2,1,0:T(8,128)(2,1)S(1)}, u32[]{:S(2)}, u32[]{:S(2)}) %collective-permute-start.3) | collective-permute-done | bytes 229408 | tf_op jit(solution)/shard_map/ppermute | solution.py:40
  34.8 2.2 collective-permute-done.12
  40.8 4.0 %collective-permute-done.14 = bf16[4,16,1664]{2,1,0:T(8,128)(2,1)S(1)} collective-permute-done((bf16[4,16,1664]{2,1,0:T(8,128)(2,1)S(1)}, bf16[4,16,1664]{2,1,0:T(8,128)(2,1)S(1)}, u32[]{:S(2)}, u32[]{:S(2)}) %collective-permute-start.14) | collective-permute-done | bytes 213024 | tf_op jit(solution)/shard_map/ppermute | solution.py:40
  45.7 9.1 %collective-permute-done.4 = bf16[4,2,16,1792]{3,2,1,0:T(8,128)(2,1)} collective-permute-done((bf16[4,2,16,1792]{3,2,1,0:T(8,128)(2,1)S(1)}, bf16[4,2,16,1792]{3,2,1,0:T(8,128)(2,1)}, u32[]{:S(2)}, u32[]{:S(2)}) %collective-permute-start.4) | collective-permute-done | bytes 458784 | tf_op jit(solution)/shard_map/ppermute | solution.py:40
  60.0 1.7 collective-permute-start.15
  61.7 4.7 %norm_one.1 = (bf16[4,256,512]{2,1,0:T(8,128)(2,1)}, bf16[4,256,128]{2,1,0:T(8,128)(2,1)}, f32[8,512]{1,0:T(8,128)}) custom-call(bf16[4,256,512]{2,1,0:T(8,128)(2,1)} %bitcast.120, bf16[512,1792]{1,0:T(8,128)(2,1)} %bitcast_select_fusion.w_ref), custom_call_target="tpu_custom_call" | custom-call | flops 134217728 | bytes 4194304 | tf_op jit(solution)/shard_map/norm_one/pallas_call | solution.py:605
  68.0 7.0 %queries.1 = (bf16[4,256,512]{2,1,0:T(8,128)(2,1)S(1)}, f32[4,256,128]{2,1,0:T(8,128)S(1)}, f32[4,8,256]{2,1,0:T(8,128)S(1)}) custom-call(bf16[4,256,512]{2,1,0:T(8,128)(2,1)S(1)} %copy-done.5, bf16[512,1792]{1,0:T(8,128)(2,1)S(1)} %copy-done, s32[4,256,8]{2,1,0:T(8,128)S(1)} %bitcast.124, s32[4,8,256]{2,1,0:T(8,128)S(1)} %copy.98.routes_t_ref), custom_call_target="tpu_custom_call" | custom-call | flops 3221225472 | bytes 6291456 | tf_op jit(solution)/shard_map/queries/pallas_call | solution.py:622
  75.0 5.7 %collective-permute-done.8 = bf16[4,256,128]{2,1,0:T(8,128)(2,1)S(1)} collective-permute-done((bf16[4,256,128]{2,1,0:T(8,128)(2,1)}, bf16[4,256,128]{2,1,0:T(8,128)(2,1)S(1)}, u32[]{:S(2)}, u32[]{:S(2)}) %collective-permute-start.8) | collective-permute-done | bytes 262176 | tf_op jit(solution)/shard_map/ppermute | solution.py:40
  83.0 12.0 %attend.1 = (bf16[4,256,512]{2,1,0:T(8,128)(2,1)S(1)}, f32[4,8,256]{2,1,0:T(8,128)S(1)}) custom-call(s32[18]{0:T(128)S(1)} %pad_add_fusion.2.plan, bf16[4,256,512]{2,1,0:T(8,128)(2,1)S(1)} %get-tuple-element.72.q_ref, bf16[16,256,128]{2,1,0:T(8,128)(2,1)S(1)} %bitcast_select_fusion.2.kv_ref, s32[4,1,256]{2,1,0:T(1,128)S(1)} %reshape.262.start_ref, ...), custom_call_target="tpu_custom_call" | custom-call | flops 12000000000 | bytes 4194304 | tf_op jit(solution)/shard_map/attend/pallas_call | solution.py:641
  99.4 28.4 %forward.1 = (bf16[4,256,1536]{2,1,0:T(8,128)(2,1)}, f32[4,256,512]{2,1,0:T(8,128)}, bf16[4,256,512]{2,1,0:T(8,128)(2,1)}, f32[4,256,512]{2,1,0:T(8,128)}, bf16[4,8,128,512]{3,2,1,0:T(8,128)(2,1)}) custom-call(bf16[4,256,512]{2,1,0:T(8,128)(2,1)} %copy-done.13, s32[4,256,8]{2,1,0:T(8,128)} %bitcast.125, bf16[4,256,512]{2,1,0:T(8,128)(2,1)} %bitcast.121, ...), custom_call_target="tpu_custom_call" | custom-call | flops 24000000000 | bytes 25165824 | tf_op jit(solution)/shard_map/forward/pallas_call | solution.py:678
  127.8 18.9 %branch_back.1 = (f32[4,256,512]{2,1,0:T(8,128)}, bf16[4,256,512]{2,1,0:T(8,128)(2,1)}, f32[4,8,256]{2,1,0:T(8,128)}, bf16[4,256,128]{2,1,0:T(8,128)(2,1)}, f32[...) custom-call(s32[1]{0:T(128)} %bitcast.7.core, f32[4,256,512]{2,1,0:T(8,128)} %get-tuple-element.89.back_ref, ...), custom_call_target="tpu_custom_call" | custom-call | flops 8000000000 | bytes 14680064 | tf_op jit(solution)/shard_map/branch_back/pallas_call | solution.py:712
  150.3 21.4 %attend_back.1 = (bf16[4,256,512]{2,1,0:T(8,128)(2,1)S(1)}, bf16[8,256,128]{2,1,0:T(8,128)(2,1)S(1)}, bf16[8,256,128]{2,1,0:T(8,128)(2,1)S(1)}) custom-call(s32[18]{0:T(128)S(1)} %pad_add_fusion.2.plan, bf16[4,256,512]{2,1,0:T(8,128)(2,1)S(1)} %copy-done.10, bf16[4,256,512]{2,1,0:T(8,128)(2,1)S(1)} %copy-done.14, ...), custom_call_target="tpu_custom_call" | custom-call | flops 24999999488 | bytes 6291456 | tf_op jit(solution)/shard_map/attend_back/pallas_call | solution.py:771
  171.8 2.9 %collective-permute-start.19 = (bf16[8,256,128]{2,1,0:T(8,128)(2,1)S(1)}, bf16[8,256,128]{2,1,0:T(8,128)(2,1)S(1)}, u32[]{:S(2)}, u32[]{:S(2)}) collective-permute-start(bf16[8,256,128]{2,1,0:T(8,128)(2,1)S(1)} %get-tuple-element.105), channel_id=1, source_target_pairs={{0,1},{1,0},{2,3},{3,2},{4,5},{5,4},{6,7},{7,6},{8,9},{9,8},{10,11... | collective-permute-start | bytes 1572872 | tf_op jit(solution)/shard_map/ppermute | solution.py:40
  176.4 6.5 %collective-permute-start.17 = (bf16[256,512]{1,0:T(8,128)(2,1)S(1)}, bf16[256,512]{1,0:T(8,128)(2,1)S(1)}, u32[]{:S(2)}, u32[]{:S(2)}) collective-permute-start(bf16[256,512]{1,0:T(8,128)(2,1)S(1)} %dynamic-slice_bitcast_fusion.2), channel_id=1, source_target_pairs={{0,3},{1,2},{2,1},{3,0},{4,7},{5,6},{6,5},{7,4},{8,11},{9,10},{10,... | collective-permute-start | bytes 786440 | tf_op jit(solution)/shard_map/ppermute | solution.py:40
  183.0 8.3 %query_weights.1 = (bf16[256,1536]{1,0:T(8,128)(2,1)S(1)}, bf16[256,1536]{1,0:T(8,128)(2,1)S(1)}, bf16[4,256,1536]{2,1,0:T(8,128)(2,1)S(1)}) custom-call(s32[1]{0:T(128)} %bitcast.7.core, bf16[4,256,512]{2,1,0:T(8,128)(2,1)S(1)} %get-tuple-element.97.dq_ref, s32[4,256,8]{2,1,0:T(8,128)S(1)} %bitcast.127, bf16[4,256,512]{2,1,0:T(8,128)(2,1)S(1)} %copy-done.6), custom_call_target="tpu_custom_call" | custom-call | flops 4000000000 | bytes 10485760 | tf_op jit(solution)/shard_map/query_weights/pallas_call | solution.py:799
  195.2 5.6 %collective-permute-done.20 = bf16[1024,128]{1,0:T(8,128)(2,1)S(1)} collective-permute-done((bf16[1024,128]{1,0:T(8,128)(2,1)S(1)}, bf16[1024,128]{1,0:T(8,128)(2,1)S(1)}, u32[]{:S(2)}, u32[]{:S(2)}) %collective-permute-start.20) | collective-permute-done | bytes 262176 | tf_op jit(solution)/shard_map/ppermute | solution.py:40
  200.9 5.7 %inputs_back.1 = (f32[4,256,512]{2,1,0:T(8,128)}, bf16[512,256]{1,0:T(8,128)(2,1)}) custom-call(bf16[4,256,1536]{2,1,0:T(8,128)(2,1)S(1)} %get-tuple-element.102.wide_ref, bf16[4,256,128]{2,1,0:T(8,128)(2,1)S(1)} %copy-done.11, bf16[4,256,128]{2,1,0:T(8,128)(2,1)S(1)} %bitcast.128, bf16[512,1792]{1,0:T(8,128)(2,1)S(1)} %copy-done, ...), custom_call_target="tpu_custom_call" | custom-call | flops 4000000000 | bytes 12582912 | tf_op jit(solution)/shard_map/inputs_back/pallas_call | solution.py:826
  206.7 2.6 collective-permute-done.24
  209.2 8.0 %collective-permute-done.22 = bf16[4,2,16,1536]{3,2,0,1:T(8,128)(2,1)S(1)} collective-permute-done((bf16[4,2,16,1536]{3,2,0,1:T(8,128)(2,1)S(1)}, bf16[4,2,16,1536]{3,2,0,1:T(8,128)(2,1)S(1)}, u32[]{:S(2)}, u32[]{:S(2)}) %collective-permute-start.22) | collective-permute-done | bytes 393248 | tf_op jit(solution)/shard_map/ppermute | solution.py:40
  219.8 8.4 %collective-permute-done.25 = bf16[4,16,3072]{2,1,0:T(8,128)(2,1)S(1)} collective-permute-done((bf16[4,16,3072]{2,1,0:T(8,128)(2,1)S(1)}, bf16[4,16,3072]{2,1,0:T(8,128)(2,1)S(1)}, u32[]{:S(2)}, u32[]{:S(2)}) %collective-permute-start.25) | collective-permute-done | bytes 393248 | tf_op jit(solution)/shard_map/ppermute | solution.py:40
  228.4 3.3 %collective-permute-start.28 = (bf16[16,3072]{1,0:T(8,128)(2,1)S(1)}, bf16[16,3072]{1,0:T(8,128)(2,1)S(1)}, u32[]{:S(2)}, u32[]{:S(2)}) collective-permute-start(bf16[16,3072]{1,0:T(8,128)(2,1)S(1)} %get-tuple-element.186), channel_id=1, source_target_pairs={{0,24},{4,28},{8,16},{12,20},{16,8},{20,12},{24,0},{28,4},{1,25},{... | collective-permute-start | bytes 294920 | tf_op jit(solution)/shard_map/ppermute | solution.py:40
  232.0 4.3 %all-to-all-start = ((bf16[32,16,256]{2,1,0:T(8,128)(2,1)}), bf16[32,16,256]{2,1,0:T(8,128)(2,1)S(1)}, u32[]{:S(2)}, u32[]{:S(2)}) async-start(bf16[32,16,256]{2,1,0:T(8,128)(2,1)} %bitcast.54), calls=%async_computation | async-start | bytes 524288 | tf_op jit(solution)/shard_map/all_to_all | solution.py:849
  236.4 3.0 %collective-permute-done.27 = bf16[16,3072]{1,0:T(8,128)(2,1)S(1)} collective-permute-done((bf16[16,3072]{1,0:T(8,128)(2,1)S(1)}, bf16[16,3072]{1,0:T(8,128)(2,1)S(1)}, u32[]{:S(2)}, u32[]{:S(2)}) %collective-permute-start.27) | collective-permute-done | bytes 98336 | tf_op jit(solution)/shard_map/ppermute | solution.py:40
  242.6 4.4 %all-to-all-done = bf16[32,16,256]{2,1,0:T(8,128)(2,1)S(1)} async-done(((bf16[32,16,256]{2,1,0:T(8,128)(2,1)}), bf16[32,16,256]{2,1,0:T(8,128)(2,1)S(1)}, u32[]{:S(2)}, u32[]{:S(2)}) %all-to-all-start) | async-done | bytes 262176 | tf_op jit(solution)/shard_map/all_to_all | solution.py:849
  248.2 6.5 %collective-permute-done.29 = bf16[4,128,512]{2,1,0:T(8,128)(2,1)S(1)} collective-permute-done((bf16[4,128,512]{2,1,0:T(8,128)(2,1)S(1)}, bf16[4,128,512]{2,1,0:T(8,128)(2,1)S(1)}, u32[]{:S(2)}, u32[]{:S(2)}) %collective-permute-start.29) | collective-permute-done | bytes 524320 | tf_op jit(solution)/shard_map/ppermute | solution.py:40
  254.9 2.1 collective-permute-start.32
  256.9 2.4 collective-permute-start.30
  260.7 2.5 collective-permute-done.32
  263.2 4.7 %collective-permute-done.31 = bf16[128,512]{1,0:T(8,128)(2,1)S(1)} collective-permute-done((bf16[128,512]{1,0:T(8,128)(2,1)S(1)}, bf16[128,512]{1,0:T(8,128)(2,1)S(1)}, u32[]{:S(2)}, u32[]{:S(2)}) %collective-permute-start.31) | collective-permute-done | bytes 131104 | tf_op jit(solution)/shard_map/ppermute | solution.py:40
  (244 shorter events, 49.6 us)
Async XLA Ops:
  7.3 92.1 %all-gather.3.cloned.1.call-start = ((), (), s32[]{:S(2)}) async-start(), calls=%async_computation.3 | async-start | bytes 4325376 | tf_op jit(solution)/shard_map/all_gather | solution.py:546
  10.3 15.1 %collective-permute-start.2 = (bf16[16,1792]{1,0:T(8,128)(2,1)S(1)}, bf16[16,1792]{1,0:T(8,128)(2,1)S(1)}, u32[]{:S(2)}, u32[]{:S(2)}) collective-permute-start(bf16[16,1792]{1,0:T(8,128)(2,1)S(1)} %concatenate.19), channel_id=1, source_target_pairs={{0,8},{4,12},{8,0},{12,4},{16,24},{20,28},{24,16},{28,20},{1,9},{5... | collective-permute-start | bytes 172040 | tf_op jit(solution)/shard_map/ppermute | solution.py:40
  13.3 12.1 %collective-permute-start.1 = (bf16[16,1792]{1,0:T(8,128)(2,1)S(1)}, bf16[16,1792]{1,0:T(8,128)(2,1)S(1)}, u32[]{:S(2)}, u32[]{:S(2)}) collective-permute-start(bf16[16,1792]{1,0:T(8,128)(2,1)S(1)} %concatenate.19), channel_id=1, source_target_pairs={{0,16},{4,20},{8,24},{12,28},{16,0},{20,4},{24,8},{28,12},{1,17},{... | collective-permute-start | bytes 172040 | tf_op jit(solution)/shard_map/ppermute | solution.py:40
  15.9 9.5 %collective-permute-start = (bf16[16,1792]{1,0:T(8,128)(2,1)S(1)}, bf16[16,1792]{1,0:T(8,128)(2,1)S(1)}, u32[]{:S(2)}, u32[]{:S(2)}) collective-permute-start(bf16[16,1792]{1,0:T(8,128)(2,1)S(1)} %concatenate.19), channel_id=1, source_target_pairs={{0,24},{4,28},{8,16},{12,20},{16,8},{20,12},{24,0},{28,4},{1,25},{... | collective-permute-start | bytes 172040 | tf_op jit(solution)/shard_map/ppermute | solution.py:40
  16.6 222.8 %reduce-scatter.2.cloned.1.call-start = ((), (), s32[]{:S(2)}) async-start(), calls=%async_computation.2 | async-start | bytes 5242880 | tf_op jit(solution)/shard_map/reduce_scatter | solution.py:768
  20.2 18.5 %collective-permute-start.5 = (bf16[256,512]{1,0:T(8,128)(2,1)S(1)}, bf16[256,512]{1,0:T(8,128)(2,1)S(1)}, u32[]{:S(2)}, u32[]{:S(2)}) collective-permute-start(bf16[256,512]{1,0:T(8,128)(2,1)S(1)} %dynamic-slice_bitcast_fusion.4), channel_id=1, source_target_pairs={{0,3},{1,2},{2,1},{3,0},{4,7},{5,6},{6,5},{7,4},{8,11},{9,10},{10,... | collective-permute-start | bytes 786440 | tf_op jit(solution)/shard_map/ppermute | solution.py:40
  25.5 9.2 %collective-permute-start.3 = (bf16[4,16,1792]{2,1,0:T(8,128)(2,1)S(1)}, bf16[4,16,1792]{2,1,0:T(8,128)(2,1)S(1)}, u32[]{:S(2)}, u32[]{:S(2)}) collective-permute-start(bf16[4,16,1792]{2,1,0:T(8,128)(2,1)S(1)} %select_select_fusion), channel_id=1, source_target_pairs={{0,2},{1,3},{2,0},{3,1},{4,6},{5,7},{6,4},{7,5},{8,10},{9,11},{10,... | collective-permute-start | bytes 688136 | tf_op jit(solution)/shard_map/ppermute | solution.py:40
  27.3 7.5 %collective-permute-start.13 = (bf16[16,1664]{1,0:T(8,128)(2,1)S(1)}, bf16[16,1664]{1,0:T(8,128)(2,1)S(1)}, u32[]{:S(2)}, u32[]{:S(2)}) collective-permute-start(bf16[16,1664]{1,0:T(8,128)(2,1)S(1)} %pad_maximum_fusion.1), channel_id=1, source_target_pairs={{0,24},{4,28},{8,16},{12,20},{16,8},{20,12},{24,0},{28,4},{1,25},{... | collective-permute-start | bytes 159752 | tf_op jit(solution)/shard_map/ppermute | solution.py:40
  31.0 6.1 %collective-permute-start.11 = (bf16[16,1664]{1,0:T(8,128)(2,1)S(1)}, bf16[16,1664]{1,0:T(8,128)(2,1)S(1)}, u32[]{:S(2)}, u32[]{:S(2)}) collective-permute-start(bf16[16,1664]{1,0:T(8,128)(2,1)S(1)} %pad_maximum_fusion.1), channel_id=1, source_target_pairs={{0,8},{4,12},{8,0},{12,4},{16,24},{20,28},{24,16},{28,20},{1,9},{5... | collective-permute-start | bytes 159752 | tf_op jit(solution)/shard_map/ppermute | solution.py:40
  37.2 7.6 %collective-permute-start.14 = (bf16[4,16,1664]{2,1,0:T(8,128)(2,1)S(1)}, bf16[4,16,1664]{2,1,0:T(8,128)(2,1)S(1)}, u32[]{:S(2)}, u32[]{:S(2)}) collective-permute-start(bf16[4,16,1664]{2,1,0:T(8,128)(2,1)S(1)} %select_select_fusion.1), channel_id=1, source_target_pairs={{0,2},{1,3},{2,0},{3,1},{4,6},{5,7},{6,4},{7,5},{8,10},{9,11},{10,... | collective-permute-start | bytes 638984 | tf_op jit(solution)/shard_map/ppermute | solution.py:40
  38.8 16.1 %collective-permute-start.4 = (bf16[4,2,16,1792]{3,2,1,0:T(8,128)(2,1)S(1)}, bf16[4,2,16,1792]{3,2,1,0:T(8,128)(2,1)}, u32[]{:S(2)}, u32[]{:S(2)}) collective-permute-start(bf16[4,2,16,1792]{3,2,1,0:T(8,128)(2,1)S(1)} %broadcast_select_fusion.3), channel_id=1, source_target_pairs={{0,4},{4,0},{8,12},{12,8},{16,20},{20,16},{24,28},{28,24},{1,5},{5... | collective-permute-start | bytes 1376264 | tf_op jit(solution)/shard_map/ppermute | solution.py:40
  40.8 16.4 %collective-permute-start.7 = (bf16[256,8]{1,0:T(8,128)(2,1)S(1)}, bf16[256,8]{1,0:T(8,128)(2,1)S(1)}, u32[]{:S(2)}, u32[]{:S(2)}) collective-permute-start(bf16[256,8]{1,0:T(8,128)(2,1)S(1)} %fusion.14), channel_id=1, source_target_pairs={{0,3},{1,2},{2,1},{3,0},{4,7},{5,6},{6,5},{7,4},{8,11},{9,10},{10,... | collective-permute-start | bytes 12296 | tf_op jit(solution)/shard_map/ppermute | solution.py:40
  60.0 21.5 %collective-permute-start.15 = (bf16[4,2,16,1664]{3,2,1,0:T(8,128)(2,1)S(1)}, bf16[4,2,16,1664]{3,2,1,0:T(8,128)(2,1)}, u32[]{:S(2)}, u32[]{:S(2)}) collective-permute-start(bf16[4,2,16,1664]{3,2,1,0:T(8,128)(2,1)S(1)} %copy-done.23), channel_id=1, source_target_pairs={{0,4},{4,0},{8,12},{12,8},{16,20},{20,16},{24,28},{28,24},{1,5},{5... | collective-permute-start | bytes 1277960 | tf_op jit(solution)/shard_map/ppermute | solution.py:40
  66.5 14.2 %collective-permute-start.8 = (bf16[4,256,128]{2,1,0:T(8,128)(2,1)}, bf16[4,256,128]{2,1,0:T(8,128)(2,1)S(1)}, u32[]{:S(2)}, u32[]{:S(2)}) collective-permute-start(bf16[4,256,128]{2,1,0:T(8,128)(2,1)} %get-tuple-element.73), channel_id=1, source_target_pairs={{0,2},{1,3},{2,0},{3,1},{4,6},{5,7},{6,4},{7,5},{8,10},{9,11},{10,... | collective-permute-start | bytes 786440 | tf_op jit(solution)/shard_map/ppermute | solution.py:40
  81.0 15.0 %collective-permute-start.10 = (bf16[256,512]{1,0:T(8,128)(2,1)S(1)}, bf16[256,512]{1,0:T(8,128)(2,1)S(1)}, u32[]{:S(2)}, u32[]{:S(2)}) collective-permute-start(bf16[256,512]{1,0:T(8,128)(2,1)S(1)} %dynamic-slice_bitcast_fusion.3), channel_id=1, source_target_pairs={{0,3},{1,2},{2,1},{3,0},{4,7},{5,6},{6,5},{7,4},{8,11},{9,10},{10,... | collective-permute-start | bytes 786440 | tf_op jit(solution)/shard_map/ppermute | solution.py:40
  82.7 13.3 %collective-permute-start.16 = (bf16[4,2,2,16,1664]{4,3,2,1,0:T(8,128)(2,1)S(1)}, bf16[4,2,2,16,1664]{4,3,2,1,0:T(8,128)(2,1)S(1)}, u32[]{:S(2)}, u32[]{:S(2)}) collective-permute-start(bf16[4,2,2,16,1664]{4,3,2,1,0:T(8,128)(2,1)S(1)} %broadcast_select_fusion.1), channel_id=1, source_target_pairs={{0,1},{1,0},{2,3},{3,2},{4,5},{5,4},{6,7},{7,6},{8,9},{9,8},{10,11... | collective-permute-start | bytes 2555912 | tf_op jit(solution)/shard_map/ppermute | solution.py:40
  171.8 19.7 %collective-permute-start.19 = (bf16[8,256,128]{2,1,0:T(8,128)(2,1)S(1)}, bf16[8,256,128]{2,1,0:T(8,128)(2,1)S(1)}, u32[]{:S(2)}, u32[]{:S(2)}) collective-permute-start(bf16[8,256,128]{2,1,0:T(8,128)(2,1)S(1)} %get-tuple-element.105), channel_id=1, source_target_pairs={{0,1},{1,0},{2,3},{3,2},{4,5},{5,4},{6,7},{7,6},{8,9},{9,8},{10,11... | collective-permute-start | bytes 1572872 | tf_op jit(solution)/shard_map/ppermute | solution.py:40
  176.3 16.1 %collective-permute-start.23 = (bf16[256,1536]{1,0:T(8,128)(2,1)S(1)}, bf16[256,1536]{1,0:T(8,128)(2,1)S(1)}, u32[]{:S(2)}, u32[]{:S(2)}) collective-permute-start(bf16[256,1536]{1,0:T(8,128)(2,1)S(1)} %copy-done.44), channel_id=1, source_target_pairs={{0,1},{1,0},{2,3},{3,2},{4,5},{5,4},{6,7},{7,6},{8,9},{9,8},{10,11... | collective-permute-start | bytes 2359304 | tf_op jit(solution)/shard_map/ppermute | solution.py:40
  176.4 41.7 %collective-permute-start.17 = (bf16[256,512]{1,0:T(8,128)(2,1)S(1)}, bf16[256,512]{1,0:T(8,128)(2,1)S(1)}, u32[]{:S(2)}, u32[]{:S(2)}) collective-permute-start(bf16[256,512]{1,0:T(8,128)(2,1)S(1)} %dynamic-slice_bitcast_fusion.2), channel_id=1, source_target_pairs={{0,3},{1,2},{2,1},{3,0},{4,7},{5,6},{6,5},{7,4},{8,11},{9,10},{10,... | collective-permute-start | bytes 786440 | tf_op jit(solution)/shard_map/ppermute | solution.py:40
  191.6 9.2 %collective-permute-start.20 = (bf16[1024,128]{1,0:T(8,128)(2,1)S(1)}, bf16[1024,128]{1,0:T(8,128)(2,1)S(1)}, u32[]{:S(2)}, u32[]{:S(2)}) collective-permute-start(bf16[1024,128]{1,0:T(8,128)(2,1)S(1)} %dynamic-slice_bitcast_fusion.1), channel_id=1, source_target_pairs={{0,2},{1,3},{2,0},{3,1},{4,6},{5,7},{6,4},{7,5},{8,10},{9,11},{10,... | collective-permute-start | bytes 786440 | tf_op jit(solution)/shard_map/ppermute | solution.py:40
  192.7 16.5 %collective-permute-start.24 = (bf16[4,2,16,1536]{3,2,0,1:T(8,128)(2,1)S(1)}, bf16[4,2,16,1536]{3,2,0,1:T(8,128)(2,1)S(1)}, u32[]{:S(2)}, u32[]{:S(2)}) collective-permute-start(bf16[4,2,16,1536]{3,2,0,1:T(8,128)(2,1)S(1)} %bitcast.141), channel_id=1, source_target_pairs={{0,2},{1,3},{2,0},{3,1},{4,6},{5,7},{6,4},{7,5},{8,10},{9,11},{10,... | collective-permute-start | bytes 1179656 | tf_op jit(solution)/shard_map/ppermute | solution.py:40
  194.4 22.8 %collective-permute-start.22 = (bf16[4,2,16,1536]{3,2,0,1:T(8,128)(2,1)S(1)}, bf16[4,2,16,1536]{3,2,0,1:T(8,128)(2,1)S(1)}, u32[]{:S(2)}, u32[]{:S(2)}) collective-permute-start(bf16[4,2,16,1536]{3,2,0,1:T(8,128)(2,1)S(1)} %bitcast.142), channel_id=1, source_target_pairs={{0,2},{1,3},{2,0},{3,1},{4,6},{5,7},{6,4},{7,5},{8,10},{9,11},{10,... | collective-permute-start | bytes 1179656 | tf_op jit(solution)/shard_map/ppermute | solution.py:40
  217.4 10.7 %collective-permute-start.25 = (bf16[4,16,3072]{2,1,0:T(8,128)(2,1)S(1)}, bf16[4,16,3072]{2,1,0:T(8,128)(2,1)S(1)}, u32[]{:S(2)}, u32[]{:S(2)}) collective-permute-start(bf16[4,16,3072]{2,1,0:T(8,128)(2,1)S(1)} %fusion.6), channel_id=1, source_target_pairs={{0,4},{4,0},{8,12},{12,8},{16,20},{20,16},{24,28},{28,24},{1,5},{5... | collective-permute-start | bytes 1179656 | tf_op jit(solution)/shard_map/ppermute | solution.py:40
  228.3 8.0 %collective-permute-start.26 = (bf16[16,3072]{1,0:T(8,128)(2,1)S(1)}, bf16[16,3072]{1,0:T(8,128)(2,1)S(1)}, u32[]{:S(2)}, u32[]{:S(2)}) collective-permute-start(bf16[16,3072]{1,0:T(8,128)(2,1)S(1)} %get-tuple-element.185), channel_id=1, source_target_pairs={{0,8},{4,12},{8,0},{12,4},{16,24},{20,28},{24,16},{28,20},{1,9},{5... | collective-permute-start | bytes 294920 | tf_op jit(solution)/shard_map/ppermute | solution.py:40
  228.4 8.0 %collective-permute-start.28 = (bf16[16,3072]{1,0:T(8,128)(2,1)S(1)}, bf16[16,3072]{1,0:T(8,128)(2,1)S(1)}, u32[]{:S(2)}, u32[]{:S(2)}) collective-permute-start(bf16[16,3072]{1,0:T(8,128)(2,1)S(1)} %get-tuple-element.186), channel_id=1, source_target_pairs={{0,24},{4,28},{8,16},{12,20},{16,8},{20,12},{24,0},{28,4},{1,25},{... | collective-permute-start | bytes 294920 | tf_op jit(solution)/shard_map/ppermute | solution.py:40
  231.7 7.7 %collective-permute-start.27 = (bf16[16,3072]{1,0:T(8,128)(2,1)S(1)}, bf16[16,3072]{1,0:T(8,128)(2,1)S(1)}, u32[]{:S(2)}, u32[]{:S(2)}) collective-permute-start(bf16[16,3072]{1,0:T(8,128)(2,1)S(1)} %get-tuple-element.187), channel_id=1, source_target_pairs={{0,16},{4,20},{8,24},{12,28},{16,0},{20,4},{24,8},{28,12},{1,17},{... | collective-permute-start | bytes 294920 | tf_op jit(solution)/shard_map/ppermute | solution.py:40
  231.9 36.8 %collective-permute-start.21 = (bf16[256,512]{1,0:T(8,128)(2,1)S(1)}, bf16[256,512]{1,0:T(8,128)(2,1)S(1)}, u32[]{:S(2)}, u32[]{:S(2)}) collective-permute-start(bf16[256,512]{1,0:T(8,128)(2,1)S(1)} %fusion.9), channel_id=1, source_target_pairs={{0,3},{1,2},{2,1},{3,0},{4,7},{5,6},{6,5},{7,4},{8,11},{9,10},{10,... | collective-permute-start | bytes 786440 | tf_op jit(solution)/shard_map/ppermute | solution.py:40
  232.0 15.0 %all-to-all-start = ((bf16[32,16,256]{2,1,0:T(8,128)(2,1)}), bf16[32,16,256]{2,1,0:T(8,128)(2,1)S(1)}, u32[]{:S(2)}, u32[]{:S(2)}) async-start(bf16[32,16,256]{2,1,0:T(8,128)(2,1)} %bitcast.54), calls=%async_computation | async-start | bytes 524288 | tf_op jit(solution)/shard_map/all_to_all | solution.py:849
  240.6 14.0 %collective-permute-start.29 = (bf16[4,128,512]{2,1,0:T(8,128)(2,1)S(1)}, bf16[4,128,512]{2,1,0:T(8,128)(2,1)S(1)}, u32[]{:S(2)}, u32[]{:S(2)}) collective-permute-start(bf16[4,128,512]{2,1,0:T(8,128)(2,1)S(1)} %dynamic-slice_bitcast_fusion), channel_id=1, source_target_pairs={{0,4},{4,0},{8,12},{12,8},{16,20},{20,16},{24,28},{28,24},{1,5},{5... | collective-permute-start | bytes 1572872 | tf_op jit(solution)/shard_map/ppermute | solution.py:40
  254.9 8.3 %collective-permute-start.32 = (bf16[128,512]{1,0:T(8,128)(2,1)S(1)}, bf16[128,512]{1,0:T(8,128)(2,1)S(1)}, u32[]{:S(2)}, u32[]{:S(2)}) collective-permute-start(bf16[128,512]{1,0:T(8,128)(2,1)S(1)} %get-tuple-element.182), channel_id=1, source_target_pairs={{0,24},{4,28},{8,16},{12,20},{16,8},{20,12},{24,0},{28,4},{1,25},{... | collective-permute-start | bytes 393224 | tf_op jit(solution)/shard_map/ppermute | solution.py:40
  256.9 11.0 %collective-permute-start.31 = (bf16[128,512]{1,0:T(8,128)(2,1)S(1)}, bf16[128,512]{1,0:T(8,128)(2,1)S(1)}, u32[]{:S(2)}, u32[]{:S(2)}) collective-permute-start(bf16[128,512]{1,0:T(8,128)(2,1)S(1)} %get-tuple-element.183), channel_id=1, source_target_pairs={{0,16},{4,20},{8,24},{12,28},{16,0},{20,4},{24,8},{28,12},{1,17},{... | collective-permute-start | bytes 393224 | tf_op jit(solution)/shard_map/ppermute | solution.py:40
  256.9 11.0 %collective-permute-start.30 = (bf16[128,512]{1,0:T(8,128)(2,1)S(1)}, bf16[128,512]{1,0:T(8,128)(2,1)S(1)}, u32[]{:S(2)}, u32[]{:S(2)}) collective-permute-start(bf16[128,512]{1,0:T(8,128)(2,1)S(1)} %get-tuple-element.184), channel_id=1, source_target_pairs={{0,8},{4,12},{8,0},{12,4},{16,24},{20,28},{24,16},{28,20},{1,9},{5... | collective-permute-start | bytes 393224 | tf_op jit(solution)/shard_map/ppermute | solution.py:40
  (49 other events, 342.8 us)
Sparse Core Ops, SparseCore 0:
  16.7 72.3 all-gather.2
  128.0 46.6 reduce-scatter.1

commit v3 on v2

--- a/solution.py
+++ b/solution.py
@@ -60,21 +60,30 @@
     return pieces[0]
 
 
-def scatter_bits(x, axis, group, dim, until=None):
+def scatter_start(x, axis, group, dim):
     low, width = group
     mine = (lax.axis_index(axis) >> low) & (2**width - 1)
-    got = [
-        flip(lax.dynamic_index_in_dim(x, mine ^ k, dim, keepdims=False), axis, k << low)
-        for k in range(1, 2**width)
+    sent = [
+        lax.dynamic_index_in_dim(x, mine ^ k, dim, keepdims=False) for k in range(1, 2**width)
     ]
+    got = [flip(a, axis, k << low) for k, a in enumerate(sent, 1)]
+    return lax.dynamic_index_in_dim(x, mine, dim, keepdims=False), got, sent
+
+
+def scatter_end(started, until=None):
+    total, got, _ = started
     if until is not None:
         got = lax.optimization_barrier((*got, until))[:-1]
-    total = lax.dynamic_index_in_dim(x, mine, dim, keepdims=False).astype(f32)
+    total = total.astype(f32)
     for g in got:
         total = total + g.astype(f32)
     return total
 
 
+def scatter_bits(x, axis, group, dim, until=None):
+    return scatter_end(scatter_start(x, axis, group, dim), until)
+
+
 def halves(row_first, row_second, like):
     lane = lax.broadcasted_iota(jnp.int32, like, 1)
     return jnp.where(lane < LANES // 2, row_first, row_second)
@@ -92,15 +101,16 @@
 def compact(wide, experts, head_pairs):
     lane = lax.broadcasted_iota(jnp.int32, experts[0].shape, 1)
     high = (lane >= LANES // 2).astype(jnp.int32)
-    straight = [e - high for e in experts]
-    crossed = [e + high for e in experts]
-    found = [jnp.zeros(experts[0].shape, f32) for _ in experts]
+    straight = [(e - high).astype(jnp.int16) for e in experts]
+    crossed = [(e + high).astype(jnp.int16) for e in experts]
+    found = [jnp.zeros(experts[0].shape, bf16) for _ in experts]
     for i in range(head_pairs):
         block = wide(i)
-        turned = turn_half(block)
+        turned = turn_half(block).astype(bf16)
+        block = block.astype(bf16)
         for j in range(len(experts)):
-            found[j] = jnp.where(straight[j] == 2 * i, block, found[j])
-            found[j] = jnp.where(crossed[j] == 2 * i + 1, turned, found[j])
+            found[j] = jnp.where(straight[j] == jnp.int16(2 * i), block, found[j])
+            found[j] = jnp.where(crossed[j] == jnp.int16(2 * i + 1), turned, found[j])
     return found
 
 
@@ -109,14 +119,14 @@
     high = (lane >= LANES // 2).astype(jnp.int32)
     sources = []
     for block, e in zip(narrow, experts):
-        sources.append((e - high, block))
-        sources.append((turn_half(e) - high, turn_half(block)))
+        sources.append(((e - high).astype(jnp.int16), block.astype(bf16)))
+        sources.append(((turn_half(e) - high).astype(jnp.int16), turn_half(block).astype(bf16)))
     wide = []
     for i in range(head_pairs):
-        out = jnp.zeros(experts[0].shape, f32)
+        out = jnp.zeros(experts[0].shape, bf16)
         for e, block in sources:
-            out = jnp.where(e == 2 * i, block, out)
-        wide.append(out.astype(bf16))
+            out = jnp.where(e == jnp.int16(2 * i), block, out)
+        wide.append(out)
     return jnp.concatenate(wide, axis=1)
 
 
@@ -153,8 +163,8 @@
     )
 
 
-def norm_kernel(x_ref, w_ref, n_ref, kv_ref, norms_ref, *, at_kv, at_misc, heads):
-    misc = w_ref[:, at_misc : at_misc + LANES].astype(f32).T
+def norm_kernel(x_ref, w_ref, n_ref, kv_ref, norms_ref, *, heads):
+    misc = w_ref[:, -LANES:].astype(f32).T
     norms = misc[heads : heads + 8, :]
     norms = jnp.concatenate(
         [norms[0:2] + norms[2:4], norms[4:6] + norms[6:8], jnp.zeros_like(norms[0:4])], axis=0
@@ -163,19 +173,19 @@
     normed, _ = normed_parts(x_ref[0].astype(f32))
     low = (normed * norms[0:1] + norms[2:3]).astype(bf16)
     n_ref[0] = low
-    kv_ref[0] = dot(low, w_ref[:, at_kv : at_kv + LANES]).astype(bf16)
+    kv_ref[0] = dot(low, w_ref[:, : kv_ref.shape[2]]).astype(bf16)
 
 
 def query_kernel(
-    n_ref, w_ref, routes_ref, routes_t_ref, q_ref, gate_ref, gate_t_ref, *, at_misc, heads, slots, hs
+    n_ref, w_ref, few_ref, routes_ref, routes_t_ref, q_ref, gate_ref, gate_t_ref, *, heads, slots, hs
 ):
     low = n_ref[0]
     head_pairs = heads // 2
-    queries = dot(low, w_ref[:, : heads * hs]) * (hs**-0.5 * LOG2E)
+    queries = dot(low, w_ref[...]) * (hs**-0.5 * LOG2E)
     experts = slot_experts(routes_ref[0], slots // 2)
     found = compact(lambda i: queries[:, i * LANES : (i + 1) * LANES], experts, head_pairs)
-    q_ref[0] = jnp.concatenate([f.astype(bf16) for f in found], axis=1)
-    logits = dot(low, w_ref[:, at_misc : at_misc + LANES]).T[:heads, :]
+    q_ref[0] = jnp.concatenate(found, axis=1)
+    logits = dot(low, few_ref[:, -LANES:]).T[:heads, :]
     expert = lax.broadcasted_iota(jnp.int32, logits.shape, 0)
     routes_t = routes_t_ref[0]
     picked = [
@@ -314,8 +324,8 @@
 
 
 def forward_kernel(
-    gc_ref, routes_ref, x_ref, og_ref, wo_ref, ff_ref, norms_ref,
-    gated_ref, mid_ref, out_ref, back_ref, sum_ref, n2t, ogt, hid, gbef,
+    moved, gc_ref, routes_ref, x_ref, og_ref, wo_ref, ff_ref, norms_ref,
+    gated_ref, mid_ref, out_ref, far_ref, back_ref, sum_ref, n2t, ogt, hid, gbef,
     *, heads, slots, width, blocks,
 ):
     step = pl.program_id(0)
@@ -355,6 +365,10 @@
         out_ref[0] = out.astype(bf16)
         back_ref[0] = back
 
+        @pl.when(step == moved[0])
+        def _():
+            far_ref[...] = out.astype(bf16)
+
     @pl.when(step >= blocks)
     def _():
         c = step - blocks
@@ -382,6 +396,11 @@
     def _():
         total = sum(dot(gbrt[b], gated_ref[b]) for b in range(blocks))
         split_core(total, core[0], per, send_ref, keep_ref)
+
+        @pl.when(step == blocks)
+        def _():
+            held = jnp.sum(wo_ref[:, heads * hs :].astype(f32), axis=0, keepdims=True)
+            sums_ref[2:3, :LANES] = held * (1.0 / per)
 
 
 def branch_back_block(
@@ -406,6 +425,7 @@
     gbrt[step] = gbr.T
     wide = dot(gbr, wo_ref[:, : heads * hs])
     found = compact(lambda i: wide[:, i * LANES : (i + 1) * LANES], experts, head_pairs)
+    found = [f.astype(f32) for f in found]
     gate = gate_ref[0]
     shape = (tokens, LANES)
     attended, products = [], []
@@ -451,17 +471,22 @@
 
 
 def input_kernel(
-    wide_ref, glog_ref, dkv_ref, w_ref, x_ref, n_ref, gm_ref, norms_ref, sums_ref,
-    ig_ref, small_ref, acck, accr, sums, *, at_kv, at_misc, heads,
+    core, wide_ref, glog_ref, dkv_ref, w_ref, few_ref, x_ref, n_ref, gm_ref, norms_ref, sums_ref,
+    ig_ref, far_ref, send_ref, keep_ref, acck, accr, sums, *, heads, per,
 ):
     dkv, glog = dkv_ref[0], glog_ref[0]
     dn = (
-        dot(wide_ref[0], w_ref[:, :at_kv], NT)
-        + dot(dkv, w_ref[:, at_kv:at_misc], NT)
-        + dot(glog, w_ref[:, at_misc : at_misc + LANES], NT)
+        dot(wide_ref[0], w_ref[...], NT)
+        + dot(dkv, few_ref[:, : dkv.shape[1]], NT)
+        + dot(glog, few_ref[:, -LANES:], NT)
     )
     vhat, rstd = normed_parts(x_ref[0].astype(f32))
-    ig_ref[0] = gm_ref[0] + norm_back(dn, vhat, rstd, norms_ref[0:1, :])
+    ig = gm_ref[0] + norm_back(dn, vhat, rstd, norms_ref[0:1, :])
+    ig_ref[0] = ig
+
+    @pl.when(pl.program_id(0) == core[1])
+    def _():
+        far_ref[...] = ig.astype(bf16)
 
     @pl.when(pl.program_id(0) == 0)
     def _():
@@ -487,8 +512,8 @@
             ],
             axis=0,
         )
-        small_ref[:, :LANES] = acck[...].astype(bf16)
-        small_ref[:, LANES:] = (accr[...] + rows.T).astype(bf16)
+        small = jnp.concatenate([acck[...], accr[...] + rows.T], axis=1)
+        split_core(small, core[0], per, send_ref, keep_ref)
 
 
 def fixed(shape):
@@ -523,7 +548,6 @@
     place = lax.axis_index("mp")
     wide = heads * hs
     slim = slots * hs
-    at_kv, at_misc = wide, wide + 2 * hs
 
     def two(v):
         high = lax.reduce_precision(v, 8, 7)
@@ -555,10 +579,11 @@
     held = jnp.broadcast_to(held.astype(bf16), (w_output.shape[0], LANES))
     first_y = gather_bits(first, "mp", y_bit, depth - 1)
     proj = far_stage(after(jnp.concatenate([w_output, held], axis=1), first), first_y)
-    first_x = gather_bits(first_y, "dp", near_group, depth - 1)
-    first = gather_bits(first_x, "mp", core_bit, depth + 1)
-    proj = gather_bits(after(proj, first_y), "mp", y_bit, depth - 1, first)
-    weights = first.reshape(model, at_misc + LANES)
+    few = gather_bits(first_y[..., wide:], "dp", near_group, depth - 1)
+    many = after(first_y[..., :wide], few)
+    few = gather_bits(few, "mp", core_bit, depth + 1).reshape(model, 2 * hs + LANES)
+    first_x = few
+    proj = gather_bits(after(proj, first_y), "mp", y_bit, depth - 1, few)
 
     single = jnp.argmax(segment_ids[:, -1] == 0).astype(jnp.int32)
 
@@ -579,7 +604,7 @@
     x = blocked(swapped(tokens))
     picks = blocked(swapped(routes, first_y, first_x))
     picks_t = jnp.swapaxes(picks, 1, 2)
-    segments = after(segment_ids, first_x)
+    segments = after(segment_ids, first_y)
     near, far = 2 * place, 2 * (peers - 1 - place) + 1
     one = jnp.arange(rows, dtype=jnp.int32) == single
     last = jnp.stack(
@@ -603,9 +628,9 @@
     start = start.astype(jnp.int32).reshape(blocks, 1, chunk)
 
     n1, kv, norms = pl.pallas_call(
-        functools.partial(norm_kernel, at_kv=at_kv, at_misc=at_misc, heads=heads),
+        functools.partial(norm_kernel, heads=heads),
         grid=(blocks,),
-        in_specs=[per_block(chunk, model), fixed(weights.shape)],
+        in_specs=[per_block(chunk, model), fixed(few.shape)],
         out_specs=[per_block(chunk, model), per_block(chunk, 2 * hs), fixed((8, model))],
         out_shape=[
             like((blocks, chunk, model), bf16),
@@ -614,16 +639,18 @@
         ],
         cost_estimate=cost(2 * count * model * LANES, 4 * MIB),
         name="norm_one",
-    )(x, weights)
-    kv_half = gather_bits(kv, "mp", y_bit, 0)
+    )(x, few)
+    many = gather_bits(many, "dp", near_group, depth - 1, kv)
+    weights = gather_bits(many, "mp", core_bit, depth + 1).reshape(model, wide)
+    kv_half = gather_bits(kv, "mp", y_bit, 0, weights)
     kv_all = gather_bits(kv_half, "mp", core_bit, 1).reshape(peers * blocks, chunk, 2 * hs)
-    proj = gather_bits(after(proj, weights), "dp", near_group, depth - 1, kv_half)
 
     q, gate, gate_t = pl.pallas_call(
-        functools.partial(query_kernel, at_misc=at_misc, heads=heads, slots=slots, hs=hs),
+        functools.partial(query_kernel, heads=heads, slots=slots, hs=hs),
         grid=(blocks,),
         in_specs=[
-            per_block(chunk, model), fixed(weights.shape), per_block(chunk, slots), per_block(slots, chunk),
+            per_block(chunk, model), fixed(weights.shape), fixed(few.shape),
+            per_block(chunk, slots), per_block(slots, chunk),
         ],
         out_specs=[per_block(chunk, slim), per_block(chunk, LANES), per_block(slots, chunk)],
         out_shape=[
@@ -634,8 +661,9 @@
         compiler_params=pltpu.CompilerParams(vmem_limit_bytes=24 * MIB),
         cost_estimate=cost(2 * count * model * wide * 2, 6 * MIB),
         name="queries",
-    )(n1, weights, picks, picks_t)
-
+    )(after(n1, kv_half), weights, few, picks, picks_t)
+
+    proj = gather_bits(after(proj, many), "dp", near_group, depth - 1, q)
     attention = dict(slots=slots, hs=hs, rows=rows, peers=peers)
     total = peers * blocks
     gc, lse = pl.pallas_call(
@@ -663,8 +691,10 @@
     )(plan, q, kv_all, start, gate_t)
 
     proj = gather_bits(proj, "mp", core_bit, depth + 1, gc).reshape(model, wide + LANES)
-    grads = blocked(swapped(out_grad, kv_half, gc))
+    grads = blocked(swapped(out_grad, q, gc))
     core = (place & 1).astype(jnp.int32)[None]
+    moved = 2 * single[None] + 1
+    core_moved = jnp.concatenate([core, moved])
     pair = peers // 2
     per = w_query.shape[0]
 
@@ -675,34 +705,39 @@
         return pl.BlockSpec(shape, lambda b, *_: (0,) * len(shape), pipeline_mode=pl.Buffered(1))
 
     feed_shape = (lax.axis_size("dp"), 2 * w_up.shape[0], width)
-    gated, mid, outs, back, feed_sum = pl.pallas_call(
+    gated, mid, outs, outs_far, back, feed_sum = pl.pallas_call(
         functools.partial(forward_kernel, heads=heads, slots=slots, width=width, blocks=blocks),
-        grid=(blocks + peers,),
-        in_specs=[
-            early(chunk, slim), early(chunk, slots), early(chunk, model), early(chunk, model),
-            once(proj.shape), once(feed.shape), once(norms.shape),
-        ],
-        out_specs=[
-            early(chunk, wide), early(chunk, model), early(chunk, model), early(chunk, model),
-            pl.BlockSpec((1, *feed_shape), lambda b: (jnp.maximum(b - blocks, 0), 0, 0, 0)),
-        ],
-        scratch_shapes=[
-            pltpu.VMEM((blocks, model, chunk), bf16),
-            pltpu.VMEM((blocks, model, chunk), bf16),
-            pltpu.VMEM((peers, blocks, chunk, width), bf16),
-            pltpu.VMEM((peers, blocks, chunk, width), bf16),
-        ],
+        grid_spec=pltpu.PrefetchScalarGridSpec(
+            num_scalar_prefetch=1,
+            grid=(blocks + peers,),
+            in_specs=[
+                early(chunk, slim), early(chunk, slots), early(chunk, model), early(chunk, model),
+                once(proj.shape), once(feed.shape), once(norms.shape),
+            ],
+            out_specs=[
+                early(chunk, wide), early(chunk, model), early(chunk, model), fixed((chunk, model)),
+                early(chunk, model),
+                pl.BlockSpec((1, *feed_shape), lambda b, *_: (jnp.maximum(b - blocks, 0), 0, 0, 0)),
+            ],
+            scratch_shapes=[
+                pltpu.VMEM((blocks, model, chunk), bf16),
+                pltpu.VMEM((blocks, model, chunk), bf16),
+                pltpu.VMEM((peers, blocks, chunk, width), bf16),
+                pltpu.VMEM((peers, blocks, chunk, width), bf16),
+            ],
+        ),
         out_shape=[
             like((blocks, chunk, wide), bf16),
             like((blocks, chunk, model), f32),
             like((blocks, chunk, model), bf16),
+            like((chunk, model), bf16),
             like((blocks, chunk, model), f32),
             like((peers, *feed_shape), bf16),
         ],
         compiler_params=pltpu.CompilerParams(vmem_limit_bytes=60 * MIB),
         cost_estimate=cost(24e9, 24 * MIB),
         name="forward",
-    )(gc, picks, x, grads, proj, feed, norms)
+    )(moved, gc, picks, x, grads, proj, feed, norms)
 
     part, parts = model, wide // model
 
@@ -795,7 +830,10 @@
         name="attend_back",
     )(plan, q, gatt, kv_all, start, lse, delta)
 
-    outputs = swapped(outs, gatt, dq).reshape(rows, local, model)
+    feed_near = scatter_start(feed_part, "dp", near_group, depth - 1)
+    dkv = across(dkv_send, dkv_keep, None).reshape(pair, blocks * chunk, 2 * hs)
+    dkv_y = scatter_start(dkv, "mp", y_bit, 0)
+    dq = after(dq, *feed_near[2], *dkv_y[2])
     wq_send, wq_keep, spread = pl.pallas_call(
         functools.partial(query_weights_kernel, heads=heads, slots=slots, per=per),
         grid_spec=pltpu.PrefetchScalarGridSpec(
@@ -812,54 +850,82 @@
             like((model // 2, wide), bf16),
             like((blocks, chunk, wide), bf16),
         ],
-        compiler_params=pltpu.CompilerParams(vmem_limit_bytes=28 * MIB),
+        compiler_params=pltpu.CompilerParams(vmem_limit_bytes=60 * MIB),
         cost_estimate=cost(4e9, 10 * MIB),
         name="query_weights",
     )(core, dq, picks, n1)
-    feed_part = low_bits(after(feed_part, dq), "dp", near_group, depth - 1, wq_send)
-    out_part = across(out_send, out_keep, dq).reshape(*groups, 2, per, wide)
-    out_part = low_bits(out_part, "mp", y_bit, depth, wq_send)
-    dkv = across(dkv_send, dkv_keep, wq_send).reshape(pair, blocks * chunk, 2 * hs)
-    dkv = low_bits(dkv, "mp", y_bit, 0).reshape(blocks, chunk, 2 * hs)
+    feed_part = scatter_end(feed_near, wq_send).astype(bf16)
+    out_part = across(out_send, out_keep, wq_send).reshape(*groups, 2, per, wide)
+    out_near = scatter_start(out_part, "dp", near_group, depth - 1)
+    dkv = scatter_end(dkv_y, wq_send).astype(bf16).reshape(blocks, chunk, 2 * hs)
     query_part = across(wq_send, wq_keep, None).reshape(*groups, 2, per, wide)
-
-    ig, small = pl.pallas_call(
-        functools.partial(input_kernel, at_kv=at_kv, at_misc=at_misc, heads=heads),
-        grid=(blocks,),
-        in_specs=[
-            per_block(chunk, wide), per_block(chunk, LANES), per_block(chunk, 2 * hs),
-            fixed(weights.shape), per_block(chunk, model), per_block(chunk, model),
-            per_block(chunk, model), fixed((8, model)), fixed((8, model)),
+    query_y = scatter_start(query_part, "mp", y_bit, depth)
+    far_low, far_count = near_group[1], bits_of("dp") - near_group[1]
+    feed_part = feed_part.reshape(*(2,) * far_count, *feed_shape[1:])
+    feed_top = scatter_start(feed_part, "dp", (far_low + far_count - 1, 1), 0)
+    spread = after(spread, *feed_top[2], *query_y[2], *out_near[2])
+
+    ig, ig_far, small_send, small_keep = pl.pallas_call(
+        functools.partial(input_kernel, heads=heads, per=per),
+        grid_spec=pltpu.PrefetchScalarGridSpec(
+            num_scalar_prefetch=1,
+            grid=(blocks,),
+            in_specs=[
+                per_block(chunk, wide), per_block(chunk, LANES), per_block(chunk, 2 * hs),
+                fixed(weights.shape), fixed(few.shape), per_block(chunk, model), per_block(chunk, model),
+                per_block(chunk, model), fixed((8, model)), fixed((8, model)),
+            ],
+            out_specs=[
+                per_block(chunk, model), fixed((chunk, model)),
+                fixed((model // 2, 2 * LANES)), fixed((model // 2, 2 * LANES)),
+            ],
+            scratch_shapes=[
+                pltpu.VMEM((model, 2 * hs), f32), pltpu.VMEM((model, LANES), f32), pltpu.VMEM((8, model), f32),
+            ],
+        ),
+        out_shape=[
+            like((blocks, chunk, model), f32),
+            like((chunk, model), bf16),
+            like((model // 2, 2 * LANES), bf16),
+            like((model // 2, 2 * LANES), bf16),
         ],
-        out_specs=[per_block(chunk, model), fixed((model, 2 * LANES))],
-        out_shape=[like((blocks, chunk, model), f32), like((model, 2 * LANES), bf16)],
-        scratch_shapes=[
-            pltpu.VMEM((model, 2 * hs), f32), pltpu.VMEM((model, LANES), f32), pltpu.VMEM((8, model), f32),
-        ],
-        compiler_params=pltpu.CompilerParams(vmem_limit_bytes=28 * MIB),
+        compiler_params=pltpu.CompilerParams(vmem_limit_bytes=60 * MIB),
         cost_estimate=cost(4e9, 12 * MIB),
         name="inputs_back",
-    )(after(spread, query_part), glog, dkv, weights, x, n1, gm, norms, sums)
-
-    feed_grad = far_scatter(feed_part, ig)
-    query_part = low_bits(query_part, "mp", y_bit, depth, ig)
-    joint = jnp.concatenate([query_part, out_part], axis=-1)
-    joint = low_bits(joint, "dp", near_group, depth - 1)
-    tiles = after(small, query_part).reshape(model // per, per, 2 * LANES)
-    tiles = lax.all_to_all(tiles, ("dp", "mp"), split_axis=0, concat_axis=0, tiled=True)
-    smalls = jnp.sum(tiles.astype(f32), axis=0)
+    )(core_moved, spread, glog, dkv, weights, few, x, n1, gm, norms, sums)
+
+    query_part = scatter_end(query_y, ig).astype(bf16)
+    query_x = scatter_start(query_part, "dp", near_group, depth - 1)
+    small = across(small_send, small_keep, None).reshape(*groups, 2, per, 2 * LANES)
+    out_part = scatter_end(out_near, ig).astype(bf16)
+    out_y = scatter_start(out_part, "mp", y_bit, depth - 1)
+    query_part = scatter_end(query_x)
+    small_y = scatter_start(after(small, query_part), "mp", y_bit, depth)
+    feed_grad = scatter_end(feed_top, small_y[2][0])
+    for bit in reversed(range(far_low, far_low + far_count - 1)):
+        feed_grad = scatter_bits(feed_grad.astype(bf16), "dp", (bit, 1), 0)
+    small = scatter_end(small_y).astype(bf16)
+    small = low_bits(small, "dp", near_group, depth - 1)
+    joint = [query_part, scatter_end(out_y), small.astype(f32)]
+    joint = far_scatter(jnp.concatenate(joint, axis=-1).astype(bf16))
     up_rows = w_up.shape[0]
-    joint = far_scatter(joint)
-    input_grad = swapped(ig).reshape(rows, local, model)
-    tallies = jnp.sum(proj.reshape(-1, per, wide + LANES)[:, 0, wide:].astype(f32), axis=0)
-    counts = tallies[:heads] + tallies[heads : 2 * heads]
+    smalls = joint[:, 2 * wide :]
+    def returned(a, piece):
+        piece = flip(piece, "mp", peers - 1).astype(a.dtype)
+        a = a.reshape(rows, 2, chunk, model)
+        a = lax.dynamic_update_slice(a, piece[None, None], (single, 1, 0, 0))
+        return a.reshape(rows, local, model)
+
+    outs_far, ig_far = (after(a, small_y[2][0]) for a in (outs_far, ig_far))
+    outputs, input_grad = returned(outs, outs_far), returned(ig, ig_far)
+    counts = sums[2, :heads] + sums[2, heads : 2 * heads]
     return (
         outputs,
         input_grad,
         counts,
         joint[:, :wide],
         smalls[:, : 2 * hs],
-        joint[:, wide:],
+        joint[:, wide : 2 * wide],
         smalls[:, LANES : LANES + heads],
         smalls[:, LANES + heads : LANES + heads + 2],
         smalls[:, LANES + heads + 2 : LANES + heads + 4],

time: 278 us -> 245 us (0.88)
  waiting for transfers between devices: 70.1 us -> 34.7 us
  local copies, waits for them, and re-layouts: 22.2 us -> 15.5 us
  starting transfers between devices: 44.6 us -> 49.7 us
  other arithmetic: 14.8 us -> 18.1 us
    ppermute x33 -> x38, waiting for transfers between devices: 65.6 us -> 34.7 us  [flip(): lax.ppermute(x, axis, [(i, i ^ mask) for i in range(lax.axis_size(axis))])]
    ppermute x33 -> x38, starting transfers between devices: 40.1 us -> 49.6 us  [flip(): lax.ppermute(x, axis, [(i, i ^ mask) for i in range(lax.axis_size(axis))])]
    unnamed x93 -> x67, local copies, waits for them, and re-layouts: 11.6 us -> 6.79 us
    all_to_all x1 -> x0, waiting for transfers between devices: 4.37 us -> none  [shards(): lax.all_to_all(tiles, ('dp', 'mp'), split_axis=0, concat_axis=0, tiled=True)]
    all_to_all x1 -> x0, starting transfers between devices: 4.35 us -> none  [shards(): lax.all_to_all(tiles, ('dp', 'mp'), split_axis=0, concat_axis=0, tiled=True)]
    convert_element_type x0 -> x6, other arithmetic: none -> 3.08 us  [the longest x1 1.71 us: shards(): scatter_end(dkv_y, wq_send).astype(bf16).reshape(blocks, chunk, 2 * hs)]
    select_n x10 -> x12, other arithmetic: 6.73 us -> 5.94 us  [gather_bits(): jnp.where(odd, pieces[k + 1], pieces[k])]
  transfers between devices with their start and end apart: 36 -> 40, of which waited for: 16 -> 12; matrix products, arithmetic and copies ran while one was open for 9% -> 11% of each run, Pallas kernels for 28% -> 32%
where the time goes in v3:
time: 245 us; the launch traced here: 243 us
  Pallas kernels  106 us (43%)
  starting transfers between devices  49.7 us (20%)
  waiting for transfers between devices  34.7 us (14%)
  between operations  18.9 us (8%)
  other arithmetic  18.1 us (7%)
  local copies, waits for them, and re-layouts  15.5 us (6%)
    ppermute x38, starting transfers between devices, flip(): lax.ppermute(x, axis, [(i, i ^ mask) for i in range(lax.axis_size(axis))])  49.6 us
    ppermute x38, waiting for transfers between devices, flip(): lax.ppermute(x, axis, [(i, i ^ mask) for i in range(lax.axis_size(axis))])  34.7 us
    pallas_call x1, Pallas kernels, shards(): pl.pallas_call(functools.partial(forward_kernel, heads=heads, slots=slots...  28 us
    pallas_call x1, Pallas kernels, shards(): pl.pallas_call(functools.partial(attend_back_kernel, **attention), grid_s...  21.3 us
    pallas_call x1, Pallas kernels, shards(): pl.pallas_call(functools.partial(branch_back_kernel, heads=heads, slots=s...  17.3 us
    pallas_call x1, Pallas kernels, shards(): pl.pallas_call(functools.partial(attend_kernel, **attention), grid_spec=p...  12 us
    pallas_call x1, Pallas kernels, shards(): pl.pallas_call(functools.partial(input_kernel, heads=heads, per=per), gri...  9.36 us
    pallas_call x1, Pallas kernels, shards(): pl.pallas_call(functools.partial(query_weights_kernel, heads=heads, slots...  9.3 us
  transfers between devices with their start and end apart: 40, of which 12 were waited for; matrix products, arithmetic and copies ran while one was open for 11% of the time, Pallas kernels for 32%

profile of v3, /device:TPU:0, one launch (start us, length us, event | category | flops | bytes accessed | tf_op | source)
XLA Modules:
  0.0 242.9 jit_solution(9533978024747747778)
XLA Ops:
  10.3 3.0 %collective-permute-start.2 = (bf16[16,1792]{1,0:T(8,128)(2,1)S(1)}, bf16[16,1792]{1,0:T(8,128)(2,1)S(1)}, u32[]{:S(2)}, u32[]{:S(2)}) collective-permute-start(bf16[16,1792]{1,0:T(8,128)(2,1)S(1)} %concatenate.23), channel_id=1, source_target_pairs={{0,8},{4,12},{8,0},{12,4},{16,24},{20,28},{24,16},{28,20},{1,9},{5... | collective-permute-start | bytes 172040 | tf_op jit(solution)/shard_map/ppermute | solution.py:40
  13.3 2.6 %collective-permute-start.1 = (bf16[16,1792]{1,0:T(8,128)(2,1)S(1)}, bf16[16,1792]{1,0:T(8,128)(2,1)S(1)}, u32[]{:S(2)}, u32[]{:S(2)}) collective-permute-start(bf16[16,1792]{1,0:T(8,128)(2,1)S(1)} %concatenate.23), channel_id=1, source_target_pairs={{0,16},{4,20},{8,24},{12,28},{16,0},{20,4},{24,8},{28,12},{1,17},{... | collective-permute-start | bytes 172040 | tf_op jit(solution)/shard_map/ppermute | solution.py:40
  24.7 3.6 %collective-permute-start.15 = (bf16[16,1664]{1,0:T(8,128)(2,1)S(1)}, bf16[16,1664]{1,0:T(8,128)(2,1)S(1)}, u32[]{:S(2)}, u32[]{:S(2)}) collective-permute-start(bf16[16,1664]{1,0:T(8,128)(2,1)S(1)} %pad_maximum_fusion.2), channel_id=1, source_target_pairs={{0,24},{4,28},{8,16},{12,20},{16,8},{20,12},{24,0},{28,4},{1,25},{... | collective-permute-start | bytes 159752 | tf_op jit(solution)/shard_map/ppermute | solution.py:40
  30.6 6.8 %collective-permute-done.3 = bf16[4,16,1792]{2,1,0:T(8,128)(2,1)S(1)} collective-permute-done((bf16[4,16,1792]{2,1,0:T(8,128)(2,1)S(1)}, bf16[4,16,1792]{2,1,0:T(8,128)(2,1)S(1)}, u32[]{:S(2)}, u32[]{:S(2)}) %collective-permute-start.3) | collective-permute-done | bytes 229408 | tf_op jit(solution)/shard_map/ppermute | solution.py:40
  39.9 2.0 collective-permute-done.5
  47.1 4.1 %norm_one.1 = (bf16[4,256,512]{2,1,0:T(8,128)(2,1)}, bf16[4,256,128]{2,1,0:T(8,128)(2,1)}, f32[8,512]{1,0:T(8,128)}) custom-call(bf16[4,256,512]{2,1,0:T(8,128)(2,1)} %bitcast.138, bf16[512,256]{1,0:T(8,128)(2,1)} %bitcast_select_fusion.3.w_ref.few_ref), custom_call_target="tpu_custom_call" | custom-call | flops 134217728 | bytes 4194304 | tf_op jit(solution)/shard_map/norm_one/pallas_call | solution.py:630
  51.2 4.3 %collective-permute-done.8 = bf16[4,2,16,1536]{3,2,1,0:T(8,128)(2,1)S(1)} collective-permute-done((bf16[4,2,16,1536]{3,2,1,0:T(8,128)(2,1)S(1)}, bf16[4,2,16,1536]{3,2,1,0:T(8,128)(2,1)S(1)}, u32[]{:S(2)}, u32[]{:S(2)}) %collective-permute-start.8) | collective-permute-done | bytes 393248 | tf_op jit(solution)/shard_map/ppermute | solution.py:40
  56.9 1.7 collective-permute-start.17
  60.1 5.4 %collective-permute-done.7 = bf16[4,256,128]{2,1,0:T(8,128)(2,1)} collective-permute-done((bf16[4,256,128]{2,1,0:T(8,128)(2,1)}, bf16[4,256,128]{2,1,0:T(8,128)(2,1)}, u32[]{:S(2)}, u32[]{:S(2)}) %collective-permute-start.7) | collective-permute-done | bytes 262176 | tf_op jit(solution)/shard_map/ppermute | solution.py:40
  66.7 4.6 %queries.1 = (bf16[4,256,512]{2,1,0:T(8,128)(2,1)S(1)}, f32[4,256,128]{2,1,0:T(8,128)S(1)}, f32[4,8,256]{2,1,0:T(8,128)S(1)}) custom-call(bf16[4,256,512]{2,1,0:T(8,128)(2,1)S(1)} %copy-done.3, bf16[512,1536]{1,0:T(8,128)(2,1)S(1)} %bitcast_select_fusion.1.w_ref, bf16[512,256]{1,0:T(8,128)(2,1)S(1)} %copy-done.2, s32[4,256,8]{2,1,0:T(8,128)S(1)} %bitcast.132, ...), custom_call_target="tpu_custom_call" | custom-call | flops 3221225472 | bytes 6291456 | tf_op jit(solution)/shard_map/queries/pallas_call | solution.py:648
  72.2 2.1 collective-permute-start.18
  74.5 12.0 %attend.1 = (bf16[4,256,512]{2,1,0:T(8,128)(2,1)S(1)}, f32[4,8,256]{2,1,0:T(8,128)S(1)}) custom-call(s32[18]{0:T(128)S(1)} %pad_add_fusion.2.plan, bf16[4,256,512]{2,1,0:T(8,128)(2,1)S(1)} %get-tuple-element.83.q_ref, bf16[16,256,128]{2,1,0:T(8,128)(2,1)S(1)} %bitcast_select_fusion.2.kv_ref, s32[4,1,256]{2,1,0:T(1,128)S(1)} %reshape.275.start_ref, ...), custom_call_target="tpu_custom_call" | custom-call | flops 12000000000 | bytes 4194304 | tf_op jit(solution)/shard_map/attend/pallas_call | solution.py:669
  89.2 28.0 %forward.1 = (bf16[4,256,1536]{2,1,0:T(8,128)(2,1)}, f32[4,256,512]{2,1,0:T(8,128)}, bf16[4,256,512]{2,1,0:T(8,128)(2,1)}, bf16[256,512]{1,0:T(8,128)(2,1)}, f32...) custom-call(s32[1]{0:T(128)S(6)} %add.158.moved, bf16[4,256,512]{2,1,0:T(8,128)(2,1)} %copy-done.8, ...), custom_call_target="tpu_custom_call" | custom-call | flops 24000000000 | bytes 25165824 | tf_op jit(solution)/shard_map/forward/pallas_call | solution.py:708
  117.2 17.3 %branch_back.1 = (f32[4,256,512]{2,1,0:T(8,128)}, bf16[4,256,512]{2,1,0:T(8,128)(2,1)}, f32[4,8,256]{2,1,0:T(8,128)}, bf16[4,256,128]{2,1,0:T(8,128)(2,1)}, f32[...) custom-call(s32[1]{0:T(128)} %bitcast.7.core, f32[4,256,512]{2,1,0:T(8,128)} %get-tuple-element.101.back_ref, ...), custom_call_target="tpu_custom_call" | custom-call | flops 8000000000 | bytes 14680064 | tf_op jit(solution)/shard_map/branch_back/pallas_call | solution.py:747
  136.4 21.3 %attend_back.1 = (bf16[4,256,512]{2,1,0:T(8,128)(2,1)S(1)}, bf16[8,256,128]{2,1,0:T(8,128)(2,1)S(1)}, bf16[8,256,128]{2,1,0:T(8,128)(2,1)S(1)}) custom-call(s32[18]{0:T(128)S(1)} %pad_add_fusion.2.plan, bf16[4,256,512]{2,1,0:T(8,128)(2,1)S(1)} %copy-done.5, bf16[4,256,512]{2,1,0:T(8,128)(2,1)S(1)} %copy-done.9, ...), custom_call_target="tpu_custom_call" | custom-call | flops 24999999488 | bytes 6291456 | tf_op jit(solution)/shard_map/attend_back/pallas_call | solution.py:806
  158.7 4.6 %collective-permute-start.19 = (bf16[8,256,128]{2,1,0:T(8,128)(2,1)S(1)}, bf16[8,256,128]{2,1,0:T(8,128)(2,1)S(1)}, u32[]{:S(2)}, u32[]{:S(2)}) collective-permute-start(bf16[8,256,128]{2,1,0:T(8,128)(2,1)S(1)} %get-tuple-element.111), channel_id=1, source_target_pairs={{0,1},{1,0},{2,3},{3,2},{4,5},{5,4},{6,7},{7,6},{8,9},{9,8},{10,11... | collective-permute-start | bytes 1572872 | tf_op jit(solution)/shard_map/ppermute | solution.py:40
  166.1 3.3 %collective-permute-start.23 = (bf16[1024,128]{1,0:T(8,128)(2,1)}, bf16[1024,128]{1,0:T(8,128)(2,1)}, u32[]{:S(2)}, u32[]{:S(2)}) collective-permute-start(bf16[1024,128]{1,0:T(8,128)(2,1)} %dynamic-slice_bitcast_fusion.4), channel_id=1, source_target_pairs={{0,2},{1,3},{2,0},{3,1},{4,6},{5,7},{6,4},{7,5},{8,10},{9,11},{10,... | collective-permute-start | bytes 786440 | tf_op jit(solution)/shard_map/ppermute | solution.py:40
  170.5 4.5 %collective-permute-start.20 = (bf16[4,128,512]{2,1,0:T(8,128)(2,1)S(1)}, bf16[4,128,512]{2,1,0:T(8,128)(2,1)S(1)}, u32[]{:S(2)}, u32[]{:S(2)}) collective-permute-start(bf16[4,128,512]{2,1,0:T(8,128)(2,1)S(1)} %dynamic-slice_bitcast_fusion), channel_id=1, source_target_pairs={{0,4},{4,0},{8,12},{12,8},{16,20},{20,16},{24,28},{28,24},{1,5},{5... | collective-permute-start | bytes 1572872 | tf_op jit(solution)/shard_map/ppermute | solution.py:40
  175.0 9.3 %query_weights.1 = (bf16[256,1536]{1,0:T(8,128)(2,1)}, bf16[256,1536]{1,0:T(8,128)(2,1)}, bf16[4,256,1536]{2,1,0:T(8,128)(2,1)}) custom-call(s32[1]{0:T(128)} %bitcast.7.core, bf16[4,256,512]{2,1,0:T(8,128)(2,1)} %copy-done.7, s32[4,256,8]{2,1,0:T(8,128)} %bitcast.135, bf16[4,256,512]{2,1,0:T(8,128)(2,1)} %get-tuple-element.80.n_ref), custom_call_target="tpu_custom_call" | custom-call | flops 4000000000 | bytes 10485760 | tf_op jit(solution)/shard_map/query_weights/pallas_call | solution.py:837
  184.9 1.7 fusion.4
  188.7 9.4 %inputs_back.1 = (f32[4,256,512]{2,1,0:T(8,128)}, bf16[256,512]{1,0:T(8,128)(2,1)}, bf16[256,256]{1,0:T(8,128)(2,1)}, bf16[256,256]{1,0:T(8,128)(2,1)}) custom-call(s32[2]{0:T(128)} %pad_add_fusion.3.core, bf16[4,256,1536]{2,1,0:T(8,128)(2,1)} %get-tuple-element.120.wide_ref, bf16[4,256,128]{2,1,0:T(8,128)(2,1)} %get-tuple-element.121.glog_ref, ...), custom_call_target="tpu_custom_call" | custom-call | flops 4000000000 | bytes 12582912 | tf_op jit(solution)/shard_map/inputs_back/pallas_call | solution.py:868
  198.3 1.8 collective-permute-start.30
  201.2 2.5 %collective-permute-start.26 = (bf16[4,16,1536]{2,1,0:T(8,128)(2,1)S(1)}, bf16[4,16,1536]{2,1,0:T(8,128)(2,1)S(1)}, u32[]{:S(2)}, u32[]{:S(2)}) collective-permute-start(bf16[4,16,1536]{2,1,0:T(8,128)(2,1)S(1)} %dynamic-slice_bitcast_fusion.8), channel_id=1, source_target_pairs={{0,4},{4,0},{8,12},{12,8},{16,20},{20,16},{24,28},{28,24},{1,5},{5... | collective-permute-start | bytes 589832 | tf_op jit(solution)/shard_map/ppermute | solution.py:40
  203.7 1.9 collective-permute-done.30
  205.7 3.3 %collective-permute-done.26 = bf16[4,16,1536]{2,1,0:T(8,128)(2,1)S(1)} collective-permute-done((bf16[4,16,1536]{2,1,0:T(8,128)(2,1)S(1)}, bf16[4,16,1536]{2,1,0:T(8,128)(2,1)S(1)}, u32[]{:S(2)}, u32[]{:S(2)}) %collective-permute-start.26) | collective-permute-done | bytes 196640 | tf_op jit(solution)/shard_map/ppermute | solution.py:40
  211.5 1.9 collective-permute-done.31
  213.4 1.8 collective-permute-start.32
  215.4 1.7 collective-permute-start.28
  217.5 1.8 collective-permute-start.33
  219.3 2.1 collective-permute-start.35
  223.7 3.9 %collective-permute-done.35 = bf16[16,3328]{1,0:T(8,128)(2,1)S(1)} collective-permute-done((bf16[16,3328]{1,0:T(8,128)(2,1)S(1)}, bf16[16,3328]{1,0:T(8,128)(2,1)S(1)}, u32[]{:S(2)}, u32[]{:S(2)}) %collective-permute-start.35) | collective-permute-done | bytes 106528 | tf_op jit(solution)/shard_map/ppermute | solution.py:40
  227.6 3.5 %collective-permute-done.34 = bf16[16,3328]{1,0:T(8,128)(2,1)S(1)} collective-permute-done((bf16[16,3328]{1,0:T(8,128)(2,1)S(1)}, bf16[16,3328]{1,0:T(8,128)(2,1)S(1)}, u32[]{:S(2)}, u32[]{:S(2)}) %collective-permute-start.34) | collective-permute-done | bytes 106528 | tf_op jit(solution)/shard_map/ppermute | solution.py:40
  (229 shorter events, 46.2 us)
Async XLA Ops:
  7.3 81.9 %all-gather.3.cloned.1.call-start = ((), (), s32[]{:S(2)}) async-start(), calls=%async_computation.2 | async-start | bytes 4325376 | tf_op jit(solution)/shard_map/all_gather | solution.py:570
  10.3 14.0 %collective-permute-start.2 = (bf16[16,1792]{1,0:T(8,128)(2,1)S(1)}, bf16[16,1792]{1,0:T(8,128)(2,1)S(1)}, u32[]{:S(2)}, u32[]{:S(2)}) collective-permute-start(bf16[16,1792]{1,0:T(8,128)(2,1)S(1)} %concatenate.23), channel_id=1, source_target_pairs={{0,8},{4,12},{8,0},{12,4},{16,24},{20,28},{24,16},{28,20},{1,9},{5... | collective-permute-start | bytes 172040 | tf_op jit(solution)/shard_map/ppermute | solution.py:40
  13.3 11.0 %collective-permute-start.1 = (bf16[16,1792]{1,0:T(8,128)(2,1)S(1)}, bf16[16,1792]{1,0:T(8,128)(2,1)S(1)}, u32[]{:S(2)}, u32[]{:S(2)}) collective-permute-start(bf16[16,1792]{1,0:T(8,128)(2,1)S(1)} %concatenate.23), channel_id=1, source_target_pairs={{0,16},{4,20},{8,24},{12,28},{16,0},{20,4},{24,8},{28,12},{1,17},{... | collective-permute-start | bytes 172040 | tf_op jit(solution)/shard_map/ppermute | solution.py:40
  15.9 8.4 %collective-permute-start = (bf16[16,1792]{1,0:T(8,128)(2,1)S(1)}, bf16[16,1792]{1,0:T(8,128)(2,1)S(1)}, u32[]{:S(2)}, u32[]{:S(2)}) collective-permute-start(bf16[16,1792]{1,0:T(8,128)(2,1)S(1)} %concatenate.23), channel_id=1, source_target_pairs={{0,24},{4,28},{8,16},{12,20},{16,8},{20,12},{24,0},{28,4},{1,25},{... | collective-permute-start | bytes 172040 | tf_op jit(solution)/shard_map/ppermute | solution.py:40
  16.6 152.8 %reduce-scatter.2.cloned.1.call-start = ((), (), s32[]{:S(2)}) async-start(), calls=%async_computation.1 | async-start | bytes 5242880 | tf_op jit(solution)/shard_map/reduce_scatter | solution.py:803
  19.5 11.1 %collective-permute-start.4 = (bf16[256,512]{1,0:T(8,128)(2,1)S(1)}, bf16[256,512]{1,0:T(8,128)(2,1)S(1)}, u32[]{:S(2)}, u32[]{:S(2)}) collective-permute-start(bf16[256,512]{1,0:T(8,128)(2,1)S(1)} %dynamic-slice_bitcast_fusion.6), channel_id=1, source_target_pairs={{0,3},{1,2},{2,1},{3,0},{4,7},{5,6},{6,5},{7,4},{8,11},{9,10},{10,... | collective-permute-start | bytes 786440 | tf_op jit(solution)/shard_map/ppermute | solution.py:40
  24.7 12.8 %collective-permute-start.15 = (bf16[16,1664]{1,0:T(8,128)(2,1)S(1)}, bf16[16,1664]{1,0:T(8,128)(2,1)S(1)}, u32[]{:S(2)}, u32[]{:S(2)}) collective-permute-start(bf16[16,1664]{1,0:T(8,128)(2,1)S(1)} %pad_maximum_fusion.2), channel_id=1, source_target_pairs={{0,24},{4,28},{8,16},{12,20},{16,8},{20,12},{24,0},{28,4},{1,25},{... | collective-permute-start | bytes 159752 | tf_op jit(solution)/shard_map/ppermute | solution.py:40
  28.3 9.2 %collective-permute-start.14 = (bf16[16,1664]{1,0:T(8,128)(2,1)S(1)}, bf16[16,1664]{1,0:T(8,128)(2,1)S(1)}, u32[]{:S(2)}, u32[]{:S(2)}) collective-permute-start(bf16[16,1664]{1,0:T(8,128)(2,1)S(1)} %pad_maximum_fusion.2), channel_id=1, source_target_pairs={{0,16},{4,20},{8,24},{12,28},{16,0},{20,4},{24,8},{28,12},{1,17},{... | collective-permute-start | bytes 159752 | tf_op jit(solution)/shard_map/ppermute | solution.py:40
  28.3 9.2 %collective-permute-start.13 = (bf16[16,1664]{1,0:T(8,128)(2,1)S(1)}, bf16[16,1664]{1,0:T(8,128)(2,1)S(1)}, u32[]{:S(2)}, u32[]{:S(2)}) collective-permute-start(bf16[16,1664]{1,0:T(8,128)(2,1)S(1)} %pad_maximum_fusion.2), channel_id=1, source_target_pairs={{0,8},{4,12},{8,0},{12,4},{16,24},{20,28},{24,16},{28,20},{1,9},{5... | collective-permute-start | bytes 159752 | tf_op jit(solution)/shard_map/ppermute | solution.py:40
  29.2 8.3 %collective-permute-start.3 = (bf16[4,16,1792]{2,1,0:T(8,128)(2,1)S(1)}, bf16[4,16,1792]{2,1,0:T(8,128)(2,1)S(1)}, u32[]{:S(2)}, u32[]{:S(2)}) collective-permute-start(bf16[4,16,1792]{2,1,0:T(8,128)(2,1)S(1)} %select_select_fusion), channel_id=1, source_target_pairs={{0,2},{1,3},{2,0},{3,1},{4,6},{5,7},{6,4},{7,5},{8,10},{9,11},{10,... | collective-permute-start | bytes 688136 | tf_op jit(solution)/shard_map/ppermute | solution.py:40
  42.0 13.5 %collective-permute-start.8 = (bf16[4,2,16,1536]{3,2,1,0:T(8,128)(2,1)S(1)}, bf16[4,2,16,1536]{3,2,1,0:T(8,128)(2,1)S(1)}, u32[]{:S(2)}, u32[]{:S(2)}) collective-permute-start(bf16[4,2,16,1536]{3,2,1,0:T(8,128)(2,1)S(1)} %slice.93), channel_id=1, source_target_pairs={{0,4},{4,0},{8,12},{12,8},{16,20},{20,16},{24,28},{28,24},{1,5},{5... | collective-permute-start | bytes 1179656 | tf_op jit(solution)/shard_map/ppermute | solution.py:40
  44.0 12.7 %collective-permute-start.16 = (bf16[4,16,1664]{2,1,0:T(8,128)(2,1)S(1)}, bf16[4,16,1664]{2,1,0:T(8,128)(2,1)S(1)}, u32[]{:S(2)}, u32[]{:S(2)}) collective-permute-start(bf16[4,16,1664]{2,1,0:T(8,128)(2,1)S(1)} %select_select_fusion.1), channel_id=1, source_target_pairs={{0,2},{1,3},{2,0},{3,1},{4,6},{5,7},{6,4},{7,5},{8,10},{9,11},{10,... | collective-permute-start | bytes 638984 | tf_op jit(solution)/shard_map/ppermute | solution.py:40
  44.8 11.8 %collective-permute-start.10 = (bf16[256,8]{1,0:T(8,128)(2,1)S(1)}, bf16[256,8]{1,0:T(8,128)(2,1)S(1)}, u32[]{:S(2)}, u32[]{:S(2)}) collective-permute-start(bf16[256,8]{1,0:T(8,128)(2,1)S(1)} %fusion.9), channel_id=1, source_target_pairs={{0,3},{1,2},{2,1},{3,0},{4,7},{5,6},{6,5},{7,4},{8,11},{9,10},{10,... | collective-permute-start | bytes 12296 | tf_op jit(solution)/shard_map/ppermute | solution.py:40
  56.5 9.0 %collective-permute-start.7 = (bf16[4,256,128]{2,1,0:T(8,128)(2,1)}, bf16[4,256,128]{2,1,0:T(8,128)(2,1)}, u32[]{:S(2)}, u32[]{:S(2)}) collective-permute-start(bf16[4,256,128]{2,1,0:T(8,128)(2,1)} %get-tuple-element.76), channel_id=1, source_target_pairs={{0,2},{1,3},{2,0},{3,1},{4,6},{5,7},{6,4},{7,5},{8,10},{9,11},{10,... | collective-permute-start | bytes 786440 | tf_op jit(solution)/shard_map/ppermute | solution.py:40
  56.9 15.1 %collective-permute-start.17 = (bf16[4,2,16,1664]{3,2,1,0:T(8,128)(2,1)S(1)}, bf16[4,2,16,1664]{3,2,1,0:T(8,128)(2,1)S(1)}, u32[]{:S(2)}, u32[]{:S(2)}) collective-permute-start(bf16[4,2,16,1664]{3,2,1,0:T(8,128)(2,1)S(1)} %broadcast_select_fusion.4), channel_id=1, source_target_pairs={{0,4},{4,0},{8,12},{12,8},{16,20},{20,16},{24,28},{28,24},{1,5},{5... | collective-permute-start | bytes 1277960 | tf_op jit(solution)/shard_map/ppermute | solution.py:40
  66.6 7.8 %collective-permute-start.11 = (bf16[2,4,256,128]{3,2,1,0:T(8,128)(2,1)S(1)}, bf16[2,4,256,128]{3,2,1,0:T(8,128)(2,1)S(1)}, u32[]{:S(2)}, u32[]{:S(2)}) collective-permute-start(bf16[2,4,256,128]{3,2,1,0:T(8,128)(2,1)S(1)} %broadcast_select_fusion.2), channel_id=1, source_target_pairs={{0,1},{1,0},{2,3},{3,2},{4,5},{5,4},{6,7},{7,6},{8,9},{9,8},{10,11... | collective-permute-start | bytes 1572872 | tf_op jit(solution)/shard_map/ppermute | solution.py:40
  72.0 14.5 %collective-permute-start.12 = (bf16[256,512]{1,0:T(8,128)(2,1)S(1)}, bf16[256,512]{1,0:T(8,128)(2,1)S(1)}, u32[]{:S(2)}, u32[]{:S(2)}) collective-permute-start(bf16[256,512]{1,0:T(8,128)(2,1)S(1)} %dynamic-slice_bitcast_fusion.5), channel_id=1, source_target_pairs={{0,3},{1,2},{2,1},{3,0},{4,7},{5,6},{6,5},{7,4},{8,11},{9,10},{10,... | collective-permute-start | bytes 786440 | tf_op jit(solution)/shard_map/ppermute | solution.py:40
  72.2 14.4 %collective-permute-start.18 = (bf16[4,2,2,16,1664]{4,3,2,1,0:T(8,128)(2,1)S(1)}, bf16[4,2,2,16,1664]{4,3,2,1,0:T(8,128)(2,1)S(1)}, u32[]{:S(2)}, u32[]{:S(2)}) collective-permute-start(bf16[4,2,2,16,1664]{4,3,2,1,0:T(8,128)(2,1)S(1)} %broadcast_select_fusion), channel_id=1, source_target_pairs={{0,1},{1,0},{2,3},{3,2},{4,5},{5,4},{6,7},{7,6},{8,9},{9,8},{10,11... | collective-permute-start | bytes 2555912 | tf_op jit(solution)/shard_map/ppermute | solution.py:40
  158.7 6.5 %collective-permute-start.19 = (bf16[8,256,128]{2,1,0:T(8,128)(2,1)S(1)}, bf16[8,256,128]{2,1,0:T(8,128)(2,1)S(1)}, u32[]{:S(2)}, u32[]{:S(2)}) collective-permute-start(bf16[8,256,128]{2,1,0:T(8,128)(2,1)S(1)} %get-tuple-element.111), channel_id=1, source_target_pairs={{0,1},{1,0},{2,3},{3,2},{4,5},{5,4},{6,7},{7,6},{8,9},{9,8},{10,11... | collective-permute-start | bytes 1572872 | tf_op jit(solution)/shard_map/ppermute | solution.py:40
  163.9 20.4 %collective-permute-start.22 = (bf16[256,1536]{1,0:T(8,128)(2,1)}, bf16[256,1536]{1,0:T(8,128)(2,1)S(1)}, u32[]{:S(2)}, u32[]{:S(2)}) collective-permute-start(bf16[256,1536]{1,0:T(8,128)(2,1)} %get-tuple-element.118), channel_id=1, source_target_pairs={{0,1},{1,0},{2,3},{3,2},{4,5},{5,4},{6,7},{7,6},{8,9},{9,8},{10,11... | collective-permute-start | bytes 2359304 | tf_op jit(solution)/shard_map/ppermute | solution.py:40
  166.1 18.4 %collective-permute-start.23 = (bf16[1024,128]{1,0:T(8,128)(2,1)}, bf16[1024,128]{1,0:T(8,128)(2,1)}, u32[]{:S(2)}, u32[]{:S(2)}) collective-permute-start(bf16[1024,128]{1,0:T(8,128)(2,1)} %dynamic-slice_bitcast_fusion.4), channel_id=1, source_target_pairs={{0,2},{1,3},{2,0},{3,1},{4,6},{5,7},{6,4},{7,5},{8,10},{9,11},{10,... | collective-permute-start | bytes 786440 | tf_op jit(solution)/shard_map/ppermute | solution.py:40
  170.5 16.8 %collective-permute-start.20 = (bf16[4,128,512]{2,1,0:T(8,128)(2,1)S(1)}, bf16[4,128,512]{2,1,0:T(8,128)(2,1)S(1)}, u32[]{:S(2)}, u32[]{:S(2)}) collective-permute-start(bf16[4,128,512]{2,1,0:T(8,128)(2,1)S(1)} %dynamic-slice_bitcast_fusion), channel_id=1, source_target_pairs={{0,4},{4,0},{8,12},{12,8},{16,20},{20,16},{24,28},{28,24},{1,5},{5... | collective-permute-start | bytes 1572872 | tf_op jit(solution)/shard_map/ppermute | solution.py:40
  184.6 13.5 %collective-permute-start.29 = (bf16[4,2,16,1536]{3,2,1,0:T(8,128)(2,1)S(1)}, bf16[4,2,16,1536]{3,2,1,0:T(8,128)(2,1)S(1)}, u32[]{:S(2)}, u32[]{:S(2)}) collective-permute-start(bf16[4,2,16,1536]{3,2,1,0:T(8,128)(2,1)S(1)} %dynamic-slice_bitcast_fusion.1), channel_id=1, source_target_pairs={{0,4},{4,0},{8,12},{12,8},{16,20},{20,16},{24,28},{28,24},{1,5},{5... | collective-permute-start | bytes 1179656 | tf_op jit(solution)/shard_map/ppermute | solution.py:40
  187.5 23.1 %collective-permute-start.36 = (bf16[2,128,512]{2,1,0:T(8,128)(2,1)S(1)}, bf16[2,128,512]{2,1,0:T(8,128)(2,1)}, u32[]{:S(2)}, u32[]{:S(2)}) collective-permute-start(bf16[2,128,512]{2,1,0:T(8,128)(2,1)S(1)} %dynamic-slice_bitcast_fusion.3), channel_id=1, source_target_pairs={{0,16},{4,20},{8,24},{12,28},{16,0},{20,4},{24,8},{28,12},{1,17},{... | collective-permute-start | bytes 786440 | tf_op jit(solution)/shard_map/ppermute | solution.py:40
  188.3 12.7 %collective-permute-start.25 = (bf16[4,2,16,1536]{3,2,1,0:T(8,128)(2,1)S(1)}, bf16[4,2,16,1536]{3,2,1,0:T(8,128)(2,1)S(1)}, u32[]{:S(2)}, u32[]{:S(2)}) collective-permute-start(bf16[4,2,16,1536]{3,2,1,0:T(8,128)(2,1)S(1)} %dynamic-slice_bitcast_fusion.2), channel_id=1, source_target_pairs={{0,2},{1,3},{2,0},{3,1},{4,6},{5,7},{6,4},{7,5},{8,10},{9,11},{10,... | collective-permute-start | bytes 1179656 | tf_op jit(solution)/shard_map/ppermute | solution.py:40
  198.3 7.4 %collective-permute-start.30 = (bf16[4,16,1536]{2,1,0:T(8,128)(2,1)S(1)}, bf16[4,16,1536]{2,1,0:T(8,128)(2,1)S(1)}, u32[]{:S(2)}, u32[]{:S(2)}) collective-permute-start(bf16[4,16,1536]{2,1,0:T(8,128)(2,1)S(1)} %dynamic-slice_bitcast_fusion.7), channel_id=1, source_target_pairs={{0,2},{1,3},{2,0},{3,1},{4,6},{5,7},{6,4},{7,5},{8,10},{9,11},{10,... | collective-permute-start | bytes 589832 | tf_op jit(solution)/shard_map/ppermute | solution.py:40
  201.2 7.8 %collective-permute-start.26 = (bf16[4,16,1536]{2,1,0:T(8,128)(2,1)S(1)}, bf16[4,16,1536]{2,1,0:T(8,128)(2,1)S(1)}, u32[]{:S(2)}, u32[]{:S(2)}) collective-permute-start(bf16[4,16,1536]{2,1,0:T(8,128)(2,1)S(1)} %dynamic-slice_bitcast_fusion.8), channel_id=1, source_target_pairs={{0,4},{4,0},{8,12},{12,8},{16,20},{20,16},{24,28},{28,24},{1,5},{5... | collective-permute-start | bytes 589832 | tf_op jit(solution)/shard_map/ppermute | solution.py:40
  215.4 19.1 %collective-permute-start.27 = (bf16[256,512]{1,0:T(8,128)(2,1)S(1)}, bf16[256,512]{1,0:T(8,128)(2,1)S(1)}, u32[]{:S(2)}, u32[]{:S(2)}) collective-permute-start(bf16[256,512]{1,0:T(8,128)(2,1)S(1)} %copy-done.30), channel_id=1, source_target_pairs={{0,3},{1,2},{2,1},{3,0},{4,7},{5,6},{6,5},{7,4},{8,11},{9,10},{10,... | collective-permute-start | bytes 786440 | tf_op jit(solution)/shard_map/ppermute | solution.py:40
  215.4 19.7 %collective-permute-start.28 = (bf16[256,512]{1,0:T(8,128)(2,1)S(1)}, bf16[256,512]{1,0:T(8,128)(2,1)S(1)}, u32[]{:S(2)}, u32[]{:S(2)}) collective-permute-start(bf16[256,512]{1,0:T(8,128)(2,1)S(1)} %copy-done.31), channel_id=1, source_target_pairs={{0,3},{1,2},{2,1},{3,0},{4,7},{5,6},{6,5},{7,4},{8,11},{9,10},{10,... | collective-permute-start | bytes 786440 | tf_op jit(solution)/shard_map/ppermute | solution.py:40
  217.5 6.2 %collective-permute-start.33 = (bf16[16,3328]{1,0:T(8,128)(2,1)S(1)}, bf16[16,3328]{1,0:T(8,128)(2,1)S(1)}, u32[]{:S(2)}, u32[]{:S(2)}) collective-permute-start(bf16[16,3328]{1,0:T(8,128)(2,1)S(1)} %get-tuple-element.190), channel_id=1, source_target_pairs={{0,8},{4,12},{8,0},{12,4},{16,24},{20,28},{24,16},{28,20},{1,9},{5... | collective-permute-start | bytes 319496 | tf_op jit(solution)/shard_map/ppermute | solution.py:40
  219.3 8.4 %collective-permute-start.35 = (bf16[16,3328]{1,0:T(8,128)(2,1)S(1)}, bf16[16,3328]{1,0:T(8,128)(2,1)S(1)}, u32[]{:S(2)}, u32[]{:S(2)}) collective-permute-start(bf16[16,3328]{1,0:T(8,128)(2,1)S(1)} %get-tuple-element.191), channel_id=1, source_target_pairs={{0,24},{4,28},{8,16},{12,20},{16,8},{20,12},{24,0},{28,4},{1,25},{... | collective-permute-start | bytes 319496 | tf_op jit(solution)/shard_map/ppermute | solution.py:40
  221.4 9.7 %collective-permute-start.34 = (bf16[16,3328]{1,0:T(8,128)(2,1)S(1)}, bf16[16,3328]{1,0:T(8,128)(2,1)S(1)}, u32[]{:S(2)}, u32[]{:S(2)}) collective-permute-start(bf16[16,3328]{1,0:T(8,128)(2,1)S(1)} %get-tuple-element.192), channel_id=1, source_target_pairs={{0,16},{4,20},{8,24},{12,28},{16,0},{20,4},{24,8},{28,12},{1,17},{... | collective-permute-start | bytes 319496 | tf_op jit(solution)/shard_map/ppermute | solution.py:40
  (40 other events, 245.8 us)
Sparse Core Ops, SparseCore 0:
  16.7 69.0 all-gather.2
  117.3 47.1 reduce-scatter.1

commit v4 on v3

--- a/solution.py
+++ b/solution.py
@@ -89,9 +89,16 @@
     return jnp.where(lane < LANES // 2, row_first, row_second)
 
 
+def slot_lanes(rows, columns, hs):
+    shape = (rows, columns)
+    slot, column = (lax.broadcasted_iota(jnp.int32, shape, i) for i in range(2))
+    return (slot == column // hs).astype(bf16)
+
+
 def slot_experts(routes, pairs):
-    shape = (routes.shape[0], LANES)
-    return [halves(routes[:, 2 * j : 2 * j + 1], routes[:, 2 * j + 1 : 2 * j + 2], shape) for j in range(pairs)]
+    slots = routes.shape[1]
+    spread = dot(routes.astype(bf16), slot_lanes(slots, pairs * LANES, LANES // 2)).astype(jnp.int32)
+    return [spread[:, j * LANES : (j + 1) * LANES] for j in range(pairs)]
 
 
 def turn_half(x):
@@ -427,10 +434,12 @@
     found = compact(lambda i: wide[:, i * LANES : (i + 1) * LANES], experts, head_pairs)
     found = [f.astype(f32) for f in found]
     gate = gate_ref[0]
-    shape = (tokens, LANES)
+    lanes = slot_lanes(LANES, slots * hs, hs)
+    coarse = gate.astype(bf16)
+    wide_gate = dot(coarse, lanes) + dot((gate - coarse.astype(f32)).astype(bf16), lanes)
     attended, products = [], []
     for j in range(pairs):
-        spread = halves(gate[:, 2 * j : 2 * j + 1], gate[:, 2 * j + 1 : 2 * j + 2], shape)
+        spread = wide_gate[:, j * LANES : (j + 1) * LANES]
         attended.append((found[j] * spread).astype(bf16))
         products.append(found[j] * gc_ref[0][:, j * LANES : (j + 1) * LANES].astype(f32))
     gatt_ref[0] = jnp.concatenate(attended, axis=1)
@@ -442,12 +451,11 @@
     inner = dot(coarse, ones) + dot(fine, ones)
     delta_ref[0] = inner.T[:slots, :]
     logit = inner - gate * jnp.sum(inner, axis=1, keepdims=True)
-    lane = lax.broadcasted_iota(jnp.int32, shape, 1)
-    spread_out = jnp.zeros(shape, f32)
-    routes = routes_ref[0]
-    for s in range(slots):
-        spread_out = jnp.where(lane == routes[:, s : s + 1], logit[:, s : s + 1], spread_out)
-    glog_ref[0] = spread_out.astype(bf16)
+    spread_out = dot(logit.astype(bf16), lanes)
+    lane = lax.broadcasted_iota(jnp.int32, spread_out.shape, 1) % hs
+    spread_out = jnp.where(lane == jnp.concatenate(experts, axis=1), spread_out, 0.0).astype(bf16)
+    column, row = (lax.broadcasted_iota(jnp.int32, (slots * hs, LANES), i) for i in (1, 0))
+    glog_ref[0] = dot(spread_out, (row % hs == column).astype(bf16)).astype(bf16)
 
 
 def query_weights_kernel(
@@ -900,32 +908,34 @@
     out_part = scatter_end(out_near, ig).astype(bf16)
     out_y = scatter_start(out_part, "mp", y_bit, depth - 1)
     query_part = scatter_end(query_x)
-    small_y = scatter_start(after(small, query_part), "mp", y_bit, depth)
-    feed_grad = scatter_end(feed_top, small_y[2][0])
+    small_y = scatter_start(small, "mp", y_bit, depth)
+    small = scatter_end(small_y).astype(bf16)
+    out_part = scatter_end(out_y)
+    small = low_bits(after(small, query_part, out_part), "dp", near_group, depth - 1)
+    joint = [query_part, out_part, small.astype(f32)]
+    joint = jnp.concatenate(joint, axis=-1).astype(bf16)
+    feed_grad = scatter_end(feed_top, joint)
     for bit in reversed(range(far_low, far_low + far_count - 1)):
         feed_grad = scatter_bits(feed_grad.astype(bf16), "dp", (bit, 1), 0)
-    small = scatter_end(small_y).astype(bf16)
-    small = low_bits(small, "dp", near_group, depth - 1)
-    joint = [query_part, scatter_end(out_y), small.astype(f32)]
-    joint = far_scatter(jnp.concatenate(joint, axis=-1).astype(bf16))
+    joint_sum = far_scatter(joint)
     up_rows = w_up.shape[0]
-    smalls = joint[:, 2 * wide :]
+    smalls = joint_sum[:, 2 * wide :]
     def returned(a, piece):
         piece = flip(piece, "mp", peers - 1).astype(a.dtype)
         a = a.reshape(rows, 2, chunk, model)
         a = lax.dynamic_update_slice(a, piece[None, None], (single, 1, 0, 0))
         return a.reshape(rows, local, model)
 
-    outs_far, ig_far = (after(a, small_y[2][0]) for a in (outs_far, ig_far))
+    outs_far, ig_far = after(outs_far, small), after(ig_far, small_y[2][0])
     outputs, input_grad = returned(outs, outs_far), returned(ig, ig_far)
     counts = sums[2, :heads] + sums[2, heads : 2 * heads]
     return (
         outputs,
         input_grad,
         counts,
-        joint[:, :wide],
+        joint_sum[:, :wide],
         smalls[:, : 2 * hs],
-        joint[:, wide : 2 * wide],
+        joint_sum[:, wide : 2 * wide],
         smalls[:, LANES : LANES + heads],
         smalls[:, LANES + heads : LANES + heads + 2],
         smalls[:, LANES + heads + 2 : LANES + heads + 4],

time: 245 us -> 244 us (level)
  waiting for transfers between devices: 34.7 us -> 37.8 us
  Pallas kernels: 106 us -> 103 us
    ppermute x38, waiting for transfers between devices: 34.7 us -> 37.8 us  [flip(): lax.ppermute(x, axis, [(i, i ^ mask) for i in range(lax.axis_size(axis))])]
  transfers between devices with their start and end apart: 40 -> 40, of which waited for: 12 -> 14; matrix products, arithmetic and copies ran while one was open for 11% -> 11% of each run, Pallas kernels for 32% -> 32%
where the time goes in v4:
time: 244 us; the launch traced here: 243 us
  Pallas kernels  103 us (42%)
  starting transfers between devices  49.9 us (20%)
  waiting for transfers between devices  37.8 us (15%)
  between operations  18.9 us (8%)
  other arithmetic  17.2 us (7%)
  local copies, waits for them, and re-layouts  16.4 us (7%)
    ppermute x38, starting transfers between devices, flip(): lax.ppermute(x, axis, [(i, i ^ mask) for i in range(lax.axis_size(axis))])  49.8 us
    ppermute x38, waiting for transfers between devices, flip(): lax.ppermute(x, axis, [(i, i ^ mask) for i in range(lax.axis_size(axis))])  37.8 us
    pallas_call x1, Pallas kernels, shards(): pl.pallas_call(functools.partial(forward_kernel, heads=heads, slots=slots...  26.6 us
    pallas_call x1, Pallas kernels, shards(): pl.pallas_call(functools.partial(attend_back_kernel, **attention), grid_s...  21.3 us
    pallas_call x1, Pallas kernels, shards(): pl.pallas_call(functools.partial(branch_back_kernel, heads=heads, slots=s...  16.4 us
    pallas_call x1, Pallas kernels, shards(): pl.pallas_call(functools.partial(attend_kernel, **attention), grid_spec=p...  12 us
    pallas_call x1, Pallas kernels, shards(): pl.pallas_call(functools.partial(input_kernel, heads=heads, per=per), gri...  9.37 us
    pallas_call x1, Pallas kernels, shards(): pl.pallas_call(functools.partial(query_weights_kernel, heads=heads, slots...  8.43 us
  transfers between devices with their start and end apart: 40, of which 14 were waited for; matrix products, arithmetic and copies ran while one was open for 11% of the time, Pallas kernels for 32%

profile of v4, /device:TPU:0, one launch (start us, length us, event | category | flops | bytes accessed | tf_op | source)
XLA Modules:
  0.0 243.5 jit_solution(5599389476897940011)
XLA Ops:
  10.3 3.0 %collective-permute-start.2 = (bf16[16,1792]{1,0:T(8,128)(2,1)S(1)}, bf16[16,1792]{1,0:T(8,128)(2,1)S(1)}, u32[]{:S(2)}, u32[]{:S(2)}) collective-permute-start(bf16[16,1792]{1,0:T(8,128)(2,1)S(1)} %concatenate.23), channel_id=1, source_target_pairs={{0,8},{4,12},{8,0},{12,4},{16,24},{20,28},{24,16},{28,20},{1,9},{5... | collective-permute-start | bytes 172040 | tf_op jit(solution)/shard_map/ppermute | solution.py:40
  13.3 2.6 %collective-permute-start.1 = (bf16[16,1792]{1,0:T(8,128)(2,1)S(1)}, bf16[16,1792]{1,0:T(8,128)(2,1)S(1)}, u32[]{:S(2)}, u32[]{:S(2)}) collective-permute-start(bf16[16,1792]{1,0:T(8,128)(2,1)S(1)} %concatenate.23), channel_id=1, source_target_pairs={{0,16},{4,20},{8,24},{12,28},{16,0},{20,4},{24,8},{28,12},{1,17},{... | collective-permute-start | bytes 172040 | tf_op jit(solution)/shard_map/ppermute | solution.py:40
  24.7 3.6 %collective-permute-start.15 = (bf16[16,1664]{1,0:T(8,128)(2,1)S(1)}, bf16[16,1664]{1,0:T(8,128)(2,1)S(1)}, u32[]{:S(2)}, u32[]{:S(2)}) collective-permute-start(bf16[16,1664]{1,0:T(8,128)(2,1)S(1)} %pad_maximum_fusion.2), channel_id=1, source_target_pairs={{0,24},{4,28},{8,16},{12,20},{16,8},{20,12},{24,0},{28,4},{1,25},{... | collective-permute-start | bytes 159752 | tf_op jit(solution)/shard_map/ppermute | solution.py:40
  30.6 6.8 %collective-permute-done.3 = bf16[4,16,1792]{2,1,0:T(8,128)(2,1)S(1)} collective-permute-done((bf16[4,16,1792]{2,1,0:T(8,128)(2,1)S(1)}, bf16[4,16,1792]{2,1,0:T(8,128)(2,1)S(1)}, u32[]{:S(2)}, u32[]{:S(2)}) %collective-permute-start.3) | collective-permute-done | bytes 229408 | tf_op jit(solution)/shard_map/ppermute | solution.py:40
  37.6 1.6 collective-permute-start.5
  39.9 2.0 collective-permute-done.5
  42.0 1.6 collective-permute-start.8
  47.1 4.1 %norm_one.1 = (bf16[4,256,512]{2,1,0:T(8,128)(2,1)}, bf16[4,256,128]{2,1,0:T(8,128)(2,1)}, f32[8,512]{1,0:T(8,128)}) custom-call(bf16[4,256,512]{2,1,0:T(8,128)(2,1)} %bitcast.141, bf16[512,256]{1,0:T(8,128)(2,1)} %bitcast_select_fusion.3.w_ref.few_ref), custom_call_target="tpu_custom_call" | custom-call | flops 134217728 | bytes 4194304 | tf_op jit(solution)/shard_map/norm_one/pallas_call | solution.py:638
  51.2 4.3 %collective-permute-done.8 = bf16[4,2,16,1536]{3,2,1,0:T(8,128)(2,1)S(1)} collective-permute-done((bf16[4,2,16,1536]{3,2,1,0:T(8,128)(2,1)S(1)}, bf16[4,2,16,1536]{3,2,1,0:T(8,128)(2,1)S(1)}, u32[]{:S(2)}, u32[]{:S(2)}) %collective-permute-start.8) | collective-permute-done | bytes 393248 | tf_op jit(solution)/shard_map/ppermute | solution.py:40
  56.9 1.7 collective-permute-start.17
  60.1 5.4 %collective-permute-done.7 = bf16[4,256,128]{2,1,0:T(8,128)(2,1)} collective-permute-done((bf16[4,256,128]{2,1,0:T(8,128)(2,1)}, bf16[4,256,128]{2,1,0:T(8,128)(2,1)}, u32[]{:S(2)}, u32[]{:S(2)}) %collective-permute-start.7) | collective-permute-done | bytes 262176 | tf_op jit(solution)/shard_map/ppermute | solution.py:40
  66.7 5.1 %queries.1 = (bf16[4,256,512]{2,1,0:T(8,128)(2,1)S(1)}, f32[4,256,128]{2,1,0:T(8,128)S(1)}, f32[4,8,256]{2,1,0:T(8,128)S(1)}) custom-call(bf16[4,256,512]{2,1,0:T(8,128)(2,1)S(1)} %copy-done.3, bf16[512,1536]{1,0:T(8,128)(2,1)S(1)} %bitcast_select_fusion.1.w_ref, bf16[512,256]{1,0:T(8,128)(2,1)S(1)} %copy-done.2, s32[4,256,8]{2,1,0:T(8,128)S(1)} %bitcast.135, ...), custom_call_target="tpu_custom_call" | custom-call | flops 3221225472 | bytes 6291456 | tf_op jit(solution)/shard_map/queries/pallas_call | solution.py:656
  72.6 1.8 collective-permute-start.18
  74.5 12.0 %attend.1 = (bf16[4,256,512]{2,1,0:T(8,128)(2,1)S(1)}, f32[4,8,256]{2,1,0:T(8,128)S(1)}) custom-call(s32[18]{0:T(128)S(1)} %pad_add_fusion.2.plan, bf16[4,256,512]{2,1,0:T(8,128)(2,1)S(1)} %get-tuple-element.83.q_ref, bf16[16,256,128]{2,1,0:T(8,128)(2,1)S(1)} %bitcast_select_fusion.2.kv_ref, s32[4,1,256]{2,1,0:T(1,128)S(1)} %reshape.275.start_ref, ...), custom_call_target="tpu_custom_call" | custom-call | flops 12000000000 | bytes 4194304 | tf_op jit(solution)/shard_map/attend/pallas_call | solution.py:677
  89.2 26.6 %forward.1 = (bf16[4,256,1536]{2,1,0:T(8,128)(2,1)}, f32[4,256,512]{2,1,0:T(8,128)}, bf16[4,256,512]{2,1,0:T(8,128)(2,1)}, bf16[256,512]{1,0:T(8,128)(2,1)}, f32...) custom-call(s32[1]{0:T(128)S(6)} %add.158.moved, bf16[4,256,512]{2,1,0:T(8,128)(2,1)} %copy-done.8, ...), custom_call_target="tpu_custom_call" | custom-call | flops 24000000000 | bytes 25165824 | tf_op jit(solution)/shard_map/forward/pallas_call | solution.py:716
  115.8 16.4 %branch_back.1 = (f32[4,256,512]{2,1,0:T(8,128)}, bf16[4,256,512]{2,1,0:T(8,128)(2,1)}, f32[4,8,256]{2,1,0:T(8,128)}, bf16[4,256,128]{2,1,0:T(8,128)(2,1)}, f32[...) custom-call(s32[1]{0:T(128)} %bitcast.7.core, f32[4,256,512]{2,1,0:T(8,128)} %get-tuple-element.101.back_ref, ...), custom_call_target="tpu_custom_call" | custom-call | flops 8000000000 | bytes 14680064 | tf_op jit(solution)/shard_map/branch_back/pallas_call | solution.py:755
  134.2 21.3 %attend_back.1 = (bf16[4,256,512]{2,1,0:T(8,128)(2,1)S(1)}, bf16[8,256,128]{2,1,0:T(8,128)(2,1)S(1)}, bf16[8,256,128]{2,1,0:T(8,128)(2,1)S(1)}) custom-call(s32[18]{0:T(128)S(1)} %pad_add_fusion.2.plan, bf16[4,256,512]{2,1,0:T(8,128)(2,1)S(1)} %copy-done.5, bf16[4,256,512]{2,1,0:T(8,128)(2,1)S(1)} %copy-done.9, ...), custom_call_target="tpu_custom_call" | custom-call | flops 24999999488 | bytes 6291456 | tf_op jit(solution)/shard_map/attend_back/pallas_call | solution.py:814
  156.5 2.4 collective-permute-start.19
  161.7 7.5 %collective-permute-start.23 = (bf16[1024,128]{1,0:T(8,128)(2,1)}, bf16[1024,128]{1,0:T(8,128)(2,1)}, u32[]{:S(2)}, u32[]{:S(2)}) collective-permute-start(bf16[1024,128]{1,0:T(8,128)(2,1)} %dynamic-slice_bitcast_fusion.4), channel_id=1, source_target_pairs={{0,2},{1,3},{2,0},{3,1},{4,6},{5,7},{6,4},{7,5},{8,10},{9,11},{10,... | collective-permute-start | bytes 786440 | tf_op jit(solution)/shard_map/ppermute | solution.py:40
  170.3 2.7 %collective-permute-start.20 = (bf16[4,128,512]{2,1,0:T(8,128)(2,1)S(1)}, bf16[4,128,512]{2,1,0:T(8,128)(2,1)S(1)}, u32[]{:S(2)}, u32[]{:S(2)}) collective-permute-start(bf16[4,128,512]{2,1,0:T(8,128)(2,1)S(1)} %dynamic-slice_bitcast_fusion), channel_id=1, source_target_pairs={{0,4},{4,0},{8,12},{12,8},{16,20},{20,16},{24,28},{28,24},{1,5},{5... | collective-permute-start | bytes 1572872 | tf_op jit(solution)/shard_map/ppermute | solution.py:40
  173.0 8.4 %query_weights.1 = (bf16[256,1536]{1,0:T(8,128)(2,1)}, bf16[256,1536]{1,0:T(8,128)(2,1)}, bf16[4,256,1536]{2,1,0:T(8,128)(2,1)}) custom-call(s32[1]{0:T(128)} %bitcast.7.core, bf16[4,256,512]{2,1,0:T(8,128)(2,1)} %copy-done.7, s32[4,256,8]{2,1,0:T(8,128)} %bitcast.138, bf16[4,256,512]{2,1,0:T(8,128)(2,1)} %get-tuple-element.80.n_ref), custom_call_target="tpu_custom_call" | custom-call | flops 4000000000 | bytes 10485760 | tf_op jit(solution)/shard_map/query_weights/pallas_call | solution.py:845
  182.5 1.7 fusion.4
  185.0 2.3 collective-permute-start.36
  187.6 2.1 collective-permute-start.26
  189.7 9.4 %inputs_back.1 = (f32[4,256,512]{2,1,0:T(8,128)}, bf16[256,512]{1,0:T(8,128)(2,1)}, bf16[256,256]{1,0:T(8,128)(2,1)}, bf16[256,256]{1,0:T(8,128)(2,1)}) custom-call(s32[2]{0:T(128)} %pad_add_fusion.3.core, bf16[4,256,1536]{2,1,0:T(8,128)(2,1)} %get-tuple-element.120.wide_ref, bf16[4,256,128]{2,1,0:T(8,128)(2,1)} %get-tuple-element.121.glog_ref, ...), custom_call_target="tpu_custom_call" | custom-call | flops 4000000000 | bytes 12582912 | tf_op jit(solution)/shard_map/inputs_back/pallas_call | solution.py:876
  203.4 3.7 %collective-permute-done.29 = bf16[4,16,1536]{2,1,0:T(8,128)(2,1)S(1)} collective-permute-done((bf16[4,16,1536]{2,1,0:T(8,128)(2,1)S(1)}, bf16[4,16,1536]{2,1,0:T(8,128)(2,1)S(1)}, u32[]{:S(2)}, u32[]{:S(2)}) %collective-permute-start.29) | collective-permute-done | bytes 196640 | tf_op jit(solution)/shard_map/ppermute | solution.py:40
  208.5 4.9 %collective-permute-done.27 = bf16[4,16,1536]{2,1,0:T(8,128)(2,1)S(1)} collective-permute-done((bf16[4,16,1536]{2,1,0:T(8,128)(2,1)S(1)}, bf16[4,16,1536]{2,1,0:T(8,128)(2,1)S(1)}, u32[]{:S(2)}, u32[]{:S(2)}) %collective-permute-start.27) | collective-permute-done | bytes 196640 | tf_op jit(solution)/shard_map/ppermute | solution.py:40
  214.7 2.8 %collective-permute-done.30 = bf16[4,16,256]{2,1,0:T(8,128)(2,1)S(1)} collective-permute-done((bf16[4,16,256]{2,1,0:T(8,128)(2,1)S(1)}, bf16[4,16,256]{2,1,0:T(8,128)(2,1)S(1)}, u32[]{:S(2)}, u32[]{:S(2)}) %collective-permute-start.30) | collective-permute-done | bytes 32800 | tf_op jit(solution)/shard_map/ppermute | solution.py:40
  217.6 5.2 %collective-permute-start.33 = (bf16[16,3328]{1,0:T(8,128)(2,1)S(1)}, bf16[16,3328]{1,0:T(8,128)(2,1)S(1)}, u32[]{:S(2)}, u32[]{:S(2)}) collective-permute-start(bf16[16,3328]{1,0:T(8,128)(2,1)S(1)} %get-tuple-element.190), channel_id=1, source_target_pairs={{0,8},{4,12},{8,0},{12,4},{16,24},{20,28},{24,16},{28,20},{1,9},{5... | collective-permute-start | bytes 319496 | tf_op jit(solution)/shard_map/ppermute | solution.py:40
  224.4 2.9 %collective-permute-start.37 = (bf16[128,512]{1,0:T(8,128)(2,1)S(1)}, bf16[128,512]{1,0:T(8,128)(2,1)S(1)}, u32[]{:S(2)}, u32[]{:S(2)}) collective-permute-start(bf16[128,512]{1,0:T(8,128)(2,1)S(1)} %dynamic-slice_bitcast_fusion.9), channel_id=1, source_target_pairs={{0,8},{4,12},{8,0},{12,4},{16,24},{20,28},{24,16},{28,20},{1,9},{5... | collective-permute-start | bytes 393224 | tf_op jit(solution)/shard_map/ppermute | solution.py:40
  228.1 1.9 collective-permute-done.35
  230.0 1.9 collective-permute-done.34
  (230 shorter events, 44.8 us)
Async XLA Ops:
  7.3 81.9 %all-gather.3.cloned.1.call-start = ((), (), s32[]{:S(2)}) async-start(), calls=%async_computation.2 | async-start | bytes 4325376 | tf_op jit(solution)/shard_map/all_gather | solution.py:578
  10.3 14.0 %collective-permute-start.2 = (bf16[16,1792]{1,0:T(8,128)(2,1)S(1)}, bf16[16,1792]{1,0:T(8,128)(2,1)S(1)}, u32[]{:S(2)}, u32[]{:S(2)}) collective-permute-start(bf16[16,1792]{1,0:T(8,128)(2,1)S(1)} %concatenate.23), channel_id=1, source_target_pairs={{0,8},{4,12},{8,0},{12,4},{16,24},{20,28},{24,16},{28,20},{1,9},{5... | collective-permute-start | bytes 172040 | tf_op jit(solution)/shard_map/ppermute | solution.py:40
  13.3 11.0 %collective-permute-start.1 = (bf16[16,1792]{1,0:T(8,128)(2,1)S(1)}, bf16[16,1792]{1,0:T(8,128)(2,1)S(1)}, u32[]{:S(2)}, u32[]{:S(2)}) collective-permute-start(bf16[16,1792]{1,0:T(8,128)(2,1)S(1)} %concatenate.23), channel_id=1, source_target_pairs={{0,16},{4,20},{8,24},{12,28},{16,0},{20,4},{24,8},{28,12},{1,17},{... | collective-permute-start | bytes 172040 | tf_op jit(solution)/shard_map/ppermute | solution.py:40
  15.9 8.4 %collective-permute-start = (bf16[16,1792]{1,0:T(8,128)(2,1)S(1)}, bf16[16,1792]{1,0:T(8,128)(2,1)S(1)}, u32[]{:S(2)}, u32[]{:S(2)}) collective-permute-start(bf16[16,1792]{1,0:T(8,128)(2,1)S(1)} %concatenate.23), channel_id=1, source_target_pairs={{0,24},{4,28},{8,16},{12,20},{16,8},{20,12},{24,0},{28,4},{1,25},{... | collective-permute-start | bytes 172040 | tf_op jit(solution)/shard_map/ppermute | solution.py:40
  16.6 152.6 %reduce-scatter.2.cloned.1.call-start = ((), (), s32[]{:S(2)}) async-start(), calls=%async_computation.1 | async-start | bytes 5242880 | tf_op jit(solution)/shard_map/reduce_scatter | solution.py:811
  19.5 11.1 %collective-permute-start.4 = (bf16[256,512]{1,0:T(8,128)(2,1)S(1)}, bf16[256,512]{1,0:T(8,128)(2,1)S(1)}, u32[]{:S(2)}, u32[]{:S(2)}) collective-permute-start(bf16[256,512]{1,0:T(8,128)(2,1)S(1)} %dynamic-slice_bitcast_fusion.6), channel_id=1, source_target_pairs={{0,3},{1,2},{2,1},{3,0},{4,7},{5,6},{6,5},{7,4},{8,11},{9,10},{10,... | collective-permute-start | bytes 786440 | tf_op jit(solution)/shard_map/ppermute | solution.py:40
  24.7 12.8 %collective-permute-start.15 = (bf16[16,1664]{1,0:T(8,128)(2,1)S(1)}, bf16[16,1664]{1,0:T(8,128)(2,1)S(1)}, u32[]{:S(2)}, u32[]{:S(2)}) collective-permute-start(bf16[16,1664]{1,0:T(8,128)(2,1)S(1)} %pad_maximum_fusion.2), channel_id=1, source_target_pairs={{0,24},{4,28},{8,16},{12,20},{16,8},{20,12},{24,0},{28,4},{1,25},{... | collective-permute-start | bytes 159752 | tf_op jit(solution)/shard_map/ppermute | solution.py:40
  28.3 9.2 %collective-permute-start.14 = (bf16[16,1664]{1,0:T(8,128)(2,1)S(1)}, bf16[16,1664]{1,0:T(8,128)(2,1)S(1)}, u32[]{:S(2)}, u32[]{:S(2)}) collective-permute-start(bf16[16,1664]{1,0:T(8,128)(2,1)S(1)} %pad_maximum_fusion.2), channel_id=1, source_target_pairs={{0,16},{4,20},{8,24},{12,28},{16,0},{20,4},{24,8},{28,12},{1,17},{... | collective-permute-start | bytes 159752 | tf_op jit(solution)/shard_map/ppermute | solution.py:40
  28.3 9.2 %collective-permute-start.13 = (bf16[16,1664]{1,0:T(8,128)(2,1)S(1)}, bf16[16,1664]{1,0:T(8,128)(2,1)S(1)}, u32[]{:S(2)}, u32[]{:S(2)}) collective-permute-start(bf16[16,1664]{1,0:T(8,128)(2,1)S(1)} %pad_maximum_fusion.2), channel_id=1, source_target_pairs={{0,8},{4,12},{8,0},{12,4},{16,24},{20,28},{24,16},{28,20},{1,9},{5... | collective-permute-start | bytes 159752 | tf_op jit(solution)/shard_map/ppermute | solution.py:40
  29.2 8.3 %collective-permute-start.3 = (bf16[4,16,1792]{2,1,0:T(8,128)(2,1)S(1)}, bf16[4,16,1792]{2,1,0:T(8,128)(2,1)S(1)}, u32[]{:S(2)}, u32[]{:S(2)}) collective-permute-start(bf16[4,16,1792]{2,1,0:T(8,128)(2,1)S(1)} %select_select_fusion), channel_id=1, source_target_pairs={{0,2},{1,3},{2,0},{3,1},{4,6},{5,7},{6,4},{7,5},{8,10},{9,11},{10,... | collective-permute-start | bytes 688136 | tf_op jit(solution)/shard_map/ppermute | solution.py:40
  42.0 13.5 %collective-permute-start.8 = (bf16[4,2,16,1536]{3,2,1,0:T(8,128)(2,1)S(1)}, bf16[4,2,16,1536]{3,2,1,0:T(8,128)(2,1)S(1)}, u32[]{:S(2)}, u32[]{:S(2)}) collective-permute-start(bf16[4,2,16,1536]{3,2,1,0:T(8,128)(2,1)S(1)} %slice.93), channel_id=1, source_target_pairs={{0,4},{4,0},{8,12},{12,8},{16,20},{20,16},{24,28},{28,24},{1,5},{5... | collective-permute-start | bytes 1179656 | tf_op jit(solution)/shard_map/ppermute | solution.py:40
  44.0 12.7 %collective-permute-start.16 = (bf16[4,16,1664]{2,1,0:T(8,128)(2,1)S(1)}, bf16[4,16,1664]{2,1,0:T(8,128)(2,1)S(1)}, u32[]{:S(2)}, u32[]{:S(2)}) collective-permute-start(bf16[4,16,1664]{2,1,0:T(8,128)(2,1)S(1)} %select_select_fusion.1), channel_id=1, source_target_pairs={{0,2},{1,3},{2,0},{3,1},{4,6},{5,7},{6,4},{7,5},{8,10},{9,11},{10,... | collective-permute-start | bytes 638984 | tf_op jit(solution)/shard_map/ppermute | solution.py:40
  44.8 11.8 %collective-permute-start.10 = (bf16[256,8]{1,0:T(8,128)(2,1)S(1)}, bf16[256,8]{1,0:T(8,128)(2,1)S(1)}, u32[]{:S(2)}, u32[]{:S(2)}) collective-permute-start(bf16[256,8]{1,0:T(8,128)(2,1)S(1)} %fusion.8), channel_id=1, source_target_pairs={{0,3},{1,2},{2,1},{3,0},{4,7},{5,6},{6,5},{7,4},{8,11},{9,10},{10,... | collective-permute-start | bytes 12296 | tf_op jit(solution)/shard_map/ppermute | solution.py:40
  56.5 9.0 %collective-permute-start.7 = (bf16[4,256,128]{2,1,0:T(8,128)(2,1)}, bf16[4,256,128]{2,1,0:T(8,128)(2,1)}, u32[]{:S(2)}, u32[]{:S(2)}) collective-permute-start(bf16[4,256,128]{2,1,0:T(8,128)(2,1)} %get-tuple-element.76), channel_id=1, source_target_pairs={{0,2},{1,3},{2,0},{3,1},{4,6},{5,7},{6,4},{7,5},{8,10},{9,11},{10,... | collective-permute-start | bytes 786440 | tf_op jit(solution)/shard_map/ppermute | solution.py:40
  56.9 15.1 %collective-permute-start.17 = (bf16[4,2,16,1664]{3,2,1,0:T(8,128)(2,1)S(1)}, bf16[4,2,16,1664]{3,2,1,0:T(8,128)(2,1)S(1)}, u32[]{:S(2)}, u32[]{:S(2)}) collective-permute-start(bf16[4,2,16,1664]{3,2,1,0:T(8,128)(2,1)S(1)} %broadcast_select_fusion.4), channel_id=1, source_target_pairs={{0,4},{4,0},{8,12},{12,8},{16,20},{20,16},{24,28},{28,24},{1,5},{5... | collective-permute-start | bytes 1277960 | tf_op jit(solution)/shard_map/ppermute | solution.py:40
  66.6 7.8 %collective-permute-start.11 = (bf16[2,4,256,128]{3,2,1,0:T(8,128)(2,1)S(1)}, bf16[2,4,256,128]{3,2,1,0:T(8,128)(2,1)S(1)}, u32[]{:S(2)}, u32[]{:S(2)}) collective-permute-start(bf16[2,4,256,128]{3,2,1,0:T(8,128)(2,1)S(1)} %broadcast_select_fusion.2), channel_id=1, source_target_pairs={{0,1},{1,0},{2,3},{3,2},{4,5},{5,4},{6,7},{7,6},{8,9},{9,8},{10,11... | collective-permute-start | bytes 1572872 | tf_op jit(solution)/shard_map/ppermute | solution.py:40
  72.0 14.5 %collective-permute-start.12 = (bf16[256,512]{1,0:T(8,128)(2,1)S(1)}, bf16[256,512]{1,0:T(8,128)(2,1)S(1)}, u32[]{:S(2)}, u32[]{:S(2)}) collective-permute-start(bf16[256,512]{1,0:T(8,128)(2,1)S(1)} %dynamic-slice_bitcast_fusion.5), channel_id=1, source_target_pairs={{0,3},{1,2},{2,1},{3,0},{4,7},{5,6},{6,5},{7,4},{8,11},{9,10},{10,... | collective-permute-start | bytes 786440 | tf_op jit(solution)/shard_map/ppermute | solution.py:40
  72.6 14.1 %collective-permute-start.18 = (bf16[4,2,2,16,1664]{4,3,2,1,0:T(8,128)(2,1)S(1)}, bf16[4,2,2,16,1664]{4,3,2,1,0:T(8,128)(2,1)S(1)}, u32[]{:S(2)}, u32[]{:S(2)}) collective-permute-start(bf16[4,2,2,16,1664]{4,3,2,1,0:T(8,128)(2,1)S(1)} %broadcast_select_fusion), channel_id=1, source_target_pairs={{0,1},{1,0},{2,3},{3,2},{4,5},{5,4},{6,7},{7,6},{8,9},{9,8},{10,11... | collective-permute-start | bytes 2555912 | tf_op jit(solution)/shard_map/ppermute | solution.py:40
  159.5 21.9 %collective-permute-start.22 = (bf16[256,1536]{1,0:T(8,128)(2,1)}, bf16[256,1536]{1,0:T(8,128)(2,1)S(1)}, u32[]{:S(2)}, u32[]{:S(2)}) collective-permute-start(bf16[256,1536]{1,0:T(8,128)(2,1)} %get-tuple-element.118), channel_id=1, source_target_pairs={{0,1},{1,0},{2,3},{3,2},{4,5},{5,4},{6,7},{7,6},{8,9},{9,8},{10,11... | collective-permute-start | bytes 2359304 | tf_op jit(solution)/shard_map/ppermute | solution.py:40
  161.7 19.9 %collective-permute-start.23 = (bf16[1024,128]{1,0:T(8,128)(2,1)}, bf16[1024,128]{1,0:T(8,128)(2,1)}, u32[]{:S(2)}, u32[]{:S(2)}) collective-permute-start(bf16[1024,128]{1,0:T(8,128)(2,1)} %dynamic-slice_bitcast_fusion.4), channel_id=1, source_target_pairs={{0,2},{1,3},{2,0},{3,1},{4,6},{5,7},{6,4},{7,5},{8,10},{9,11},{10,... | collective-permute-start | bytes 786440 | tf_op jit(solution)/shard_map/ppermute | solution.py:40
  170.3 14.5 %collective-permute-start.20 = (bf16[4,128,512]{2,1,0:T(8,128)(2,1)S(1)}, bf16[4,128,512]{2,1,0:T(8,128)(2,1)S(1)}, u32[]{:S(2)}, u32[]{:S(2)}) collective-permute-start(bf16[4,128,512]{2,1,0:T(8,128)(2,1)S(1)} %dynamic-slice_bitcast_fusion), channel_id=1, source_target_pairs={{0,4},{4,0},{8,12},{12,8},{16,20},{20,16},{24,28},{28,24},{1,5},{5... | collective-permute-start | bytes 1572872 | tf_op jit(solution)/shard_map/ppermute | solution.py:40
  182.5 16.6 %collective-permute-start.28 = (bf16[4,2,16,1536]{3,2,1,0:T(8,128)(2,1)}, bf16[4,2,16,1536]{3,2,1,0:T(8,128)(2,1)S(1)}, u32[]{:S(2)}, u32[]{:S(2)}) collective-permute-start(bf16[4,2,16,1536]{3,2,1,0:T(8,128)(2,1)} %dynamic-slice_bitcast_fusion.1), channel_id=1, source_target_pairs={{0,4},{4,0},{8,12},{12,8},{16,20},{20,16},{24,28},{28,24},{1,5},{5... | collective-permute-start | bytes 1179656 | tf_op jit(solution)/shard_map/ppermute | solution.py:40
  185.0 32.6 %collective-permute-start.36 = (bf16[2,128,512]{2,1,0:T(8,128)(2,1)S(1)}, bf16[2,128,512]{2,1,0:T(8,128)(2,1)S(1)}, u32[]{:S(2)}, u32[]{:S(2)}) collective-permute-start(bf16[2,128,512]{2,1,0:T(8,128)(2,1)S(1)} %dynamic-slice_bitcast_fusion.3), channel_id=1, source_target_pairs={{0,16},{4,20},{8,24},{12,28},{16,0},{20,4},{24,8},{28,12},{1,17},{... | collective-permute-start | bytes 786440 | tf_op jit(solution)/shard_map/ppermute | solution.py:40
  187.6 19.6 %collective-permute-start.26 = (bf16[4,2,16,1536]{3,2,1,0:T(8,128)(2,1)S(1)}, bf16[4,2,16,1536]{3,2,1,0:T(8,128)(2,1)S(1)}, u32[]{:S(2)}, u32[]{:S(2)}) collective-permute-start(bf16[4,2,16,1536]{3,2,1,0:T(8,128)(2,1)S(1)} %dynamic-slice_bitcast_fusion.2), channel_id=1, source_target_pairs={{0,2},{1,3},{2,0},{3,1},{4,6},{5,7},{6,4},{7,5},{8,10},{9,11},{10,... | collective-permute-start | bytes 1179656 | tf_op jit(solution)/shard_map/ppermute | solution.py:40
  199.3 7.8 %collective-permute-start.29 = (bf16[4,16,1536]{2,1,0:T(8,128)(2,1)S(1)}, bf16[4,16,1536]{2,1,0:T(8,128)(2,1)S(1)}, u32[]{:S(2)}, u32[]{:S(2)}) collective-permute-start(bf16[4,16,1536]{2,1,0:T(8,128)(2,1)S(1)} %dynamic-slice_bitcast_fusion.7), channel_id=1, source_target_pairs={{0,2},{1,3},{2,0},{3,1},{4,6},{5,7},{6,4},{7,5},{8,10},{9,11},{10,... | collective-permute-start | bytes 589832 | tf_op jit(solution)/shard_map/ppermute | solution.py:40
  201.8 6.7 %collective-permute-start.25 = (bf16[4,2,16,256]{3,2,0,1:T(8,128)(2,1)S(1)}, bf16[4,2,16,256]{3,2,0,1:T(8,128)(2,1)S(1)}, u32[]{:S(2)}, u32[]{:S(2)}) collective-permute-start(bf16[4,2,16,256]{3,2,0,1:T(8,128)(2,1)S(1)} %bitcast.161), channel_id=1, source_target_pairs={{0,2},{1,3},{2,0},{3,1},{4,6},{5,7},{6,4},{7,5},{8,10},{9,11},{10,... | collective-permute-start | bytes 196616 | tf_op jit(solution)/shard_map/ppermute | solution.py:40
  202.4 11.4 %collective-permute-start.32 = (bf16[256,512]{1,0:T(8,128)(2,1)S(1)}, bf16[256,512]{1,0:T(8,128)(2,1)S(1)}, u32[]{:S(2)}, u32[]{:S(2)}) collective-permute-start(bf16[256,512]{1,0:T(8,128)(2,1)S(1)} %copy-done.31), channel_id=1, source_target_pairs={{0,3},{1,2},{2,1},{3,0},{4,7},{5,6},{6,5},{7,4},{8,11},{9,10},{10,... | collective-permute-start | bytes 786440 | tf_op jit(solution)/shard_map/ppermute | solution.py:40
  217.6 10.5 %collective-permute-start.33 = (bf16[16,3328]{1,0:T(8,128)(2,1)S(1)}, bf16[16,3328]{1,0:T(8,128)(2,1)S(1)}, u32[]{:S(2)}, u32[]{:S(2)}) collective-permute-start(bf16[16,3328]{1,0:T(8,128)(2,1)S(1)} %get-tuple-element.190), channel_id=1, source_target_pairs={{0,8},{4,12},{8,0},{12,4},{16,24},{20,28},{24,16},{28,20},{1,9},{5... | collective-permute-start | bytes 319496 | tf_op jit(solution)/shard_map/ppermute | solution.py:40
  222.8 7.2 %collective-permute-start.35 = (bf16[16,3328]{1,0:T(8,128)(2,1)S(1)}, bf16[16,3328]{1,0:T(8,128)(2,1)S(1)}, u32[]{:S(2)}, u32[]{:S(2)}) collective-permute-start(bf16[16,3328]{1,0:T(8,128)(2,1)S(1)} %get-tuple-element.191), channel_id=1, source_target_pairs={{0,24},{4,28},{8,16},{12,20},{16,8},{20,12},{24,0},{28,4},{1,25},{... | collective-permute-start | bytes 319496 | tf_op jit(solution)/shard_map/ppermute | solution.py:40
  222.8 9.1 %collective-permute-start.34 = (bf16[16,3328]{1,0:T(8,128)(2,1)S(1)}, bf16[16,3328]{1,0:T(8,128)(2,1)S(1)}, u32[]{:S(2)}, u32[]{:S(2)}) collective-permute-start(bf16[16,3328]{1,0:T(8,128)(2,1)S(1)} %get-tuple-element.192), channel_id=1, source_target_pairs={{0,16},{4,20},{8,24},{12,28},{16,0},{20,4},{24,8},{28,12},{1,17},{... | collective-permute-start | bytes 319496 | tf_op jit(solution)/shard_map/ppermute | solution.py:40
  224.4 10.8 %collective-permute-start.37 = (bf16[128,512]{1,0:T(8,128)(2,1)S(1)}, bf16[128,512]{1,0:T(8,128)(2,1)S(1)}, u32[]{:S(2)}, u32[]{:S(2)}) collective-permute-start(bf16[128,512]{1,0:T(8,128)(2,1)S(1)} %dynamic-slice_bitcast_fusion.9), channel_id=1, source_target_pairs={{0,8},{4,12},{8,0},{12,4},{16,24},{20,28},{24,16},{28,20},{1,9},{5... | collective-permute-start | bytes 393224 | tf_op jit(solution)/shard_map/ppermute | solution.py:40
  227.3 8.6 %collective-permute-start.31 = (bf16[256,512]{1,0:T(8,128)(2,1)S(1)}, bf16[256,512]{1,0:T(8,128)(2,1)S(1)}, u32[]{:S(2)}, u32[]{:S(2)}) collective-permute-start(bf16[256,512]{1,0:T(8,128)(2,1)S(1)} %copy-done.30), channel_id=1, source_target_pairs={{0,3},{1,2},{2,1},{3,0},{4,7},{5,6},{6,5},{7,4},{8,11},{9,10},{10,... | collective-permute-start | bytes 786440 | tf_op jit(solution)/shard_map/ppermute | solution.py:40
  (40 other events, 236.7 us)
Sparse Core Ops, SparseCore 0:
  16.7 69.0 all-gather.2
  115.9 50.2 reduce-scatter.1

commit v5 on v4

--- a/solution.py
+++ b/solution.py
@@ -917,9 +917,17 @@
     feed_grad = scatter_end(feed_top, joint)
     for bit in reversed(range(far_low, far_low + far_count - 1)):
         feed_grad = scatter_bits(feed_grad.astype(bf16), "dp", (bit, 1), 0)
-    joint_sum = far_scatter(joint)
+    started = [joint]
+    for i, group in enumerate(far_groups[:-1]):
+        started = [scatter_bits(started[0], "dp", group, depth - 2 - i).astype(bf16)]
+    own, got, _ = scatter_start(started[0], "dp", far_groups[-1], 0)
+
+    def summed(first, last):
+        return scatter_end((own[:, first:last], [g[:, first:last] for g in got], None))
+
+    query_grad, out_grads = summed(0, wide), summed(wide, 2 * wide)
     up_rows = w_up.shape[0]
-    smalls = joint_sum[:, 2 * wide :]
+    smalls = summed(2 * wide, 2 * wide + 2 * LANES)
     def returned(a, piece):
         piece = flip(piece, "mp", peers - 1).astype(a.dtype)
         a = a.reshape(rows, 2, chunk, model)
@@ -933,9 +941,9 @@
         outputs,
         input_grad,
         counts,
-        joint_sum[:, :wide],
+        query_grad,
         smalls[:, : 2 * hs],
-        joint_sum[:, wide : 2 * wide],
+        out_grads,
         smalls[:, LANES : LANES + heads],
         smalls[:, LANES + heads : LANES + heads + 2],
         smalls[:, LANES + heads + 2 : LANES + heads + 4],

time: 244 us -> 241 us (0.988)
  transfers between devices with their start and end apart: 40 -> 40, of which waited for: 14 -> 11; matrix products, arithmetic and copies ran while one was open for 11% -> 10% of each run, Pallas kernels for 32% -> 32%
where the time goes in v5:
time: 241 us; the launch traced here: 240 us
  Pallas kernels  103 us (43%)
  starting transfers between devices  50.6 us (21%)
  waiting for transfers between devices  36.3 us (15%)
  between operations  18.9 us (8%)
  other arithmetic  16.9 us (7%)
  local copies, waits for them, and re-layouts  14.2 us (6%)
    ppermute x38, starting transfers between devices, flip(): lax.ppermute(x, axis, [(i, i ^ mask) for i in range(lax.axis_size(axis))])  50.5 us
    ppermute x38, waiting for transfers between devices, flip(): lax.ppermute(x, axis, [(i, i ^ mask) for i in range(lax.axis_size(axis))])  36.3 us
    pallas_call x1, Pallas kernels, shards(): pl.pallas_call(functools.partial(forward_kernel, heads=heads, slots=slots...  26.6 us
    pallas_call x1, Pallas kernels, shards(): pl.pallas_call(functools.partial(attend_back_kernel, **attention), grid_s...  21.3 us
    pallas_call x1, Pallas kernels, shards(): pl.pallas_call(functools.partial(branch_back_kernel, heads=heads, slots=s...  16.3 us
    pallas_call x1, Pallas kernels, shards(): pl.pallas_call(functools.partial(attend_kernel, **attention), grid_spec=p...  12 us
    pallas_call x1, Pallas kernels, shards(): pl.pallas_call(functools.partial(input_kernel, heads=heads, per=per), gri...  9.37 us
    pallas_call x1, Pallas kernels, shards(): pl.pallas_call(functools.partial(query_weights_kernel, heads=heads, slots...  8.45 us
  transfers between devices with their start and end apart: 40, of which 11 were waited for; matrix products, arithmetic and copies ran while one was open for 10% of the time, Pallas kernels for 32%

profile of v5, /device:TPU:0, one launch (start us, length us, event | category | flops | bytes accessed | tf_op | source)
XLA Modules:
  0.0 240.2 jit_solution(2476158924983114651)
XLA Ops:
  10.3 3.0 %collective-permute-start.2 = (bf16[16,1792]{1,0:T(8,128)(2,1)S(1)}, bf16[16,1792]{1,0:T(8,128)(2,1)S(1)}, u32[]{:S(2)}, u32[]{:S(2)}) collective-permute-start(bf16[16,1792]{1,0:T(8,128)(2,1)S(1)} %concatenate.23), channel_id=1, source_target_pairs={{0,8},{4,12},{8,0},{12,4},{16,24},{20,28},{24,16},{28,20},{1,9},{5... | collective-permute-start | bytes 172040 | tf_op jit(solution)/shard_map/ppermute | solution.py:40
  13.3 2.6 %collective-permute-start.1 = (bf16[16,1792]{1,0:T(8,128)(2,1)S(1)}, bf16[16,1792]{1,0:T(8,128)(2,1)S(1)}, u32[]{:S(2)}, u32[]{:S(2)}) collective-permute-start(bf16[16,1792]{1,0:T(8,128)(2,1)S(1)} %concatenate.23), channel_id=1, source_target_pairs={{0,16},{4,20},{8,24},{12,28},{16,0},{20,4},{24,8},{28,12},{1,17},{... | collective-permute-start | bytes 172040 | tf_op jit(solution)/shard_map/ppermute | solution.py:40
  24.7 3.6 %collective-permute-start.15 = (bf16[16,1664]{1,0:T(8,128)(2,1)S(1)}, bf16[16,1664]{1,0:T(8,128)(2,1)S(1)}, u32[]{:S(2)}, u32[]{:S(2)}) collective-permute-start(bf16[16,1664]{1,0:T(8,128)(2,1)S(1)} %pad_maximum_fusion.2), channel_id=1, source_target_pairs={{0,24},{4,28},{8,16},{12,20},{16,8},{20,12},{24,0},{28,4},{1,25},{... | collective-permute-start | bytes 159752 | tf_op jit(solution)/shard_map/ppermute | solution.py:40
  30.6 6.8 %collective-permute-done.3 = bf16[4,16,1792]{2,1,0:T(8,128)(2,1)S(1)} collective-permute-done((bf16[4,16,1792]{2,1,0:T(8,128)(2,1)S(1)}, bf16[4,16,1792]{2,1,0:T(8,128)(2,1)S(1)}, u32[]{:S(2)}, u32[]{:S(2)}) %collective-permute-start.3) | collective-permute-done | bytes 229408 | tf_op jit(solution)/shard_map/ppermute | solution.py:40
  37.6 1.6 collective-permute-start.5
  39.9 2.0 collective-permute-done.5
  42.0 1.6 collective-permute-start.8
  47.1 4.1 %norm_one.1 = (bf16[4,256,512]{2,1,0:T(8,128)(2,1)}, bf16[4,256,128]{2,1,0:T(8,128)(2,1)}, f32[8,512]{1,0:T(8,128)}) custom-call(bf16[4,256,512]{2,1,0:T(8,128)(2,1)} %bitcast.136, bf16[512,256]{1,0:T(8,128)(2,1)} %bitcast_select_fusion.3.w_ref.few_ref), custom_call_target="tpu_custom_call" | custom-call | flops 134217728 | bytes 4194304 | tf_op jit(solution)/shard_map/norm_one/pallas_call | solution.py:638
  51.2 4.3 %collective-permute-done.8 = bf16[4,2,16,1536]{3,2,1,0:T(8,128)(2,1)S(1)} collective-permute-done((bf16[4,2,16,1536]{3,2,1,0:T(8,128)(2,1)S(1)}, bf16[4,2,16,1536]{3,2,1,0:T(8,128)(2,1)S(1)}, u32[]{:S(2)}, u32[]{:S(2)}) %collective-permute-start.8) | collective-permute-done | bytes 393248 | tf_op jit(solution)/shard_map/ppermute | solution.py:40
  56.9 1.7 collective-permute-start.17
  58.6 1.5 bitcast_select_fusion.1.w_ref
  60.1 5.4 %collective-permute-done.7 = bf16[4,256,128]{2,1,0:T(8,128)(2,1)} collective-permute-done((bf16[4,256,128]{2,1,0:T(8,128)(2,1)}, bf16[4,256,128]{2,1,0:T(8,128)(2,1)}, u32[]{:S(2)}, u32[]{:S(2)}) %collective-permute-start.7) | collective-permute-done | bytes 262176 | tf_op jit(solution)/shard_map/ppermute | solution.py:40
  66.7 5.1 %queries.1 = (bf16[4,256,512]{2,1,0:T(8,128)(2,1)S(1)}, f32[4,256,128]{2,1,0:T(8,128)S(1)}, f32[4,8,256]{2,1,0:T(8,128)S(1)}) custom-call(bf16[4,256,512]{2,1,0:T(8,128)(2,1)S(1)} %copy-done.3, bf16[512,1536]{1,0:T(8,128)(2,1)S(1)} %bitcast_select_fusion.1.w_ref, bf16[512,256]{1,0:T(8,128)(2,1)S(1)} %copy-done.2, s32[4,256,8]{2,1,0:T(8,128)S(1)} %bitcast.130, ...), custom_call_target="tpu_custom_call" | custom-call | flops 3221225472 | bytes 6291456 | tf_op jit(solution)/shard_map/queries/pallas_call | solution.py:656
  72.6 1.8 collective-permute-start.18
  74.5 12.0 %attend.1 = (bf16[4,256,512]{2,1,0:T(8,128)(2,1)S(1)}, f32[4,8,256]{2,1,0:T(8,128)S(1)}) custom-call(s32[18]{0:T(128)S(1)} %pad_add_fusion.2.plan, bf16[4,256,512]{2,1,0:T(8,128)(2,1)S(1)} %get-tuple-element.83.q_ref, bf16[16,256,128]{2,1,0:T(8,128)(2,1)S(1)} %bitcast_select_fusion.2.kv_ref, s32[4,1,256]{2,1,0:T(1,128)S(1)} %reshape.273.start_ref, ...), custom_call_target="tpu_custom_call" | custom-call | flops 12000000000 | bytes 4194304 | tf_op jit(solution)/shard_map/attend/pallas_call | solution.py:677
  89.2 26.6 %forward.1 = (bf16[4,256,1536]{2,1,0:T(8,128)(2,1)}, f32[4,256,512]{2,1,0:T(8,128)}, bf16[4,256,512]{2,1,0:T(8,128)(2,1)}, bf16[256,512]{1,0:T(8,128)(2,1)}, f32...) custom-call(s32[1]{0:T(128)S(6)} %add.176.moved, bf16[4,256,512]{2,1,0:T(8,128)(2,1)} %copy-done.8, ...), custom_call_target="tpu_custom_call" | custom-call | flops 24000000000 | bytes 25165824 | tf_op jit(solution)/shard_map/forward/pallas_call | solution.py:716
  115.8 16.3 %branch_back.1 = (f32[4,256,512]{2,1,0:T(8,128)}, bf16[4,256,512]{2,1,0:T(8,128)(2,1)}, f32[4,8,256]{2,1,0:T(8,128)}, bf16[4,256,128]{2,1,0:T(8,128)(2,1)}, f32[...) custom-call(s32[1]{0:T(128)} %bitcast.7.core, f32[4,256,512]{2,1,0:T(8,128)} %get-tuple-element.101.back_ref, ...), custom_call_target="tpu_custom_call" | custom-call | flops 8000000000 | bytes 14680064 | tf_op jit(solution)/shard_map/branch_back/pallas_call | solution.py:755
  134.1 21.3 %attend_back.1 = (bf16[4,256,512]{2,1,0:T(8,128)(2,1)S(1)}, bf16[8,256,128]{2,1,0:T(8,128)(2,1)S(1)}, bf16[8,256,128]{2,1,0:T(8,128)(2,1)S(1)}) custom-call(s32[18]{0:T(128)S(1)} %pad_add_fusion.2.plan, bf16[4,256,512]{2,1,0:T(8,128)(2,1)S(1)} %copy-done.5, bf16[4,256,512]{2,1,0:T(8,128)(2,1)S(1)} %copy-done.9, ...), custom_call_target="tpu_custom_call" | custom-call | flops 24999999488 | bytes 6291456 | tf_op jit(solution)/shard_map/attend_back/pallas_call | solution.py:814
  156.4 2.3 collective-permute-start.19
  160.7 12.3 %collective-permute-start.23 = (bf16[1024,128]{1,0:T(8,128)(2,1)S(1)}, bf16[1024,128]{1,0:T(8,128)(2,1)S(1)}, u32[]{:S(2)}, u32[]{:S(2)}) collective-permute-start(bf16[1024,128]{1,0:T(8,128)(2,1)S(1)} %dynamic-slice_bitcast_fusion.3), channel_id=1, source_target_pairs={{0,2},{1,3},{2,0},{3,1},{4,6},{5,7},{6,4},{7,5},{8,10},{9,11},{10,... | collective-permute-start | bytes 786440 | tf_op jit(solution)/shard_map/ppermute | solution.py:40
  174.2 8.4 %query_weights.1 = (bf16[256,1536]{1,0:T(8,128)(2,1)}, bf16[256,1536]{1,0:T(8,128)(2,1)}, bf16[4,256,1536]{2,1,0:T(8,128)(2,1)}) custom-call(s32[1]{0:T(128)} %bitcast.7.core, bf16[4,256,512]{2,1,0:T(8,128)(2,1)} %copy-done.7, s32[4,256,8]{2,1,0:T(8,128)} %bitcast.133, bf16[4,256,512]{2,1,0:T(8,128)(2,1)} %get-tuple-element.80.n_ref), custom_call_target="tpu_custom_call" | custom-call | flops 4000000000 | bytes 10485760 | tf_op jit(solution)/shard_map/query_weights/pallas_call | solution.py:845
  183.2 1.8 collective-permute-start.28
  185.8 3.1 %collective-permute-done.20 = bf16[4,128,512]{2,1,0:T(8,128)(2,1)S(1)} collective-permute-done((bf16[4,128,512]{2,1,0:T(8,128)(2,1)S(1)}, bf16[4,128,512]{2,1,0:T(8,128)(2,1)S(1)}, u32[]{:S(2)}, u32[]{:S(2)}) %collective-permute-start.20) | collective-permute-done | bytes 524320 | tf_op jit(solution)/shard_map/ppermute | solution.py:40
  189.5 9.4 %inputs_back.1 = (f32[4,256,512]{2,1,0:T(8,128)}, bf16[256,512]{1,0:T(8,128)(2,1)}, bf16[256,256]{1,0:T(8,128)(2,1)}, bf16[256,256]{1,0:T(8,128)(2,1)}) custom-call(s32[2]{0:T(128)} %pad_add_fusion.3.core, bf16[4,256,1536]{2,1,0:T(8,128)(2,1)} %get-tuple-element.120.wide_ref, bf16[4,256,128]{2,1,0:T(8,128)(2,1)} %get-tuple-element.121.glog_ref, ...), custom_call_target="tpu_custom_call" | custom-call | flops 4000000000 | bytes 12582912 | tf_op jit(solution)/shard_map/inputs_back/pallas_call | solution.py:876
  199.2 2.1 collective-permute-start.29
  203.8 3.2 %collective-permute-done.29 = bf16[4,16,1536]{2,1,0:T(8,128)(2,1)S(1)} collective-permute-done((bf16[4,16,1536]{2,1,0:T(8,128)(2,1)S(1)}, bf16[4,16,1536]{2,1,0:T(8,128)(2,1)S(1)}, u32[]{:S(2)}, u32[]{:S(2)}) %collective-permute-start.29) | collective-permute-done | bytes 196640 | tf_op jit(solution)/shard_map/ppermute | solution.py:40
  207.2 2.1 collective-permute-start.27
  209.3 4.5 %collective-permute-done.27 = bf16[4,16,1536]{2,1,0:T(8,128)(2,1)S(1)} collective-permute-done((bf16[4,16,1536]{2,1,0:T(8,128)(2,1)S(1)}, bf16[4,16,1536]{2,1,0:T(8,128)(2,1)S(1)}, u32[]{:S(2)}, u32[]{:S(2)}) %collective-permute-start.27) | collective-permute-done | bytes 196640 | tf_op jit(solution)/shard_map/ppermute | solution.py:40
  213.8 1.7 collective-permute-start.30
  218.0 2.9 %collective-permute-start.34 = (bf16[16,3328]{1,0:T(8,128)(2,1)S(1)}, bf16[16,3328]{1,0:T(8,128)(2,1)S(1)}, u32[]{:S(2)}, u32[]{:S(2)}) collective-permute-start(bf16[16,3328]{1,0:T(8,128)(2,1)S(1)} %get-tuple-element.196), channel_id=1, source_target_pairs={{0,16},{4,20},{8,24},{12,28},{16,0},{20,4},{24,8},{28,12},{1,17},{... | collective-permute-start | bytes 319496 | tf_op jit(solution)/shard_map/ppermute | solution.py:40
  223.2 2.5 %collective-permute-done.35 = bf16[16,3328]{1,0:T(8,128)(2,1)S(1)} collective-permute-done((bf16[16,3328]{1,0:T(8,128)(2,1)S(1)}, bf16[16,3328]{1,0:T(8,128)(2,1)S(1)}, u32[]{:S(2)}, u32[]{:S(2)}) %collective-permute-start.35) | collective-permute-done | bytes 106528 | tf_op jit(solution)/shard_map/ppermute | solution.py:40
  225.7 2.8 %collective-permute-done.34 = bf16[16,3328]{1,0:T(8,128)(2,1)S(1)} collective-permute-done((bf16[16,3328]{1,0:T(8,128)(2,1)S(1)}, bf16[16,3328]{1,0:T(8,128)(2,1)S(1)}, u32[]{:S(2)}, u32[]{:S(2)}) %collective-permute-start.34) | collective-permute-done | bytes 106528 | tf_op jit(solution)/shard_map/ppermute | solution.py:40
  (230 shorter events, 40.7 us)
Async XLA Ops:
  7.3 81.9 %all-gather.3.cloned.1.call-start = ((), (), s32[]{:S(2)}) async-start(), calls=%async_computation.2 | async-start | bytes 4325376 | tf_op jit(solution)/shard_map/all_gather | solution.py:578
  10.3 14.0 %collective-permute-start.2 = (bf16[16,1792]{1,0:T(8,128)(2,1)S(1)}, bf16[16,1792]{1,0:T(8,128)(2,1)S(1)}, u32[]{:S(2)}, u32[]{:S(2)}) collective-permute-start(bf16[16,1792]{1,0:T(8,128)(2,1)S(1)} %concatenate.23), channel_id=1, source_target_pairs={{0,8},{4,12},{8,0},{12,4},{16,24},{20,28},{24,16},{28,20},{1,9},{5... | collective-permute-start | bytes 172040 | tf_op jit(solution)/shard_map/ppermute | solution.py:40
  13.3 11.0 %collective-permute-start.1 = (bf16[16,1792]{1,0:T(8,128)(2,1)S(1)}, bf16[16,1792]{1,0:T(8,128)(2,1)S(1)}, u32[]{:S(2)}, u32[]{:S(2)}) collective-permute-start(bf16[16,1792]{1,0:T(8,128)(2,1)S(1)} %concatenate.23), channel_id=1, source_target_pairs={{0,16},{4,20},{8,24},{12,28},{16,0},{20,4},{24,8},{28,12},{1,17},{... | collective-permute-start | bytes 172040 | tf_op jit(solution)/shard_map/ppermute | solution.py:40
  15.9 8.4 %collective-permute-start = (bf16[16,1792]{1,0:T(8,128)(2,1)S(1)}, bf16[16,1792]{1,0:T(8,128)(2,1)S(1)}, u32[]{:S(2)}, u32[]{:S(2)}) collective-permute-start(bf16[16,1792]{1,0:T(8,128)(2,1)S(1)} %concatenate.23), channel_id=1, source_target_pairs={{0,24},{4,28},{8,16},{12,20},{16,8},{20,12},{24,0},{28,4},{1,25},{... | collective-permute-start | bytes 172040 | tf_op jit(solution)/shard_map/ppermute | solution.py:40
  16.6 156.5 %reduce-scatter.2.cloned.1.call-start = ((), (), s32[]{:S(2)}) async-start(), calls=%async_computation.1 | async-start | bytes 5242880 | tf_op jit(solution)/shard_map/reduce_scatter | solution.py:811
  19.5 11.1 %collective-permute-start.4 = (bf16[256,512]{1,0:T(8,128)(2,1)S(1)}, bf16[256,512]{1,0:T(8,128)(2,1)S(1)}, u32[]{:S(2)}, u32[]{:S(2)}) collective-permute-start(bf16[256,512]{1,0:T(8,128)(2,1)S(1)} %dynamic-slice_bitcast_fusion.5), channel_id=1, source_target_pairs={{0,3},{1,2},{2,1},{3,0},{4,7},{5,6},{6,5},{7,4},{8,11},{9,10},{10,... | collective-permute-start | bytes 786440 | tf_op jit(solution)/shard_map/ppermute | solution.py:40
  24.7 12.8 %collective-permute-start.15 = (bf16[16,1664]{1,0:T(8,128)(2,1)S(1)}, bf16[16,1664]{1,0:T(8,128)(2,1)S(1)}, u32[]{:S(2)}, u32[]{:S(2)}) collective-permute-start(bf16[16,1664]{1,0:T(8,128)(2,1)S(1)} %pad_maximum_fusion.2), channel_id=1, source_target_pairs={{0,24},{4,28},{8,16},{12,20},{16,8},{20,12},{24,0},{28,4},{1,25},{... | collective-permute-start | bytes 159752 | tf_op jit(solution)/shard_map/ppermute | solution.py:40
  28.3 9.2 %collective-permute-start.14 = (bf16[16,1664]{1,0:T(8,128)(2,1)S(1)}, bf16[16,1664]{1,0:T(8,128)(2,1)S(1)}, u32[]{:S(2)}, u32[]{:S(2)}) collective-permute-start(bf16[16,1664]{1,0:T(8,128)(2,1)S(1)} %pad_maximum_fusion.2), channel_id=1, source_target_pairs={{0,16},{4,20},{8,24},{12,28},{16,0},{20,4},{24,8},{28,12},{1,17},{... | collective-permute-start | bytes 159752 | tf_op jit(solution)/shard_map/ppermute | solution.py:40
  28.3 9.2 %collective-permute-start.13 = (bf16[16,1664]{1,0:T(8,128)(2,1)S(1)}, bf16[16,1664]{1,0:T(8,128)(2,1)S(1)}, u32[]{:S(2)}, u32[]{:S(2)}) collective-permute-start(bf16[16,1664]{1,0:T(8,128)(2,1)S(1)} %pad_maximum_fusion.2), channel_id=1, source_target_pairs={{0,8},{4,12},{8,0},{12,4},{16,24},{20,28},{24,16},{28,20},{1,9},{5... | collective-permute-start | bytes 159752 | tf_op jit(solution)/shard_map/ppermute | solution.py:40
  29.2 8.3 %collective-permute-start.3 = (bf16[4,16,1792]{2,1,0:T(8,128)(2,1)S(1)}, bf16[4,16,1792]{2,1,0:T(8,128)(2,1)S(1)}, u32[]{:S(2)}, u32[]{:S(2)}) collective-permute-start(bf16[4,16,1792]{2,1,0:T(8,128)(2,1)S(1)} %select_select_fusion), channel_id=1, source_target_pairs={{0,2},{1,3},{2,0},{3,1},{4,6},{5,7},{6,4},{7,5},{8,10},{9,11},{10,... | collective-permute-start | bytes 688136 | tf_op jit(solution)/shard_map/ppermute | solution.py:40
  42.0 13.5 %collective-permute-start.8 = (bf16[4,2,16,1536]{3,2,1,0:T(8,128)(2,1)S(1)}, bf16[4,2,16,1536]{3,2,1,0:T(8,128)(2,1)S(1)}, u32[]{:S(2)}, u32[]{:S(2)}) collective-permute-start(bf16[4,2,16,1536]{3,2,1,0:T(8,128)(2,1)S(1)} %slice.128), channel_id=1, source_target_pairs={{0,4},{4,0},{8,12},{12,8},{16,20},{20,16},{24,28},{28,24},{1,5},{5... | collective-permute-start | bytes 1179656 | tf_op jit(solution)/shard_map/ppermute | solution.py:40
  44.0 12.7 %collective-permute-start.16 = (bf16[4,16,1664]{2,1,0:T(8,128)(2,1)S(1)}, bf16[4,16,1664]{2,1,0:T(8,128)(2,1)S(1)}, u32[]{:S(2)}, u32[]{:S(2)}) collective-permute-start(bf16[4,16,1664]{2,1,0:T(8,128)(2,1)S(1)} %select_select_fusion.1), channel_id=1, source_target_pairs={{0,2},{1,3},{2,0},{3,1},{4,6},{5,7},{6,4},{7,5},{8,10},{9,11},{10,... | collective-permute-start | bytes 638984 | tf_op jit(solution)/shard_map/ppermute | solution.py:40
  44.8 11.8 %collective-permute-start.10 = (bf16[256,8]{1,0:T(8,128)(2,1)S(1)}, bf16[256,8]{1,0:T(8,128)(2,1)S(1)}, u32[]{:S(2)}, u32[]{:S(2)}) collective-permute-start(bf16[256,8]{1,0:T(8,128)(2,1)S(1)} %fusion.6), channel_id=1, source_target_pairs={{0,3},{1,2},{2,1},{3,0},{4,7},{5,6},{6,5},{7,4},{8,11},{9,10},{10,... | collective-permute-start | bytes 12296 | tf_op jit(solution)/shard_map/ppermute | solution.py:40
  56.5 9.0 %collective-permute-start.7 = (bf16[4,256,128]{2,1,0:T(8,128)(2,1)}, bf16[4,256,128]{2,1,0:T(8,128)(2,1)}, u32[]{:S(2)}, u32[]{:S(2)}) collective-permute-start(bf16[4,256,128]{2,1,0:T(8,128)(2,1)} %get-tuple-element.76), channel_id=1, source_target_pairs={{0,2},{1,3},{2,0},{3,1},{4,6},{5,7},{6,4},{7,5},{8,10},{9,11},{10,... | collective-permute-start | bytes 786440 | tf_op jit(solution)/shard_map/ppermute | solution.py:40
  56.9 15.1 %collective-permute-start.17 = (bf16[4,2,16,1664]{3,2,1,0:T(8,128)(2,1)S(1)}, bf16[4,2,16,1664]{3,2,1,0:T(8,128)(2,1)S(1)}, u32[]{:S(2)}, u32[]{:S(2)}) collective-permute-start(bf16[4,2,16,1664]{3,2,1,0:T(8,128)(2,1)S(1)} %broadcast_select_fusion.4), channel_id=1, source_target_pairs={{0,4},{4,0},{8,12},{12,8},{16,20},{20,16},{24,28},{28,24},{1,5},{5... | collective-permute-start | bytes 1277960 | tf_op jit(solution)/shard_map/ppermute | solution.py:40
  66.6 7.8 %collective-permute-start.11 = (bf16[2,4,256,128]{3,2,1,0:T(8,128)(2,1)S(1)}, bf16[2,4,256,128]{3,2,1,0:T(8,128)(2,1)S(1)}, u32[]{:S(2)}, u32[]{:S(2)}) collective-permute-start(bf16[2,4,256,128]{3,2,1,0:T(8,128)(2,1)S(1)} %broadcast_select_fusion.2), channel_id=1, source_target_pairs={{0,1},{1,0},{2,3},{3,2},{4,5},{5,4},{6,7},{7,6},{8,9},{9,8},{10,11... | collective-permute-start | bytes 1572872 | tf_op jit(solution)/shard_map/ppermute | solution.py:40
  72.0 14.5 %collective-permute-start.12 = (bf16[256,512]{1,0:T(8,128)(2,1)S(1)}, bf16[256,512]{1,0:T(8,128)(2,1)S(1)}, u32[]{:S(2)}, u32[]{:S(2)}) collective-permute-start(bf16[256,512]{1,0:T(8,128)(2,1)S(1)} %dynamic-slice_bitcast_fusion.4), channel_id=1, source_target_pairs={{0,3},{1,2},{2,1},{3,0},{4,7},{5,6},{6,5},{7,4},{8,11},{9,10},{10,... | collective-permute-start | bytes 786440 | tf_op jit(solution)/shard_map/ppermute | solution.py:40
  72.6 14.1 %collective-permute-start.18 = (bf16[4,2,2,16,1664]{4,3,2,1,0:T(8,128)(2,1)S(1)}, bf16[4,2,2,16,1664]{4,3,2,1,0:T(8,128)(2,1)S(1)}, u32[]{:S(2)}, u32[]{:S(2)}) collective-permute-start(bf16[4,2,2,16,1664]{4,3,2,1,0:T(8,128)(2,1)S(1)} %broadcast_select_fusion), channel_id=1, source_target_pairs={{0,1},{1,0},{2,3},{3,2},{4,5},{5,4},{6,7},{7,6},{8,9},{9,8},{10,11... | collective-permute-start | bytes 2555912 | tf_op jit(solution)/shard_map/ppermute | solution.py:40
  159.2 23.7 %collective-permute-start.22 = (bf16[256,1536]{1,0:T(8,128)(2,1)}, bf16[256,1536]{1,0:T(8,128)(2,1)S(1)}, u32[]{:S(2)}, u32[]{:S(2)}) collective-permute-start(bf16[256,1536]{1,0:T(8,128)(2,1)} %get-tuple-element.118), channel_id=1, source_target_pairs={{0,1},{1,0},{2,3},{3,2},{4,5},{5,4},{6,7},{7,6},{8,9},{9,8},{10,11... | collective-permute-start | bytes 2359304 | tf_op jit(solution)/shard_map/ppermute | solution.py:40
  160.7 22.4 %collective-permute-start.23 = (bf16[1024,128]{1,0:T(8,128)(2,1)S(1)}, bf16[1024,128]{1,0:T(8,128)(2,1)S(1)}, u32[]{:S(2)}, u32[]{:S(2)}) collective-permute-start(bf16[1024,128]{1,0:T(8,128)(2,1)S(1)} %dynamic-slice_bitcast_fusion.3), channel_id=1, source_target_pairs={{0,2},{1,3},{2,0},{3,1},{4,6},{5,7},{6,4},{7,5},{8,10},{9,11},{10,... | collective-permute-start | bytes 786440 | tf_op jit(solution)/shard_map/ppermute | solution.py:40
  174.1 14.8 %collective-permute-start.20 = (bf16[4,128,512]{2,1,0:T(8,128)(2,1)S(1)}, bf16[4,128,512]{2,1,0:T(8,128)(2,1)S(1)}, u32[]{:S(2)}, u32[]{:S(2)}) collective-permute-start(bf16[4,128,512]{2,1,0:T(8,128)(2,1)S(1)} %dynamic-slice_bitcast_fusion), channel_id=1, source_target_pairs={{0,4},{4,0},{8,12},{12,8},{16,20},{20,16},{24,28},{28,24},{1,5},{5... | collective-permute-start | bytes 1572872 | tf_op jit(solution)/shard_map/ppermute | solution.py:40
  183.2 15.7 %collective-permute-start.28 = (bf16[4,2,16,1536]{3,2,0,1:T(8,128)(2,1)S(1)}, bf16[4,2,16,1536]{3,2,0,1:T(8,128)(2,1)S(1)}, u32[]{:S(2)}, u32[]{:S(2)}) collective-permute-start(bf16[4,2,16,1536]{3,2,0,1:T(8,128)(2,1)S(1)} %bitcast.154), channel_id=1, source_target_pairs={{0,4},{4,0},{8,12},{12,8},{16,20},{20,16},{24,28},{28,24},{1,5},{5... | collective-permute-start | bytes 1179656 | tf_op jit(solution)/shard_map/ppermute | solution.py:40
  189.1 28.7 %collective-permute-start.36 = (bf16[2,128,512]{2,1,0:T(8,128)(2,1)S(1)}, bf16[2,128,512]{2,1,0:T(8,128)(2,1)S(1)}, u32[]{:S(2)}, u32[]{:S(2)}) collective-permute-start(bf16[2,128,512]{2,1,0:T(8,128)(2,1)S(1)} %dynamic-slice_bitcast_fusion.2), channel_id=1, source_target_pairs={{0,16},{4,20},{8,24},{12,28},{16,0},{20,4},{24,8},{28,12},{1,17},{... | collective-permute-start | bytes 786440 | tf_op jit(solution)/shard_map/ppermute | solution.py:40
  189.5 17.6 %collective-permute-start.26 = (bf16[4,2,16,1536]{3,2,1,0:T(8,128)(2,1)S(1)}, bf16[4,2,16,1536]{3,2,1,0:T(8,128)(2,1)S(1)}, u32[]{:S(2)}, u32[]{:S(2)}) collective-permute-start(bf16[4,2,16,1536]{3,2,1,0:T(8,128)(2,1)S(1)} %dynamic-slice_bitcast_fusion.1), channel_id=1, source_target_pairs={{0,2},{1,3},{2,0},{3,1},{4,6},{5,7},{6,4},{7,5},{8,10},{9,11},{10,... | collective-permute-start | bytes 1179656 | tf_op jit(solution)/shard_map/ppermute | solution.py:40
  199.2 7.8 %collective-permute-start.29 = (bf16[4,16,1536]{2,1,0:T(8,128)(2,1)S(1)}, bf16[4,16,1536]{2,1,0:T(8,128)(2,1)S(1)}, u32[]{:S(2)}, u32[]{:S(2)}) collective-permute-start(bf16[4,16,1536]{2,1,0:T(8,128)(2,1)S(1)} %dynamic-slice_bitcast_fusion.6), channel_id=1, source_target_pairs={{0,2},{1,3},{2,0},{3,1},{4,6},{5,7},{6,4},{7,5},{8,10},{9,11},{10,... | collective-permute-start | bytes 589832 | tf_op jit(solution)/shard_map/ppermute | solution.py:40
  202.2 7.1 %collective-permute-start.25 = (bf16[4,2,16,256]{3,2,1,0:T(8,128)(2,1)S(1)}, bf16[4,2,16,256]{3,2,1,0:T(8,128)(2,1)S(1)}, u32[]{:S(2)}, u32[]{:S(2)}) collective-permute-start(bf16[4,2,16,256]{3,2,1,0:T(8,128)(2,1)S(1)} %dynamic-slice_bitcast_fusion.13), channel_id=1, source_target_pairs={{0,2},{1,3},{2,0},{3,1},{4,6},{5,7},{6,4},{7,5},{8,10},{9,11},{10,... | collective-permute-start | bytes 196616 | tf_op jit(solution)/shard_map/ppermute | solution.py:40
  203.6 11.9 %collective-permute-start.32 = (bf16[256,512]{1,0:T(8,128)(2,1)S(1)}, bf16[256,512]{1,0:T(8,128)(2,1)S(1)}, u32[]{:S(2)}, u32[]{:S(2)}) collective-permute-start(bf16[256,512]{1,0:T(8,128)(2,1)S(1)} %copy-done.31), channel_id=1, source_target_pairs={{0,3},{1,2},{2,1},{3,0},{4,7},{5,6},{6,5},{7,4},{8,11},{9,10},{10,... | collective-permute-start | bytes 786440 | tf_op jit(solution)/shard_map/ppermute | solution.py:40
  217.9 7.8 %collective-permute-start.35 = (bf16[16,3328]{1,0:T(8,128)(2,1)S(1)}, bf16[16,3328]{1,0:T(8,128)(2,1)S(1)}, u32[]{:S(2)}, u32[]{:S(2)}) collective-permute-start(bf16[16,3328]{1,0:T(8,128)(2,1)S(1)} %get-tuple-element.195), channel_id=1, source_target_pairs={{0,24},{4,28},{8,16},{12,20},{16,8},{20,12},{24,0},{28,4},{1,25},{... | collective-permute-start | bytes 319496 | tf_op jit(solution)/shard_map/ppermute | solution.py:40
  218.0 10.5 %collective-permute-start.34 = (bf16[16,3328]{1,0:T(8,128)(2,1)S(1)}, bf16[16,3328]{1,0:T(8,128)(2,1)S(1)}, u32[]{:S(2)}, u32[]{:S(2)}) collective-permute-start(bf16[16,3328]{1,0:T(8,128)(2,1)S(1)} %get-tuple-element.196), channel_id=1, source_target_pairs={{0,16},{4,20},{8,24},{12,28},{16,0},{20,4},{24,8},{28,12},{1,17},{... | collective-permute-start | bytes 319496 | tf_op jit(solution)/shard_map/ppermute | solution.py:40
  221.0 7.6 %collective-permute-start.33 = (bf16[16,3328]{1,0:T(8,128)(2,1)S(1)}, bf16[16,3328]{1,0:T(8,128)(2,1)S(1)}, u32[]{:S(2)}, u32[]{:S(2)}) collective-permute-start(bf16[16,3328]{1,0:T(8,128)(2,1)S(1)} %get-tuple-element.197), channel_id=1, source_target_pairs={{0,8},{4,12},{8,0},{12,4},{16,24},{20,28},{24,16},{28,20},{1,9},{5... | collective-permute-start | bytes 319496 | tf_op jit(solution)/shard_map/ppermute | solution.py:40
  222.5 9.3 %collective-permute-start.37 = (bf16[128,512]{1,0:T(8,128)(2,1)S(1)}, bf16[128,512]{1,0:T(8,128)(2,1)S(1)}, u32[]{:S(2)}, u32[]{:S(2)}) collective-permute-start(bf16[128,512]{1,0:T(8,128)(2,1)S(1)} %dynamic-slice_bitcast_fusion.8), channel_id=1, source_target_pairs={{0,8},{4,12},{8,0},{12,4},{16,24},{20,28},{24,16},{28,20},{1,9},{5... | collective-permute-start | bytes 393224 | tf_op jit(solution)/shard_map/ppermute | solution.py:40
  223.2 9.4 %collective-permute-start.31 = (bf16[256,512]{1,0:T(8,128)(2,1)S(1)}, bf16[256,512]{1,0:T(8,128)(2,1)S(1)}, u32[]{:S(2)}, u32[]{:S(2)}) collective-permute-start(bf16[256,512]{1,0:T(8,128)(2,1)S(1)} %copy-done.30), channel_id=1, source_target_pairs={{0,3},{1,2},{2,1},{3,0},{4,7},{5,6},{6,5},{7,4},{8,11},{9,10},{10,... | collective-permute-start | bytes 786440 | tf_op jit(solution)/shard_map/ppermute | solution.py:40
  (40 other events, 236.7 us)
Sparse Core Ops, SparseCore 0:
  16.7 69.0 all-gather.2
  115.9 48.6 reduce-scatter.1
